TPU v7x, 32 devices: a whole 2x2x4 slice. The times are simulated.
32 devices in a mesh: row: 16 (over z, x, core), col: 2 (over y).
Axes of the slice: x: 2, y: 2, z: 4, core: 2. Of those that a mesh axis runs over, the one named last changes fastest.
Arguments:
- amplitudes: bfloat16 [128, 64, 256], P('col', 'row'), may hold values from -6 to 6
- integrals: bfloat16 [64, 12, 256, 256], P('row', 'col'), may hold values from -0.0625 to 0.0625
- screen: int32 [64, 12], P('row', 'col'), may hold values from -1 to 7, as said below
- owner_map: int32 [2, 8], P('col'), may hold values from 0 to 7, each once within a row
Outputs:
- ladder: float32 [128, 16, 256], P('row', 'col')
Inputs may be any that keep to these rules, and one draw needn't show every extreme that they name: `screen`: in each row and column group the 6 slots first name distinct result tiles of that group, then hold -1; at least 2 are live, and some group of some row has all 6 live.
All inputs are finite; a program needn't handle non-finite values.
Results may differ from a plain program's by a relative error of at most 0.0003.
Values may be sent and summed in bfloat16 or wider, within the bound.
No kernel may reach another device: no remote copies, remote signals or barrier semaphores. Data moves between devices by JAX's collectives and lax.ppermute only.
A program may use at most 64 MiB of HBM per device.

v0:
```python
import jax
import jax.numpy as jnp
from jax import lax
from jax.sharding import PartitionSpec as P


def body(amplitudes, integrals, screen, owner_map):
    gathered = lax.all_gather(amplitudes, "col", axis=0, tiled=True)
    group_tiles = owner_map.shape[1]
    live_slot = screen >= 0
    labels = jnp.arange(group_tiles, dtype=jnp.int32)
    matches = screen[:, :, None] == labels[None, None, :]
    stored = jnp.sum(jnp.where(matches, owner_map[0][None, None, :], 0), axis=2)
    selector = ((stored[:, :, None] == labels[None, None, :]) & live_slot[:, :, None]).astype(
        jnp.bfloat16
    )
    placed = jnp.einsum(
        "kla,klwv->kawv", selector, integrals, preferred_element_type=jnp.float32
    ).astype(jnp.bfloat16)
    return lax.psum_scatter(
        jnp.einsum("pkw,kawv->pav", gathered, placed, preferred_element_type=jnp.float32),
        "row",
        scatter_dimension=0,
        tiled=True,
    )


def solution(mesh):
    return jax.shard_map(
        body,
        mesh=mesh,
        in_specs=(
            P("col", "row", None),
            P("row", "col", None, None),
            P("row", "col"),
            P("col", None),
        ),
        out_specs=P("row", "col", None),
        check_vma=False,
    )
```

profile of v0, /device:TPU:0, one launch (start us, length us, event | category | flops | bytes accessed | tf_op | source)
XLA Modules:
  0.0 91.2 jit_solution(10092747847685109064)
XLA Ops:
  6.5 0.0 copy-start
  6.5 0.0 reduce-scatter.2.cloned.1.call-start
  6.5 0.8 broadcast_compare_fusion
  7.4 0.9 copy.9
  8.3 0.9 select_reduce_fusion
  9.2 0.1 copy.10
  9.3 0.9 %copy.12 = bf16[64,4,256]{2,0,1:T(8,128)(2,1)S(1)} copy(bf16[64,4,256]{2,1,0:T(4,128)(2,1)} %param.4) | data formatting | bytes 262144 | tf_op args[0]
  10.2 7.1 %all_gather.3 = bf16[128,4,256]{2,0,1:T(8,128)(2,1)S(1)} all-gather(bf16[64,4,256]{2,0,1:T(8,128)(2,1)S(1)} %copy.12), channel_id=1, replica_groups=mesh['row'=16,'col'=2] {'col'}, dimensions={0}, use_global_device_ids=true | all-gather | bytes 393216 | tf_op jit(solution)/shard_map/all_gather | solution.py:8
  17.3 0.0 copy-done
  17.3 2.0 %fusion.4 = bf16[4,8,256,256]{3,1,2,0:T(8,128)(2,1)S(1)} fusion(bf16[4,6,256,256]{3,2,1,0:T(8,128)(2,1)S(1)} %copy-done, s32[4,6]{1,0:T(4,128)S(1)} %copy.10, pred[4,6]{1,0:T(4,128)(4,1)S(1)} %broadcast_compare_fusion), kind=kOutput, calls=%fused_computation.4 | convolution fusion | flops 27263360 | bytes 7340152 | tf_op jit(solution)/shard_map/kla,klwv->kawv/dot_general | solution.py:17
  19.3 3.2 %fusion.7 = f32[128,8,256]{0,2,1:T(8,128)} fusion(bf16[4,8,256,256]{3,1,2,0:T(8,128)(2,1)S(1)} %fusion.4, bf16[128,4,256]{2,0,1:T(8,128)(2,1)S(1)} %all_gather.3), kind=kOutput, calls=%fused_computation.5 | convolution fusion | flops 536870912 | bytes 5505024 | tf_op jit(solution)/shard_map/pkw,kawv->pav/dot_general | solution.py:21
  22.5 2.7 %copy.14 = f32[128,8,256]{2,1,0:T(8,128)} copy(f32[128,8,256]{0,2,1:T(8,128)} %fusion.7) | data formatting | bytes 2097152 | tf_op jit(solution)/shard_map/pkw,kawv->pav/dot_general | solution.py:21
  25.2 0.0 reduce-scatter.2.cloned.1.call-update
  25.2 59.1 %reduce-scatter.2.cloned.1.call-done = f32[8,8,256]{2,1,0:T(8,128)} async-done(((f32[128,8,256]{2,1,0:T(8,128)}), f32[8,8,256]{2,1,0:T(8,128)}) %reduce-scatter.2.cloned.1.call-update) | async-done | bytes 65552 | tf_op jit(solution)/shard_map/reduce_scatter | solution.py:20
Async XLA Ops:
  6.5 10.8 %copy-start = (bf16[4,6,256,256]{3,2,1,0:T(8,128)(2,1)S(1)}, bf16[4,6,256,256]{3,2,1,0:T(8,128)(2,1)}, u32[]{:S(2)}) copy-start(bf16[4,6,256,256]{3,2,1,0:T(8,128)(2,1)} %param.5) | copy-start | bytes 9437188
  6.5 77.8 %reduce-scatter.2.cloned.1.call-start = ((), (), s32[]{:S(2)}) async-start(), calls=%async_computation.1 | async-start | bytes 1114112 | tf_op jit(solution)/shard_map/reduce_scatter | solution.py:20
Sparse Core Ops, SparseCore 0:
  25.3 58.9 reduce-scatter.1
where the time goes:
time: 91.3 us; the launch traced here: 91.2 us
  waiting for transfers between devices  59.1 us (65%)
  between operations  13.4 us (15%)
  blocking collectives  7.12 us (8%)
  matrix products  5.22 us (6%)
  local copies, waits for them, and re-layouts  4.57 us (5%)
  other arithmetic  1.73 us (2%)
    reduce_scatter x1, waiting for transfers between devices, body(): lax.psum_scatter(jnp.einsum('pkw,kawv->pav', gathered, placed, preferred_...  59.1 us
    all_gather x1, blocking collectives, body(): gathered = lax.all_gather(amplitudes, 'col', axis=0, tiled=True)  7.12 us
    dot_general x1, matrix products, body(): jnp.einsum('pkw,kawv->pav', gathered, placed, preferred_element_type=jnp....  3.24 us
    dot_general x1, local copies, waits for them, and re-layouts, body(): jnp.einsum('pkw,kawv->pav', gathered, placed, preferred_element_type=jnp....  2.66 us
    dot_general x1, matrix products, body(): jnp.einsum('kla,klwv->kawv', selector, integrals, preferred_element_type=...  1.98 us
  transfers between devices with their start and end apart: 1, of which 1 were waited for; matrix products, arithmetic and copies ran while one was open for 0% of the time, Pallas kernels for 0%

commit v1 on v0

v1 whole, which is shorter than its diff:
```python
import functools

import jax
import jax.numpy as jnp
from jax import lax
from jax.experimental import pallas as pl
from jax.experimental.pallas import tpu as pltpu
from jax.sharding import PartitionSpec as P

def partial_kernel(n_col, masks, size, screen, owner, own, *refs):
    others, integrals = refs[: n_col - 1], refs[n_col - 1]
    send, keep = refs[n_col], refs[n_col + 1 : -3]
    lhs, total, table = refs[-3:]
    tiles, slots = screen.shape
    targets = owner.shape[1]
    half = own.shape[1]
    row, col = lax.axis_index("row"), lax.axis_index("col")

    for at in range(tiles * targets):
        table[at] = -1
    for k in range(tiles):
        for s in range(slots):
            name = screen[k, s]
            stored = owner[0, jnp.maximum(name, 0)]
            table[jnp.where(name >= 0, k * targets + stored, tiles * targets)] = s

    for step in range(n_col):
        source = own if step == 0 else others[step - 1]
        owner_col = lax.rem(col + n_col - step, n_col)
        for k in range(tiles):
            lhs[k, pl.ds(pl.multiple_of(owner_col * half, half), half), :] = source[k]

    for t in range(targets):
        acc = None
        for k in range(tiles):
            s = table[k * targets + t]
            left = jnp.where(s >= 0, lhs[k], jnp.zeros_like(lhs[k]))
            term = jnp.dot(left, integrals[k, jnp.maximum(s, 0)], preferred_element_type=jnp.float32)
            acc = term if acc is None else acc + term
        total[t] = acc

    def block(t, j):
        return total[t, pl.ds(pl.multiple_of((row ^ j) * size, size), size), :]

    order = [0]
    for m in reversed(masks):
        order = order + [m ^ o for o in order]
    parts, low = [], 0
    for ref in reversed(keep):
        parts.append((ref, order[low : low + ref.shape[0]]))
        low += ref.shape[0]
    for t in range(targets):
        rows = pl.ds(t * size, size)
        for at, j in enumerate(order):
            send[at, rows, :] = block(t, j ^ 1)
        for ref, js in parts:
            for at, j in enumerate(js):
                ref[at, rows, :] = block(t, j)


def final_kernel(targets, size, a, b, out):
    x = a[0] + b[0]
    for t in range(targets):
        out[:, t, :] = x[t * size : (t + 1) * size, :]


def body(n_row, n_col, amplitudes, integrals, screen, owner_map):
    half, tiles, width = amplitudes.shape
    targets = owner_map.shape[1]
    out_width = integrals.shape[3]
    depth = n_row.bit_length() - 1
    masks = [1 << b for b in range(1, depth)]
    pairs = half * n_col
    size = pairs // n_row

    def vmem(x):
        return pltpu.with_memory_space_constraint(x, pltpu.VMEM)

    def swap(x, mask):
        return lax.ppermute(x, "row", [(i, i ^ mask) for i in range(n_row)])

    own = jnp.transpose(amplitudes, (1, 0, 2))
    others = [
        lax.ppermute(own, "col", [(i, (i + step) % n_col) for i in range(n_col)])
        for step in range(1, n_col)
    ]
    sizes = [1 << (len(masks) - 1 - i) for i in range(len(masks))] + [1]
    block = (targets * size, out_width)
    spec = pl.BlockSpec(memory_space=pltpu.VMEM)
    smem = pl.BlockSpec(memory_space=pltpu.SMEM)
    outs = pl.pallas_call(
        functools.partial(partial_kernel, n_col, masks, size),
        out_shape=[pltpu.VMEM((n_row // 2,) + block, jnp.float32)]
        + [pltpu.VMEM((n,) + block, jnp.float32) for n in sizes],
        in_specs=[smem, smem] + [spec] * (n_col + 1),
        out_specs=[spec] * (1 + len(sizes)),
        scratch_shapes=[
            pltpu.VMEM((tiles, pairs, width), jnp.bfloat16),
            pltpu.VMEM((targets, pairs, out_width), jnp.float32),
            pltpu.SMEM((tiles * targets + 1,), jnp.int32),
        ],
        cost_estimate=pl.CostEstimate(
            flops=2 * pairs * tiles * targets * width * out_width,
            bytes_accessed=integrals.size * 2,
            transcendentals=0,
        ),
        compiler_params=pltpu.CompilerParams(vmem_limit_bytes=24 * 1024 * 1024),
        name="partial_sums",
    )(screen, owner_map, vmem(own), *[vmem(o) for o in others], vmem(integrals))
    send, keep = outs[0], list(outs[1:])

    got = swap(send, 1)
    for at, mask in enumerate([None] + masks[:-1]):
        if mask is not None:
            got = swap(keep[0], mask)
            keep = keep[1:]
        top = got.shape[0]
        fresh = []
        for part in keep:
            fresh.append(part + got[top - part.shape[0] : top])
            top -= part.shape[0]
        keep = fresh
    got = swap(keep[0], masks[-1])
    return pl.pallas_call(
        functools.partial(final_kernel, targets, size),
        out_shape=jax.ShapeDtypeStruct((size, targets, out_width), jnp.float32),
        in_specs=[spec, spec],
        out_specs=spec,
        name="own_block",
    )(vmem(keep[1]), vmem(got))


def solution(mesh):
    return jax.shard_map(
        functools.partial(body, mesh.shape["row"], mesh.shape["col"]),
        mesh=mesh,
        in_specs=(
            P("col", "row", None),
            P("row", "col", None, None),
            P("row", "col"),
            P("col", None),
        ),
        out_specs=P("row", "col", None),
        check_vma=False,
    )
```

time: 91.3 us -> 33.8 us (0.37)
  waiting for transfers between devices: 59.1 us -> 17.6 us
  between operations: 13.4 us -> 0.04 us
  starting transfers between devices: 0.01 us -> 9.62 us
  blocking collectives: 7.12 us -> 0 us
  matrix products: 5.22 us -> 0 us
  Pallas kernels: 0 us -> 2.13 us
  other arithmetic: 1.73 us -> 0.09 us
    reduce_scatter x1 -> x0, waiting for transfers between devices: 59.1 us -> none  [body(): lax.psum_scatter(jnp.einsum('pkw,kawv->pav', gathered, placed, preferred_...]
    ppermute x0 -> x5, waiting for transfers between devices: none -> 17.6 us  [the longest x4 14.1 us: swap(): return lax.ppermute(x, 'row', [(i, i ^ mask) for i in range(n_row)])]
    ppermute x0 -> x5, starting transfers between devices: none -> 9.62 us  [the longest x4 6.58 us: swap(): return lax.ppermute(x, 'row', [(i, i ^ mask) for i in range(n_row)])]
    all_gather x1 -> x0, blocking collectives: 7.12 us -> none  [body(): gathered = lax.all_gather(amplitudes, 'col', axis=0, tiled=True)]
    dot_general x2 -> x0, matrix products: 5.22 us -> none  [the longest x1 3.24 us: body(): jnp.einsum('pkw,kawv->pav', gathered, placed, preferred_element_type=jnp....]
    dot_general x1 -> x0, local copies, waits for them, and re-layouts: 2.66 us -> none  [body(): jnp.einsum('pkw,kawv->pav', gathered, placed, preferred_element_type=jnp....]
    unnamed x4 -> x7, local copies, waits for them, and re-layouts: 1.82 us -> 4.14 us
    pallas_call x0 -> x2, Pallas kernels: none -> 2.13 us  [the longest x1 1.47 us: body(): pl.pallas_call(functools.partial(partial_kernel, n_col, masks, size), out...]
  transfers between devices with their start and end apart: 1 -> 5, of which waited for: 1 -> 5; matrix products, arithmetic and copies ran while one was open for 0% -> 0% of each run, Pallas kernels for 0% -> 0%
where the time goes in v1:
time: 33.8 us; the launch traced here: 33.6 us
  waiting for transfers between devices  17.6 us (52%)
  starting transfers between devices  9.62 us (28%)
  local copies, waits for them, and re-layouts  4.14 us (12%)
  Pallas kernels  2.13 us (6%)
    ppermute x4, waiting for transfers between devices, swap(): return lax.ppermute(x, 'row', [(i, i ^ mask) for i in range(n_row)])  14.1 us
    ppermute x4, starting transfers between devices, swap(): return lax.ppermute(x, 'row', [(i, i ^ mask) for i in range(n_row)])  6.58 us
    unnamed x7, local copies, waits for them, and re-layouts  4.14 us
    ppermute x1, waiting for transfers between devices, body(): lax.ppermute(own, 'col', [(i, (i + step) % n_col) for i in range(n_col)])  3.5 us
    ppermute x1, starting transfers between devices, body(): lax.ppermute(own, 'col', [(i, (i + step) % n_col) for i in range(n_col)])  3.03 us
    pallas_call x1, Pallas kernels, body(): pl.pallas_call(functools.partial(partial_kernel, n_col, masks, size), out...  1.47 us
  transfers between devices with their start and end apart: 5, of which 5 were waited for; matrix products, arithmetic and copies ran while one was open for 0% of the time, Pallas kernels for 0%

profile of v1, /device:TPU:0, one launch (start us, length us, event | category | flops | bytes accessed | tf_op | source)
XLA Modules:
  0.0 33.6 jit_solution(13991153020716248803)
XLA Ops:
  0.0 0.9 %copy.7 = bf16[64,4,256]{2,0,1:T(8,128)(2,1)S(1)} copy(bf16[64,4,256]{2,1,0:T(4,128)(2,1)} %param.4) | data formatting | bytes 262144 | tf_op args[0]
  0.9 3.0 %collective-permute-start = (bf16[4,64,256]{2,1,0:T(8,128)(2,1)S(1)}, bf16[4,64,256]{2,1,0:T(8,128)(2,1)S(1)}, u32[]{:S(2)}, u32[]{:S(2)}) collective-permute-start(bf16[4,64,256]{2,1,0:T(8,128)(2,1)S(1)} %bitcast.3), channel_id=1, source_target_pairs={{0,1},{1,0},{2,3},{3,2},{4,5},{5,4},{6,7},{7,6},{8,9},{9,8},{10,11... | collective-permute-start | bytes 393224 | tf_op jit(solution)/shard_map/ppermute | solution.py:84
  4.0 3.5 %collective-permute-done.refs_0_ = bf16[4,64,256]{2,1,0:T(8,128)(2,1)S(1)} collective-permute-done((bf16[4,64,256]{2,1,0:T(8,128)(2,1)S(1)}, bf16[4,64,256]{2,1,0:T(8,128)(2,1)S(1)}, u32[]{:S(2)}, u32[]{:S(2)}) %collective-permute-start) | collective-permute-done | bytes 131104 | tf_op jit(solution)/shard_map/ppermute | solution.py:84
  7.5 0.0 copy-start
  7.5 1.9 %copy-done = bf16[4,6,256,256]{3,2,1,0:T(8,128)(2,1)S(1)} copy-done((bf16[4,6,256,256]{3,2,1,0:T(8,128)(2,1)S(1)}, bf16[4,6,256,256]{3,2,1,0:T(8,128)(2,1)}, u32[]{:S(2)}) %copy-start) | copy-done | bytes 3145752
  9.3 0.0 copy-start.1
  9.3 0.7 %copy-done.1 = s32[4,6]{1,0:T(4,128)S(1)} copy-done((s32[4,6]{1,0:T(4,128)S(1)}, s32[4,6]{1,0:T(4,128)}, u32[]{:S(2)}) %copy-start.1) | copy-done | bytes 120
  10.0 0.0 copy-start.2
  10.0 0.7 %copy-done.2 = s32[1,8]{1,0:T(1,128)S(1)} copy-done((s32[1,8]{1,0:T(1,128)S(1)}, s32[1,8]{1,0:T(1,128)}, u32[]{:S(2)}) %copy-start.2) | copy-done | bytes 56
  10.7 1.5 %partial_sums.1 = (f32[8,64,256]{2,1,0:T(8,128)S(1)}, f32[4,64,256]{2,1,0:T(8,128)S(1)}, f32[2,64,256]{2,1,0:T(8,128)S(1)}, f32[1,64,256]{2,1,0:T(8,128)S(1)}, f32[1,64,256]{2,1,0:T(8,128)S(1)}) custom-call(s32[4,6]{1,0:T(4,128)S(1)} %copy-done.1, s32[1,8]{1,0:T(1,128)S(1)} %copy-done.2, bf16[4,64,256]{2,1,0:T(8,128)(2,1)S(1)} %bitcast.4, ...), custom_call_target="tpu_custom_call" | custom-call | flops 536870912 | bytes 3145728 | tf_op jit(solution)/shard_map/partial_sums/pallas_call | solution.py:91
  12.2 0.1 collective-permute-start.1
  12.2 1.9 %collective-permute-done.1 = f32[8,64,256]{2,1,0:T(8,128)S(1)} collective-permute-done((f32[8,64,256]{2,1,0:T(8,128)S(1)}, f32[8,64,256]{2,1,0:T(8,128)S(1)}, u32[]{:S(2)}, u32[]{:S(2)}) %collective-permute-start.1) | collective-permute-done | bytes 524320 | tf_op jit(solution)/shard_map/ppermute | solution.py:80
  14.2 1.8 %collective-permute-start.2 = (f32[4,64,256]{2,1,0:T(8,128)S(1)}, f32[4,64,256]{2,1,0:T(8,128)S(1)}, u32[]{:S(2)}, u32[]{:S(2)}) collective-permute-start(f32[4,64,256]{2,1,0:T(8,128)S(1)} %slice_add_fusion), channel_id=1, source_target_pairs={{0,4},{2,6},{4,0},{6,2},{8,12},{10,14},{12,8},{14,10},{16,20},{18,... | collective-permute-start | bytes 786440 | tf_op jit(solution)/shard_map/ppermute | solution.py:80
  16.0 6.6 %collective-permute-done.2 = f32[4,64,256]{2,1,0:T(8,128)S(1)} collective-permute-done((f32[4,64,256]{2,1,0:T(8,128)S(1)}, f32[4,64,256]{2,1,0:T(8,128)S(1)}, u32[]{:S(2)}, u32[]{:S(2)}) %collective-permute-start.2) | collective-permute-done | bytes 262176 | tf_op jit(solution)/shard_map/ppermute | solution.py:80
  22.6 1.9 %collective-permute-start.3 = (f32[2,64,256]{2,1,0:T(8,128)S(1)}, f32[2,64,256]{2,1,0:T(8,128)S(1)}, u32[]{:S(2)}, u32[]{:S(2)}) collective-permute-start(f32[2,64,256]{2,1,0:T(8,128)S(1)} %slice_add_fusion.1), channel_id=1, source_target_pairs={{0,8},{2,10},{4,12},{6,14},{8,0},{10,2},{12,4},{14,6},{16,24},{18,... | collective-permute-start | bytes 393224 | tf_op jit(solution)/shard_map/ppermute | solution.py:80
  24.5 3.2 %collective-permute-done.3 = f32[2,64,256]{2,1,0:T(8,128)S(1)} collective-permute-done((f32[2,64,256]{2,1,0:T(8,128)S(1)}, f32[2,64,256]{2,1,0:T(8,128)S(1)}, u32[]{:S(2)}, u32[]{:S(2)}) %collective-permute-start.3) | collective-permute-done | bytes 131104 | tf_op jit(solution)/shard_map/ppermute | solution.py:80
  27.7 2.9 %collective-permute-start.4 = (f32[1,64,256]{2,1,0:T(8,128)S(1)}, f32[1,64,256]{2,1,0:T(8,128)S(1)}, u32[]{:S(2)}, u32[]{:S(2)}) collective-permute-start(f32[1,64,256]{2,1,0:T(8,128)S(1)} %get-tuple-element.15), channel_id=1, source_target_pairs={{0,16},{2,18},{4,20},{6,22},{8,24},{10,26},{12,28},{14,30},{16,0},... | collective-permute-start | bytes 196616 | tf_op jit(solution)/shard_map/ppermute | solution.py:80
  30.6 2.4 %collective-permute-done.4.b = f32[1,64,256]{2,1,0:T(8,128)S(1)} collective-permute-done((f32[1,64,256]{2,1,0:T(8,128)S(1)}, f32[1,64,256]{2,1,0:T(8,128)S(1)}, u32[]{:S(2)}, u32[]{:S(2)}) %collective-permute-start.4) | collective-permute-done | bytes 65568 | tf_op jit(solution)/shard_map/ppermute | solution.py:80
  32.9 0.7 %own_block.1 = f32[8,8,256]{2,1,0:T(8,128)} custom-call(f32[1,64,256]{2,1,0:T(8,128)S(1)} %get-tuple-element.16.a, f32[1,64,256]{2,1,0:T(8,128)S(1)} %collective-permute-done.4.b), custom_call_target="tpu_custom_call" | custom-call | tf_op jit(solution)/shard_map/own_block/pallas_call | solution.py:124
  (3 shorter events, 0.1 us)
Async XLA Ops:
  0.9 6.5 %collective-permute-start = (bf16[4,64,256]{2,1,0:T(8,128)(2,1)S(1)}, bf16[4,64,256]{2,1,0:T(8,128)(2,1)S(1)}, u32[]{:S(2)}, u32[]{:S(2)}) collective-permute-start(bf16[4,64,256]{2,1,0:T(8,128)(2,1)S(1)} %bitcast.3), channel_id=1, source_target_pairs={{0,1},{1,0},{2,3},{3,2},{4,5},{5,4},{6,7},{7,6},{8,9},{9,8},{10,11... | collective-permute-start | bytes 393224 | tf_op jit(solution)/shard_map/ppermute | solution.py:84
  7.5 1.9 %copy-start = (bf16[4,6,256,256]{3,2,1,0:T(8,128)(2,1)S(1)}, bf16[4,6,256,256]{3,2,1,0:T(8,128)(2,1)}, u32[]{:S(2)}) copy-start(bf16[4,6,256,256]{3,2,1,0:T(8,128)(2,1)} %refs_1_.1) | copy-start | bytes 9437188
  9.3 0.7 %copy-start.1 = (s32[4,6]{1,0:T(4,128)S(1)}, s32[4,6]{1,0:T(4,128)}, u32[]{:S(2)}) copy-start(s32[4,6]{1,0:T(4,128)} %screen.1) | copy-start | bytes 292
  10.0 0.7 %copy-start.2 = (s32[1,8]{1,0:T(1,128)S(1)}, s32[1,8]{1,0:T(1,128)}, u32[]{:S(2)}) copy-start(s32[1,8]{1,0:T(1,128)} %owner.1) | copy-start | bytes 100
  12.2 2.0 %collective-permute-start.1 = (f32[8,64,256]{2,1,0:T(8,128)S(1)}, f32[8,64,256]{2,1,0:T(8,128)S(1)}, u32[]{:S(2)}, u32[]{:S(2)}) collective-permute-start(f32[8,64,256]{2,1,0:T(8,128)S(1)} %get-tuple-element.11), channel_id=1, source_target_pairs={{0,2},{2,0},{4,6},{6,4},{8,10},{10,8},{12,14},{14,12},{16,18},{18,... | collective-permute-start | bytes 1572872 | tf_op jit(solution)/shard_map/ppermute | solution.py:80
  14.2 8.4 %collective-permute-start.2 = (f32[4,64,256]{2,1,0:T(8,128)S(1)}, f32[4,64,256]{2,1,0:T(8,128)S(1)}, u32[]{:S(2)}, u32[]{:S(2)}) collective-permute-start(f32[4,64,256]{2,1,0:T(8,128)S(1)} %slice_add_fusion), channel_id=1, source_target_pairs={{0,4},{2,6},{4,0},{6,2},{8,12},{10,14},{12,8},{14,10},{16,20},{18,... | collective-permute-start | bytes 786440 | tf_op jit(solution)/shard_map/ppermute | solution.py:80
  22.6 5.0 %collective-permute-start.3 = (f32[2,64,256]{2,1,0:T(8,128)S(1)}, f32[2,64,256]{2,1,0:T(8,128)S(1)}, u32[]{:S(2)}, u32[]{:S(2)}) collective-permute-start(f32[2,64,256]{2,1,0:T(8,128)S(1)} %slice_add_fusion.1), channel_id=1, source_target_pairs={{0,8},{2,10},{4,12},{6,14},{8,0},{10,2},{12,4},{14,6},{16,24},{18,... | collective-permute-start | bytes 393224 | tf_op jit(solution)/shard_map/ppermute | solution.py:80
  27.7 5.2 %collective-permute-start.4 = (f32[1,64,256]{2,1,0:T(8,128)S(1)}, f32[1,64,256]{2,1,0:T(8,128)S(1)}, u32[]{:S(2)}, u32[]{:S(2)}) collective-permute-start(f32[1,64,256]{2,1,0:T(8,128)S(1)} %get-tuple-element.15), channel_id=1, source_target_pairs={{0,16},{2,18},{4,20},{6,22},{8,24},{10,26},{12,28},{14,30},{16,0},... | collective-permute-start | bytes 196616 | tf_op jit(solution)/shard_map/ppermute | solution.py:80

commit v2 on v1

--- a/solution.py
+++ b/solution.py
@@ -7,37 +7,70 @@
 from jax.experimental.pallas import tpu as pltpu
 from jax.sharding import PartitionSpec as P
 
-def partial_kernel(n_col, masks, size, screen, owner, own, *refs):
-    others, integrals = refs[: n_col - 1], refs[n_col - 1]
-    send, keep = refs[n_col], refs[n_col + 1 : -3]
-    lhs, total, table = refs[-3:]
+def place_kernel(screen_hbm, owner_hbm, own_hbm, integrals, placed, own, screen, owner, table, raw, sems, small):
     tiles, slots = screen.shape
     targets = owner.shape[1]
-    half = own.shape[1]
+    loads = [
+        pltpu.make_async_copy(src, dst, small.at[at])
+        for at, (src, dst) in enumerate(((screen_hbm, screen), (owner_hbm, owner), (own_hbm, raw)))
+    ]
+    for load in loads:
+        load.start()
+    for at in range(tiles * targets):
+        table[at] = 0
+    for load in loads[:2]:
+        load.wait()
+
+    def live_copy(k, s):
+        name = screen[k, s]
+        t = owner[0, jnp.maximum(name, 0)]
+        copy = pltpu.make_async_copy(integrals.at[k, s], placed.at[t, k], sems.at[k, s])
+        return name >= 0, t, copy
+
+    for k in range(tiles):
+        for s in range(slots):
+            live, t, copy = live_copy(k, s)
+
+            @pl.when(live)
+            def _():
+                copy.start()
+                table[k * targets + t] = 1
+
+    loads[2].wait()
+    own[...] = jnp.swapaxes(raw[...], 0, 1)
+    for k in range(tiles):
+        for t in range(targets):
+
+            @pl.when(table[k * targets + t] == 0)
+            def _():
+                placed[t, k] = jnp.zeros(placed.shape[2:], placed.dtype)
+
+    for k in range(tiles):
+        for s in range(slots):
+            live, t, copy = live_copy(k, s)
+
+            @pl.when(live)
+            def _():
+                copy.wait()
+
+
+def partial_kernel(n_col, masks, size, own, *refs):
+    others, placed = refs[: n_col - 1], refs[n_col - 1]
+    send, keep = refs[n_col], refs[n_col + 1 : -2]
+    lhs, total = refs[-2:]
+    tiles, half, width = own.shape
+    targets = placed.shape[0]
     row, col = lax.axis_index("row"), lax.axis_index("col")
 
-    for at in range(tiles * targets):
-        table[at] = -1
-    for k in range(tiles):
-        for s in range(slots):
-            name = screen[k, s]
-            stored = owner[0, jnp.maximum(name, 0)]
-            table[jnp.where(name >= 0, k * targets + stored, tiles * targets)] = s
-
     for step in range(n_col):
-        source = own if step == 0 else others[step - 1]
+        source = own[...] if step == 0 else jnp.swapaxes(others[step - 1][...], 0, 1)
         owner_col = lax.rem(col + n_col - step, n_col)
         for k in range(tiles):
-            lhs[k, pl.ds(pl.multiple_of(owner_col * half, half), half), :] = source[k]
+            lhs[pl.ds(pl.multiple_of(owner_col * half, half), half), k * width : (k + 1) * width] = source[k]
 
     for t in range(targets):
-        acc = None
-        for k in range(tiles):
-            s = table[k * targets + t]
-            left = jnp.where(s >= 0, lhs[k], jnp.zeros_like(lhs[k]))
-            term = jnp.dot(left, integrals[k, jnp.maximum(s, 0)], preferred_element_type=jnp.float32)
-            acc = term if acc is None else acc + term
-        total[t] = acc
+        weights = placed[t].reshape(tiles * width, placed.shape[3])
+        total[t] = jnp.dot(lhs[...], weights, preferred_element_type=jnp.float32)
 
     def block(t, j):
         return total[t, pl.ds(pl.multiple_of((row ^ j) * size, size), size), :]
@@ -79,34 +112,51 @@
     def swap(x, mask):
         return lax.ppermute(x, "row", [(i, i ^ mask) for i in range(n_row)])
 
-    own = jnp.transpose(amplitudes, (1, 0, 2))
     others = [
-        lax.ppermute(own, "col", [(i, (i + step) % n_col) for i in range(n_col)])
+        lax.ppermute(amplitudes, "col", [(i, (i + step) % n_col) for i in range(n_col)])
         for step in range(1, n_col)
     ]
     sizes = [1 << (len(masks) - 1 - i) for i in range(len(masks))] + [1]
     block = (targets * size, out_width)
     spec = pl.BlockSpec(memory_space=pltpu.VMEM)
-    smem = pl.BlockSpec(memory_space=pltpu.SMEM)
+    hbm = pl.BlockSpec(memory_space=pl.ANY)
+    params = pltpu.CompilerParams(vmem_limit_bytes=24 * 1024 * 1024)
+    placed, own = pl.pallas_call(
+        place_kernel,
+        out_shape=[
+            pltpu.VMEM((targets, tiles, width, out_width), jnp.bfloat16),
+            pltpu.VMEM((tiles, half, width), jnp.bfloat16),
+        ],
+        in_specs=[hbm] * 4,
+        out_specs=[spec, spec],
+        scratch_shapes=[
+            pltpu.SMEM(screen.shape, jnp.int32),
+            pltpu.SMEM(owner_map.shape, jnp.int32),
+            pltpu.SMEM((tiles * targets,), jnp.int32),
+            pltpu.VMEM(amplitudes.shape, jnp.bfloat16),
+            pltpu.SemaphoreType.DMA(screen.shape),
+            pltpu.SemaphoreType.DMA((3,)),
+        ],
+        cost_estimate=pl.CostEstimate(flops=0, bytes_accessed=integrals.size * 2, transcendentals=0),
+        compiler_params=params,
+        name="place_tiles",
+    )(*[pltpu.with_memory_space_constraint(x, pltpu.HBM) for x in (screen, owner_map, amplitudes, integrals)])
     outs = pl.pallas_call(
         functools.partial(partial_kernel, n_col, masks, size),
         out_shape=[pltpu.VMEM((n_row // 2,) + block, jnp.float32)]
         + [pltpu.VMEM((n,) + block, jnp.float32) for n in sizes],
-        in_specs=[smem, smem] + [spec] * (n_col + 1),
+        in_specs=[spec] * (n_col + 1),
         out_specs=[spec] * (1 + len(sizes)),
         scratch_shapes=[
-            pltpu.VMEM((tiles, pairs, width), jnp.bfloat16),
+            pltpu.VMEM((pairs, tiles * width), jnp.bfloat16),
             pltpu.VMEM((targets, pairs, out_width), jnp.float32),
-            pltpu.SMEM((tiles * targets + 1,), jnp.int32),
         ],
         cost_estimate=pl.CostEstimate(
-            flops=2 * pairs * tiles * targets * width * out_width,
-            bytes_accessed=integrals.size * 2,
-            transcendentals=0,
+            flops=2 * pairs * tiles * targets * width * out_width, bytes_accessed=0, transcendentals=0
         ),
-        compiler_params=pltpu.CompilerParams(vmem_limit_bytes=24 * 1024 * 1024),
+        compiler_params=params,
         name="partial_sums",
-    )(screen, owner_map, vmem(own), *[vmem(o) for o in others], vmem(integrals))
+    )(vmem(own), *[vmem(o) for o in others], vmem(placed))
     send, keep = outs[0], list(outs[1:])
 
     got = swap(send, 1)

time: 33.8 us -> 29 us (0.86)
  local copies, waits for them, and re-layouts: 4.14 us -> 0 us
  waiting for transfers between devices: 17.6 us -> 15.1 us
  Pallas kernels: 2.13 us -> 4.1 us
    unnamed x7 -> x0, local copies, waits for them, and re-layouts: 4.14 us -> none
    pallas_call x0 -> x1, Pallas kernels: none -> 2.66 us  [body(): pl.pallas_call(place_kernel, out_shape=[pltpu.VMEM((targets, tiles, width...]
    ppermute x1, waiting for transfers between devices: 3.5 us -> 1.03 us  [body(): lax.ppermute(amplitudes, 'col', [(i, (i + step) % n_col) for i in range(n...]
    pallas_call x1, Pallas kernels: 1.47 us -> 0.79 us  [body(): pl.pallas_call(functools.partial(partial_kernel, n_col, masks, size), out...]
  transfers between devices with their start and end apart: 5 -> 5, of which waited for: 5 -> 5; matrix products, arithmetic and copies ran while one was open for 0% -> 0% of each run, Pallas kernels for 0% -> 9%
where the time goes in v2:
time: 29 us; the launch traced here: 28.9 us
  waiting for transfers between devices  15.1 us (52%)
  starting transfers between devices  9.56 us (33%)
  Pallas kernels  4.1 us (14%)
    ppermute x4, waiting for transfers between devices, swap(): return lax.ppermute(x, 'row', [(i, i ^ mask) for i in range(n_row)])  14 us
    ppermute x4, starting transfers between devices, swap(): return lax.ppermute(x, 'row', [(i, i ^ mask) for i in range(n_row)])  6.59 us
    ppermute x1, starting transfers between devices, body(): lax.ppermute(amplitudes, 'col', [(i, (i + step) % n_col) for i in range(n...  2.97 us
    pallas_call x1, Pallas kernels, body(): pl.pallas_call(place_kernel, out_shape=[pltpu.VMEM((targets, tiles, width...  2.66 us
    ppermute x1, waiting for transfers between devices, body(): lax.ppermute(amplitudes, 'col', [(i, (i + step) % n_col) for i in range(n...  1.03 us
    pallas_call x1, Pallas kernels, body(): pl.pallas_call(functools.partial(partial_kernel, n_col, masks, size), out...  0.79 us
    pallas_call x1, Pallas kernels, body(): pl.pallas_call(functools.partial(final_kernel, targets, size), out_shape=...  0.65 us
  transfers between devices with their start and end apart: 5, of which 5 were waited for; matrix products, arithmetic and copies ran while one was open for 0% of the time, Pallas kernels for 9%

profile of v2, /device:TPU:0, one launch (start us, length us, event | category | flops | bytes accessed | tf_op | source)
XLA Modules:
  0.0 28.9 jit_solution(11820624558337670631)
XLA Ops:
  0.0 3.0 %collective-permute-start = (bf16[64,4,256]{2,1,0:T(4,128)(2,1)}, bf16[64,4,256]{2,1,0:T(4,128)(2,1)S(1)}, u32[]{:S(2)}, u32[]{:S(2)}) collective-permute-start(bf16[64,4,256]{2,1,0:T(4,128)(2,1)} %own_hbm.1), channel_id=1, source_target_pairs={{0,1},{1,0},{2,3},{3,2},{4,5},{5,4},{6,7},{7,6},{8,9},{9,8},{10,11... | collective-permute-start | bytes 393224 | tf_op jit(solution)/shard_map/ppermute | solution.py:116
  3.0 2.7 %place_tiles.1 = (bf16[8,4,256,256]{3,2,1,0:T(8,128)(2,1)S(1)}, bf16[4,64,256]{2,1,0:T(8,128)(2,1)S(1)}) custom-call(s32[4,6]{1,0:T(4,128)} %screen_hbm.1, s32[1,8]{1,0:T(1,128)} %owner_hbm.1, bf16[64,4,256]{2,1,0:T(4,128)(2,1)} %own_hbm.1, bf16[4,6,256,256]{3,2,1,0:T(8,128)(2,1)} %integrals.1), custom_call_target="tpu_custom_call" | custom-call | bytes 3145728 | tf_op jit(solution)/shard_map/place_tiles/pallas_call | solution.py:124
  5.6 1.0 %collective-permute-done.refs_0_ = bf16[64,4,256]{2,1,0:T(4,128)(2,1)S(1)} collective-permute-done((bf16[64,4,256]{2,1,0:T(4,128)(2,1)}, bf16[64,4,256]{2,1,0:T(4,128)(2,1)S(1)}, u32[]{:S(2)}, u32[]{:S(2)}) %collective-permute-start) | collective-permute-done | bytes 131104 | tf_op jit(solution)/shard_map/ppermute | solution.py:116
  6.7 0.8 %partial_sums.1 = (f32[8,64,256]{2,1,0:T(8,128)S(1)}, f32[4,64,256]{2,1,0:T(8,128)S(1)}, f32[2,64,256]{2,1,0:T(8,128)S(1)}, f32[1,64,256]{2,1,0:T(8,128)S(1)}, f32[1,64,256]{2,1,0:T(8,128)S(1)}) custom-call(bf16[4,64,256]{2,1,0:T(8,128)(2,1)S(1)} %get-tuple-element.12.own, bf16[64,4,256]{2,1,0:T(4,128)(2,1)S(1)} %collective-permute-done.refs_0_, ...), custom_call_target="tpu_custom_call" | custom-call | flops 536870912 | tf_op jit(solution)/shard_map/partial_sums/pallas_call | solution.py:144
  7.5 0.1 collective-permute-start.1
  7.5 1.9 %collective-permute-done.1 = f32[8,64,256]{2,1,0:T(8,128)S(1)} collective-permute-done((f32[8,64,256]{2,1,0:T(8,128)S(1)}, f32[8,64,256]{2,1,0:T(8,128)S(1)}, u32[]{:S(2)}, u32[]{:S(2)}) %collective-permute-start.1) | collective-permute-done | bytes 524320 | tf_op jit(solution)/shard_map/ppermute | solution.py:113
  9.5 1.8 %collective-permute-start.2 = (f32[4,64,256]{2,1,0:T(8,128)S(1)}, f32[4,64,256]{2,1,0:T(8,128)S(1)}, u32[]{:S(2)}, u32[]{:S(2)}) collective-permute-start(f32[4,64,256]{2,1,0:T(8,128)S(1)} %slice_add_fusion), channel_id=1, source_target_pairs={{0,4},{2,6},{4,0},{6,2},{8,12},{10,14},{12,8},{14,10},{16,20},{18,... | collective-permute-start | bytes 786440 | tf_op jit(solution)/shard_map/ppermute | solution.py:113
  11.3 6.6 %collective-permute-done.2 = f32[4,64,256]{2,1,0:T(8,128)S(1)} collective-permute-done((f32[4,64,256]{2,1,0:T(8,128)S(1)}, f32[4,64,256]{2,1,0:T(8,128)S(1)}, u32[]{:S(2)}, u32[]{:S(2)}) %collective-permute-start.2) | collective-permute-done | bytes 262176 | tf_op jit(solution)/shard_map/ppermute | solution.py:113
  17.9 1.9 %collective-permute-start.3 = (f32[2,64,256]{2,1,0:T(8,128)S(1)}, f32[2,64,256]{2,1,0:T(8,128)S(1)}, u32[]{:S(2)}, u32[]{:S(2)}) collective-permute-start(f32[2,64,256]{2,1,0:T(8,128)S(1)} %slice_add_fusion.1), channel_id=1, source_target_pairs={{0,8},{2,10},{4,12},{6,14},{8,0},{10,2},{12,4},{14,6},{16,24},{18,... | collective-permute-start | bytes 393224 | tf_op jit(solution)/shard_map/ppermute | solution.py:113
  19.8 3.2 %collective-permute-done.3 = f32[2,64,256]{2,1,0:T(8,128)S(1)} collective-permute-done((f32[2,64,256]{2,1,0:T(8,128)S(1)}, f32[2,64,256]{2,1,0:T(8,128)S(1)}, u32[]{:S(2)}, u32[]{:S(2)}) %collective-permute-start.3) | collective-permute-done | bytes 131104 | tf_op jit(solution)/shard_map/ppermute | solution.py:113
  23.0 2.9 %collective-permute-start.4 = (f32[1,64,256]{2,1,0:T(8,128)S(1)}, f32[1,64,256]{2,1,0:T(8,128)S(1)}, u32[]{:S(2)}, u32[]{:S(2)}) collective-permute-start(f32[1,64,256]{2,1,0:T(8,128)S(1)} %get-tuple-element.19), channel_id=1, source_target_pairs={{0,16},{2,18},{4,20},{6,22},{8,24},{10,26},{12,28},{14,30},{16,0},... | collective-permute-start | bytes 196616 | tf_op jit(solution)/shard_map/ppermute | solution.py:113
  25.9 2.4 %collective-permute-done.4.b = f32[1,64,256]{2,1,0:T(8,128)S(1)} collective-permute-done((f32[1,64,256]{2,1,0:T(8,128)S(1)}, f32[1,64,256]{2,1,0:T(8,128)S(1)}, u32[]{:S(2)}, u32[]{:S(2)}) %collective-permute-start.4) | collective-permute-done | bytes 65568 | tf_op jit(solution)/shard_map/ppermute | solution.py:113
  28.2 0.7 %own_block.1 = f32[8,8,256]{2,1,0:T(8,128)} custom-call(f32[1,64,256]{2,1,0:T(8,128)S(1)} %get-tuple-element.20.a, f32[1,64,256]{2,1,0:T(8,128)S(1)} %collective-permute-done.4.b), custom_call_target="tpu_custom_call" | custom-call | tf_op jit(solution)/shard_map/own_block/pallas_call | solution.py:174
  (3 shorter events, 0.1 us)
Async XLA Ops:
  0.0 6.7 %collective-permute-start = (bf16[64,4,256]{2,1,0:T(4,128)(2,1)}, bf16[64,4,256]{2,1,0:T(4,128)(2,1)S(1)}, u32[]{:S(2)}, u32[]{:S(2)}) collective-permute-start(bf16[64,4,256]{2,1,0:T(4,128)(2,1)} %own_hbm.1), channel_id=1, source_target_pairs={{0,1},{1,0},{2,3},{3,2},{4,5},{5,4},{6,7},{7,6},{8,9},{9,8},{10,11... | collective-permute-start | bytes 393224 | tf_op jit(solution)/shard_map/ppermute | solution.py:116
  7.5 2.0 %collective-permute-start.1 = (f32[8,64,256]{2,1,0:T(8,128)S(1)}, f32[8,64,256]{2,1,0:T(8,128)S(1)}, u32[]{:S(2)}, u32[]{:S(2)}) collective-permute-start(f32[8,64,256]{2,1,0:T(8,128)S(1)} %get-tuple-element.15), channel_id=1, source_target_pairs={{0,2},{2,0},{4,6},{6,4},{8,10},{10,8},{12,14},{14,12},{16,18},{18,... | collective-permute-start | bytes 1572872 | tf_op jit(solution)/shard_map/ppermute | solution.py:113
  9.5 8.4 %collective-permute-start.2 = (f32[4,64,256]{2,1,0:T(8,128)S(1)}, f32[4,64,256]{2,1,0:T(8,128)S(1)}, u32[]{:S(2)}, u32[]{:S(2)}) collective-permute-start(f32[4,64,256]{2,1,0:T(8,128)S(1)} %slice_add_fusion), channel_id=1, source_target_pairs={{0,4},{2,6},{4,0},{6,2},{8,12},{10,14},{12,8},{14,10},{16,20},{18,... | collective-permute-start | bytes 786440 | tf_op jit(solution)/shard_map/ppermute | solution.py:113
  17.9 5.0 %collective-permute-start.3 = (f32[2,64,256]{2,1,0:T(8,128)S(1)}, f32[2,64,256]{2,1,0:T(8,128)S(1)}, u32[]{:S(2)}, u32[]{:S(2)}) collective-permute-start(f32[2,64,256]{2,1,0:T(8,128)S(1)} %slice_add_fusion.1), channel_id=1, source_target_pairs={{0,8},{2,10},{4,12},{6,14},{8,0},{10,2},{12,4},{14,6},{16,24},{18,... | collective-permute-start | bytes 393224 | tf_op jit(solution)/shard_map/ppermute | solution.py:113
  23.0 5.2 %collective-permute-start.4 = (f32[1,64,256]{2,1,0:T(8,128)S(1)}, f32[1,64,256]{2,1,0:T(8,128)S(1)}, u32[]{:S(2)}, u32[]{:S(2)}) collective-permute-start(f32[1,64,256]{2,1,0:T(8,128)S(1)} %get-tuple-element.19), channel_id=1, source_target_pairs={{0,16},{2,18},{4,20},{6,22},{8,24},{10,26},{12,28},{14,30},{16,0},... | collective-permute-start | bytes 196616 | tf_op jit(solution)/shard_map/ppermute | solution.py:113

commit v3 on v2

--- a/solution.py
+++ b/solution.py
@@ -6,6 +6,9 @@
 from jax.experimental import pallas as pl
 from jax.experimental.pallas import tpu as pltpu
 from jax.sharding import PartitionSpec as P
+
+SPARE = 16
+LEAST = -100
 
 def place_kernel(screen_hbm, owner_hbm, own_hbm, integrals, placed, own, screen, owner, table, raw, sems, small):
     tiles, slots = screen.shape
@@ -54,10 +57,9 @@
                 copy.wait()
 
 
-def partial_kernel(n_col, masks, size, own, *refs):
+def partial_kernel(n_col, order, size, own, *refs):
     others, placed = refs[: n_col - 1], refs[n_col - 1]
-    send, keep = refs[n_col], refs[n_col + 1 : -2]
-    lhs, total = refs[-2:]
+    send, keep, lhs, total = refs[n_col:]
     tiles, half, width = own.shape
     targets = placed.shape[0]
     row, col = lax.axis_index("row"), lax.axis_index("col")
@@ -75,24 +77,69 @@
     def block(t, j):
         return total[t, pl.ds(pl.multiple_of((row ^ j) * size, size), size), :]
 
-    order = [0]
-    for m in reversed(masks):
-        order = order + [m ^ o for o in order]
-    parts, low = [], 0
-    for ref in reversed(keep):
-        parts.append((ref, order[low : low + ref.shape[0]]))
-        low += ref.shape[0]
     for t in range(targets):
         rows = pl.ds(t * size, size)
         for at, j in enumerate(order):
             send[at, rows, :] = block(t, j ^ 1)
-        for ref, js in parts:
-            for at, j in enumerate(js):
-                ref[at, rows, :] = block(t, j)
-
-
-def final_kernel(targets, size, a, b, out):
-    x = a[0] + b[0]
+            keep[at, rows, :] = block(t, j)
+
+
+def encode(values, out):
+    rows, width = values[0].shape
+    at_row = lax.broadcasted_iota(jnp.int32, (SPARE, width), 0)
+    exponents = jnp.zeros((SPARE, width), jnp.int32)
+    for at, x in enumerate(values):
+        largest = jnp.maximum(jnp.max(jnp.abs(x), axis=0, keepdims=True), 2.0**LEAST)
+        exponent = jnp.floor(jnp.log2(largest)) + 1.0
+        code = jnp.round(x * jnp.exp2(15.0 - exponent))
+        code = jnp.clip(code, -32767.0, 32767.0).astype(jnp.int32)
+        out[at * rows : (at + 1) * rows, :] = code.astype(jnp.int16)
+        exponents = jnp.where(at_row == at, exponent.astype(jnp.int32), exponents)
+    out[len(values) * rows :, :] = exponents.astype(jnp.int16)
+
+
+def decode(coded, at, rows):
+    count = (coded.shape[0] - SPARE) // rows
+    exponents = coded[count * rows :, :].astype(jnp.int32)[at : at + 1, :].astype(jnp.float32)
+    code = coded[at * rows : (at + 1) * rows, :].astype(jnp.int32).astype(jnp.float32)
+    return code * jnp.exp2(exponents - 15.0)
+
+
+def first_kernel(groups, keep, got, *outs):
+    at = 0
+    for out, count in zip(outs, groups):
+        values = [keep[at + i] + got[at + i] for i in range(count)]
+        if out is outs[-1]:
+            for i in range(count):
+                out[i] = values[i]
+        else:
+            encode(values, out)
+        at += count
+
+
+def next_kernel(groups, arrived, keep, *refs):
+    coded, outs = refs[:arrived], refs[arrived:]
+    at = 0
+    for out, count in zip(outs, groups):
+        values = []
+        for i in range(at, at + count):
+            x = keep[i]
+            for part in coded:
+                x = x + decode(part, i, keep.shape[1])
+            values.append(x)
+        if out is outs[-1]:
+            for i in range(count):
+                out[i] = values[i]
+        else:
+            encode(values, out)
+        at += count
+
+
+def final_kernel(targets, size, keep, *refs):
+    coded, out = refs[:-1], refs[-1]
+    x = keep[0]
+    for part in coded:
+        x = x + decode(part, 0, targets * size)
     for t in range(targets):
         out[:, t, :] = x[t * size : (t + 1) * size, :]
 
@@ -116,7 +163,14 @@
         lax.ppermute(amplitudes, "col", [(i, (i + step) % n_col) for i in range(n_col)])
         for step in range(1, n_col)
     ]
-    sizes = [1 << (len(masks) - 1 - i) for i in range(len(masks))] + [1]
+    stages = [masks[at : at + 2] for at in range(0, len(masks), 2)]
+    plans, order = [], [0]
+    for stage in reversed(stages):
+        partners = [0]
+        for mask in stage:
+            partners = [mask | p for p in partners] + partners
+        plans.insert(0, (partners[:-1], len(order)))
+        order = [p ^ o for p in partners for o in order]
     block = (targets * size, out_width)
     spec = pl.BlockSpec(memory_space=pltpu.VMEM)
     hbm = pl.BlockSpec(memory_space=pl.ANY)
@@ -142,11 +196,10 @@
         name="place_tiles",
     )(*[pltpu.with_memory_space_constraint(x, pltpu.HBM) for x in (screen, owner_map, amplitudes, integrals)])
     outs = pl.pallas_call(
-        functools.partial(partial_kernel, n_col, masks, size),
-        out_shape=[pltpu.VMEM((n_row // 2,) + block, jnp.float32)]
-        + [pltpu.VMEM((n,) + block, jnp.float32) for n in sizes],
+        functools.partial(partial_kernel, n_col, order, size),
+        out_shape=[pltpu.VMEM((len(order),) + block, jnp.float32)] * 2,
         in_specs=[spec] * (n_col + 1),
-        out_specs=[spec] * (1 + len(sizes)),
+        out_specs=[spec] * 2,
         scratch_shapes=[
             pltpu.VMEM((pairs, tiles * width), jnp.bfloat16),
             pltpu.VMEM((targets, pairs, out_width), jnp.float32),
@@ -157,27 +210,33 @@
         compiler_params=params,
         name="partial_sums",
     )(vmem(own), *[vmem(o) for o in others], vmem(placed))
-    send, keep = outs[0], list(outs[1:])
-
-    got = swap(send, 1)
-    for at, mask in enumerate([None] + masks[:-1]):
-        if mask is not None:
-            got = swap(keep[0], mask)
-            keep = keep[1:]
-        top = got.shape[0]
-        fresh = []
-        for part in keep:
-            fresh.append(part + got[top - part.shape[0] : top])
-            top -= part.shape[0]
-        keep = fresh
-    got = swap(keep[0], masks[-1])
+    send, keep = outs
+    arrived = [swap(send, 1)]
+    for at, (partners, count) in enumerate(plans):
+        groups = [count] * (len(partners) + 1)
+        step = (
+            functools.partial(first_kernel, groups)
+            if at == 0
+            else functools.partial(next_kernel, groups, len(arrived))
+        )
+        *coded, keep = pl.pallas_call(
+            step,
+            out_shape=[pltpu.VMEM((count * block[0] + SPARE, out_width), jnp.int16)] * len(partners)
+            + [pltpu.VMEM((count,) + block, jnp.float32)],
+            in_specs=[spec] * (1 + len(arrived)),
+            out_specs=[spec] * (1 + len(partners)),
+            compiler_params=params,
+            name="encode_stage",
+        )(vmem(keep), *[vmem(part) for part in arrived])
+        arrived = [swap(part, partner) for part, partner in zip(coded, partners)]
     return pl.pallas_call(
         functools.partial(final_kernel, targets, size),
         out_shape=jax.ShapeDtypeStruct((size, targets, out_width), jnp.float32),
-        in_specs=[spec, spec],
+        in_specs=[spec] * (1 + len(arrived)),
         out_specs=spec,
+        compiler_params=params,
         name="own_block",
-    )(vmem(keep[1]), vmem(got))
+    )(vmem(keep), *[vmem(part) for part in arrived])
 
 
 def solution(mesh):

time: 29 us -> 23 us (0.79)
  waiting for transfers between devices: 15.1 us -> 9.26 us
  starting transfers between devices: 9.56 us -> 9.24 us
    ppermute x4 -> x5, waiting for transfers between devices: 14 us -> 8.26 us  [swap(): return lax.ppermute(x, 'row', [(i, i ^ mask) for i in range(n_row)])]
    ppermute x4 -> x5, starting transfers between devices: 6.59 us -> 6.27 us  [swap(): return lax.ppermute(x, 'row', [(i, i ^ mask) for i in range(n_row)])]
    pallas_call x1 -> x3, Pallas kernels: 0.79 us -> 0.98 us  [the longest x1 0.79 us: body(): pl.pallas_call(functools.partial(partial_kernel, n_col, order, size), out...]
  transfers between devices with their start and end apart: 5 -> 6, of which waited for: 5 -> 6; matrix products, arithmetic and copies ran while one was open for 0% -> 0% of each run, Pallas kernels for 9% -> 12%
where the time goes in v3:
time: 23 us; the launch traced here: 22.9 us
  waiting for transfers between devices  9.26 us (40%)
  starting transfers between devices  9.24 us (40%)
  Pallas kernels  4.34 us (19%)
    ppermute x5, waiting for transfers between devices, swap(): return lax.ppermute(x, 'row', [(i, i ^ mask) for i in range(n_row)])  8.26 us
    ppermute x5, starting transfers between devices, swap(): return lax.ppermute(x, 'row', [(i, i ^ mask) for i in range(n_row)])  6.27 us
    ppermute x1, starting transfers between devices, body(): lax.ppermute(amplitudes, 'col', [(i, (i + step) % n_col) for i in range(n...  2.97 us
    pallas_call x1, Pallas kernels, body(): pl.pallas_call(place_kernel, out_shape=[pltpu.VMEM((targets, tiles, width...  2.7 us
    ppermute x1, waiting for transfers between devices, body(): lax.ppermute(amplitudes, 'col', [(i, (i + step) % n_col) for i in range(n...  1 us
    pallas_call x1, Pallas kernels, body(): pl.pallas_call(functools.partial(partial_kernel, n_col, order, size), out...  0.79 us
    pallas_call x1, Pallas kernels, body(): pl.pallas_call(functools.partial(final_kernel, targets, size), out_shape=...  0.67 us
  transfers between devices with their start and end apart: 6, of which 6 were waited for; matrix products, arithmetic and copies ran while one was open for 0% of the time, Pallas kernels for 12%

profile of v3, /device:TPU:0, one launch (start us, length us, event | category | flops | bytes accessed | tf_op | source)
XLA Modules:
  0.0 22.9 jit_solution(8866267032113289508)
XLA Ops:
  0.0 3.0 %collective-permute-start = (bf16[64,4,256]{2,1,0:T(4,128)(2,1)}, bf16[64,4,256]{2,1,0:T(4,128)(2,1)S(1)}, u32[]{:S(2)}, u32[]{:S(2)}) collective-permute-start(bf16[64,4,256]{2,1,0:T(4,128)(2,1)} %own_hbm.1), channel_id=1, source_target_pairs={{0,1},{1,0},{2,3},{3,2},{4,5},{5,4},{6,7},{7,6},{8,9},{9,8},{10,11... | collective-permute-start | bytes 393224 | tf_op jit(solution)/shard_map/ppermute | solution.py:163
  3.0 2.7 %place_tiles.1 = (bf16[8,4,256,256]{3,2,1,0:T(8,128)(2,1)S(1)}, bf16[4,64,256]{2,1,0:T(8,128)(2,1)S(1)}) custom-call(s32[4,6]{1,0:T(4,128)} %screen_hbm.1, s32[1,8]{1,0:T(1,128)} %owner_hbm.1, bf16[64,4,256]{2,1,0:T(4,128)(2,1)} %own_hbm.1, bf16[4,6,256,256]{3,2,1,0:T(8,128)(2,1)} %integrals.1), custom_call_target="tpu_custom_call" | custom-call | bytes 3145728 | tf_op jit(solution)/shard_map/place_tiles/pallas_call | solution.py:178
  5.7 1.0 %collective-permute-done.refs_0_ = bf16[64,4,256]{2,1,0:T(4,128)(2,1)S(1)} collective-permute-done((bf16[64,4,256]{2,1,0:T(4,128)(2,1)}, bf16[64,4,256]{2,1,0:T(4,128)(2,1)S(1)}, u32[]{:S(2)}, u32[]{:S(2)}) %collective-permute-start) | collective-permute-done | bytes 131104 | tf_op jit(solution)/shard_map/ppermute | solution.py:163
  6.7 0.8 %partial_sums.1 = (f32[8,64,256]{2,1,0:T(8,128)S(1)}, f32[8,64,256]{2,1,0:T(8,128)S(1)}) custom-call(bf16[4,64,256]{2,1,0:T(8,128)(2,1)S(1)} %get-tuple-element.15.own, bf16[64,4,256]{2,1,0:T(4,128)(2,1)S(1)} %collective-permute-done.refs_0_, bf16[8,4,256,256]{3,2,1,0:T(8,128)(2,1)S(1)} %get-tuple-element.16.refs_1_), custom_call_target="tpu_custom_call" | custom-call | flops 536870912 | tf_op jit(solution)/shard_map/partial_sums/pallas_call | solution.py:198
  7.5 0.1 collective-permute-start.1
  7.5 1.9 %collective-permute-done.1.got = f32[8,64,256]{2,1,0:T(8,128)S(1)} collective-permute-done((f32[8,64,256]{2,1,0:T(8,128)S(1)}, f32[8,64,256]{2,1,0:T(8,128)S(1)}, u32[]{:S(2)}, u32[]{:S(2)}) %collective-permute-start.1) | collective-permute-done | bytes 524320 | tf_op jit(solution)/shard_map/ppermute | solution.py:160
  9.4 0.1 encode_stage.2
  9.6 2.8 %collective-permute-start.2 = (s16[144,256]{1,0:T(8,128)(2,1)S(1)}, s16[144,256]{1,0:T(8,128)(2,1)S(1)}, u32[]{:S(2)}, u32[]{:S(2)}) collective-permute-start(s16[144,256]{1,0:T(8,128)(2,1)S(1)} %get-tuple-element.20), channel_id=1, source_target_pairs={{0,12},{2,14},{4,8},{6,10},{8,4},{10,6},{12,0},{14,2},{16,28},{18,... | collective-permute-start | bytes 221192 | tf_op jit(solution)/shard_map/ppermute | solution.py:160
  12.4 0.5 %collective-permute-start.3 = (s16[144,256]{1,0:T(8,128)(2,1)S(1)}, s16[144,256]{1,0:T(8,128)(2,1)S(1)}, u32[]{:S(2)}, u32[]{:S(2)}) collective-permute-start(s16[144,256]{1,0:T(8,128)(2,1)S(1)} %get-tuple-element.21), channel_id=1, source_target_pairs={{0,8},{2,10},{4,12},{6,14},{8,0},{10,2},{12,4},{14,6},{16,24},{18,... | collective-permute-start | bytes 221192 | tf_op jit(solution)/shard_map/ppermute | solution.py:160
  12.8 0.3 %collective-permute-start.4 = (s16[144,256]{1,0:T(8,128)(2,1)S(1)}, s16[144,256]{1,0:T(8,128)(2,1)S(1)}, u32[]{:S(2)}, u32[]{:S(2)}) collective-permute-start(s16[144,256]{1,0:T(8,128)(2,1)S(1)} %get-tuple-element.22), channel_id=1, source_target_pairs={{0,4},{2,6},{4,0},{6,2},{8,12},{10,14},{12,8},{14,10},{16,20},{18,... | collective-permute-start | bytes 221192 | tf_op jit(solution)/shard_map/ppermute | solution.py:160
  13.1 2.0 %collective-permute-done.2.refs_0_ = s16[144,256]{1,0:T(8,128)(2,1)S(1)} collective-permute-done((s16[144,256]{1,0:T(8,128)(2,1)S(1)}, s16[144,256]{1,0:T(8,128)(2,1)S(1)}, u32[]{:S(2)}, u32[]{:S(2)}) %collective-permute-start.2) | collective-permute-done | bytes 73760 | tf_op jit(solution)/shard_map/ppermute | solution.py:160
  15.1 1.6 %collective-permute-done.3.refs_1_ = s16[144,256]{1,0:T(8,128)(2,1)S(1)} collective-permute-done((s16[144,256]{1,0:T(8,128)(2,1)S(1)}, s16[144,256]{1,0:T(8,128)(2,1)S(1)}, u32[]{:S(2)}, u32[]{:S(2)}) %collective-permute-start.3) | collective-permute-done | bytes 73760 | tf_op jit(solution)/shard_map/ppermute | solution.py:160
  16.7 0.4 %collective-permute-done.4.refs_2_ = s16[144,256]{1,0:T(8,128)(2,1)S(1)} collective-permute-done((s16[144,256]{1,0:T(8,128)(2,1)S(1)}, s16[144,256]{1,0:T(8,128)(2,1)S(1)}, u32[]{:S(2)}, u32[]{:S(2)}) %collective-permute-start.4) | collective-permute-done | bytes 73760 | tf_op jit(solution)/shard_map/ppermute | solution.py:160
  17.2 0.1 encode_stage.3
  17.2 2.6 %collective-permute-start.5 = (s16[80,256]{1,0:T(8,128)(2,1)S(1)}, s16[80,256]{1,0:T(8,128)(2,1)S(1)}, u32[]{:S(2)}, u32[]{:S(2)}) collective-permute-start(s16[80,256]{1,0:T(8,128)(2,1)S(1)} %get-tuple-element.24), channel_id=1, source_target_pairs={{0,16},{2,18},{4,20},{6,22},{8,24},{10,26},{12,28},{14,30},{16,0},... | collective-permute-start | bytes 122888 | tf_op jit(solution)/shard_map/ppermute | solution.py:160
  19.9 2.3 %collective-permute-done.5.refs_0_ = s16[80,256]{1,0:T(8,128)(2,1)S(1)} collective-permute-done((s16[80,256]{1,0:T(8,128)(2,1)S(1)}, s16[80,256]{1,0:T(8,128)(2,1)S(1)}, u32[]{:S(2)}, u32[]{:S(2)}) %collective-permute-start.5) | collective-permute-done | bytes 40992 | tf_op jit(solution)/shard_map/ppermute | solution.py:160
  22.2 0.7 %own_block.1 = f32[8,8,256]{2,1,0:T(8,128)} custom-call(f32[1,64,256]{2,1,0:T(8,128)S(1)} %get-tuple-element.23.keep, s16[80,256]{1,0:T(8,128)(2,1)S(1)} %collective-permute-done.5.refs_0_), custom_call_target="tpu_custom_call" | custom-call | tf_op jit(solution)/shard_map/own_block/pallas_call | solution.py:232
Async XLA Ops:
  0.0 6.7 %collective-permute-start = (bf16[64,4,256]{2,1,0:T(4,128)(2,1)}, bf16[64,4,256]{2,1,0:T(4,128)(2,1)S(1)}, u32[]{:S(2)}, u32[]{:S(2)}) collective-permute-start(bf16[64,4,256]{2,1,0:T(4,128)(2,1)} %own_hbm.1), channel_id=1, source_target_pairs={{0,1},{1,0},{2,3},{3,2},{4,5},{5,4},{6,7},{7,6},{8,9},{9,8},{10,11... | collective-permute-start | bytes 393224 | tf_op jit(solution)/shard_map/ppermute | solution.py:163
  7.5 2.0 %collective-permute-start.1 = (f32[8,64,256]{2,1,0:T(8,128)S(1)}, f32[8,64,256]{2,1,0:T(8,128)S(1)}, u32[]{:S(2)}, u32[]{:S(2)}) collective-permute-start(f32[8,64,256]{2,1,0:T(8,128)S(1)} %get-tuple-element.18), channel_id=1, source_target_pairs={{0,2},{2,0},{4,6},{6,4},{8,10},{10,8},{12,14},{14,12},{16,18},{18,... | collective-permute-start | bytes 1572872 | tf_op jit(solution)/shard_map/ppermute | solution.py:160
  9.6 5.6 %collective-permute-start.2 = (s16[144,256]{1,0:T(8,128)(2,1)S(1)}, s16[144,256]{1,0:T(8,128)(2,1)S(1)}, u32[]{:S(2)}, u32[]{:S(2)}) collective-permute-start(s16[144,256]{1,0:T(8,128)(2,1)S(1)} %get-tuple-element.20), channel_id=1, source_target_pairs={{0,12},{2,14},{4,8},{6,10},{8,4},{10,6},{12,0},{14,2},{16,28},{18,... | collective-permute-start | bytes 221192 | tf_op jit(solution)/shard_map/ppermute | solution.py:160
  12.4 4.4 %collective-permute-start.3 = (s16[144,256]{1,0:T(8,128)(2,1)S(1)}, s16[144,256]{1,0:T(8,128)(2,1)S(1)}, u32[]{:S(2)}, u32[]{:S(2)}) collective-permute-start(s16[144,256]{1,0:T(8,128)(2,1)S(1)} %get-tuple-element.21), channel_id=1, source_target_pairs={{0,8},{2,10},{4,12},{6,14},{8,0},{10,2},{12,4},{14,6},{16,24},{18,... | collective-permute-start | bytes 221192 | tf_op jit(solution)/shard_map/ppermute | solution.py:160
  12.8 4.4 %collective-permute-start.4 = (s16[144,256]{1,0:T(8,128)(2,1)S(1)}, s16[144,256]{1,0:T(8,128)(2,1)S(1)}, u32[]{:S(2)}, u32[]{:S(2)}) collective-permute-start(s16[144,256]{1,0:T(8,128)(2,1)S(1)} %get-tuple-element.22), channel_id=1, source_target_pairs={{0,4},{2,6},{4,0},{6,2},{8,12},{10,14},{12,8},{14,10},{16,20},{18,... | collective-permute-start | bytes 221192 | tf_op jit(solution)/shard_map/ppermute | solution.py:160
  17.2 5.0 %collective-permute-start.5 = (s16[80,256]{1,0:T(8,128)(2,1)S(1)}, s16[80,256]{1,0:T(8,128)(2,1)S(1)}, u32[]{:S(2)}, u32[]{:S(2)}) collective-permute-start(s16[80,256]{1,0:T(8,128)(2,1)S(1)} %get-tuple-element.24), channel_id=1, source_target_pairs={{0,16},{2,18},{4,20},{6,22},{8,24},{10,26},{12,28},{14,30},{16,0},... | collective-permute-start | bytes 122888 | tf_op jit(solution)/shard_map/ppermute | solution.py:160

commit v4 on v0

v4 whole, which is shorter than its diff:
```python
import functools

import jax
import jax.numpy as jnp
from jax import lax
from jax.experimental import pallas as pl
from jax.experimental.pallas import tpu as pltpu
from jax.sharding import PartitionSpec as P

SPARE = 16
LEAST = -100
LANES = 128
ACROSS, ALONG = 2, 4


def place(size, total, places):
    targets, near = total.shape[0] - 1, total.shape[1] // size
    low = lax.rem(lax.axis_index("row"), near)
    for ref, at, offset in places:
        first = pl.multiple_of((low ^ offset) * size, size)
        for t in range(targets):
            ref[at, t * size : (t + 1) * size, :] = total[t, pl.ds(first, size), :]


def lay_out(size, totals, keep, send):
    second = lax.rem(lax.axis_index("row"), 2) == 1
    mine, other = jnp.where(second, ALONG, ACROSS), jnp.where(second, ACROSS, ALONG)
    for h, total in enumerate(totals):
        kept = (ACROSS | ALONG, mine, mine ^ 1, 0)
        sent = (ACROSS | ALONG | 1, other ^ 1, other, 1)
        places = [(keep, 4 * h + at, j) for at, j in enumerate(kept)]
        place(size, total, places + [(send, 4 * h + at, j) for at, j in enumerate(sent)])


def sides(raw):
    by_tile = jnp.swapaxes(raw, 0, 1)
    return [by_tile[k] for k in range(by_tile.shape[0])]


def spare(count):
    return -(-count // SPARE) * SPARE


def encode(values, out):
    rows, width = values[0].shape
    pieces = [x[:, c : c + LANES] for x in values for c in range(0, width, LANES)]
    last = spare(len(pieces))
    at_row = lax.broadcasted_iota(jnp.int32, (last, LANES), 0)
    exponents = jnp.zeros((last, LANES), jnp.int32)
    for at, x in enumerate(pieces):
        largest = jnp.maximum(jnp.max(jnp.abs(x), axis=0, keepdims=True), 2.0**LEAST)
        exponent = jnp.floor(jnp.log2(largest)) + 1.0
        code = jnp.round(x * jnp.exp2(15.0 - exponent))
        code = jnp.clip(code, -32767.0, 32767.0).astype(jnp.int32)
        out[at * rows : (at + 1) * rows, :] = code.astype(jnp.int16)
        exponents = jnp.where(at_row == at, exponent.astype(jnp.int32), exponents)
    data = len(pieces) * rows
    for at in range(data, out.shape[0] - last, SPARE):
        out[at : at + SPARE, :] = jnp.zeros((SPARE, LANES), jnp.int16)
    out[out.shape[0] - last :, :] = exponents.astype(jnp.int16)


def decode(coded, at, rows, width):
    each = width // LANES
    count = coded.shape[0] // rows
    exponents = coded[coded.shape[0] - spare(count) :, :].astype(jnp.int32)
    parts = []
    for i in range(at * each, (at + 1) * each):
        code = coded[i * rows : (i + 1) * rows, :].astype(jnp.int32).astype(jnp.float32)
        parts.append(code * jnp.exp2(exponents[i : i + 1, :].astype(jnp.float32) - 15.0))
    return jnp.concatenate(parts, axis=1)


def early_kernel(
    size, screen_hbm, owner_hbm, own_hbm, integrals,
    tiles, aim, send, keep, screen, owner, raw, total, sems, small,
):
    depth, slots = screen.shape
    targets = owner.shape[1]
    loads = [
        pltpu.make_async_copy(src, dst, small.at[at])
        for at, (src, dst) in enumerate(((screen_hbm, screen), (owner_hbm, owner), (own_hbm, raw)))
    ]

    for load in loads:
        load.start()
    copies = [
        pltpu.make_async_copy(integrals.at[k], tiles.at[pl.ds(k * slots, slots)], sems.at[k]) for k in range(depth)
    ]
    for at, copy in enumerate(copies):
        copy.start(priority=min(at, 1))
    total[...] = jnp.zeros(total.shape, total.dtype)
    for load in loads:
        load.wait()
    for k in range(depth):
        for s in range(slots):
            name = screen[k, s]
            aim[k * slots + s] = jnp.where(name >= 0, owner[0, jnp.maximum(name, 0)], targets)
    lhs = sides(raw[...])
    for k in range(depth):
        copies[k].wait()
        for s in range(slots):
            add_tile(lhs[k], tiles, aim, k * slots + s, total)
    lay_out(size, [total], keep, send)


def add_tile(lhs, tiles, aim, i, total):
    t = aim[i]
    total[t] += jnp.dot(lhs, tiles[i], preferred_element_type=jnp.float32)


def late_kernel(size, count, *refs):
    others, (tiles, aim, out, keep, send, totals) = refs[:count], refs[count:]
    slots = aim.shape[0] // others[0].shape[1]
    totals[...] = jnp.zeros(totals.shape, totals.dtype)
    for h, raw in enumerate(others):
        lhs = sides(raw[...])
        for i in range(aim.shape[0]):
            add_tile(lhs[i // slots], tiles, aim, i, totals.at[h])
    lay_out(size, [totals.at[h] for h in range(count)], keep, send)
    encode([send[i] for i in range(4 * count)], out)


def early_sums_kernel(keep, got, ahead, out):
    sums = [keep[at] + got[at] for at in range(4)]
    encode(sums[1:3], ahead)
    out[0] = sums[0]
    out[1] = sums[3]


def near_kernel(n_col, early, late_keep, late_got, side, diagonal, out):
    rows, width = early.shape[1:]
    sums = []
    for at in range(4):
        sums.append([late_keep[i] + decode(late_got, i, rows, width) for i in range(at, (n_col - 1) * 4, 4)])
    encode(sums[1] + sums[2], side)
    encode([early[0]] + sums[0], diagonal)
    out[0] = early[1]
    for h in range(n_col - 1):
        out[1 + h] = sums[3][h]


def emit(groups, values, outs):
    at = 0
    for out, count in zip(outs, groups):
        if out is outs[-1]:
            for i in range(count):
                out[i] = values[at + i]
        else:
            encode(values[at : at + count], out)
        at += count


def pass_kernel(rows, each, ahead, side, out):
    late = (side.shape[0] // rows) // 2
    out[:rows, :] = ahead[rows : 2 * rows, :]
    out[rows : (1 + late) * rows, :] = side[late * rows : 2 * late * rows, :]
    first = ahead[ahead.shape[0] - SPARE :, :].astype(jnp.int32)[each : 2 * each]
    rest = side[2 * late * rows :, :].astype(jnp.int32)[late * each : 2 * late * each]
    last = out.shape[0] - (1 + late) * rows
    lines = [first, rest]
    if last > (1 + late) * each:
        lines.append(jnp.zeros((last - (1 + late) * each, LANES), jnp.int32))
    out[(1 + late) * rows :, :] = jnp.concatenate(lines, axis=0).astype(jnp.int16)


def sort_kernel(n_col, near, far, groups, keep, ahead, side, diagonal, passed, *refs):
    outs, sums = refs[:-1], refs[-1]
    rows, width = keep.shape[1:]
    for h in range(n_col):
        x = keep[h] + (decode(ahead, 0, rows, width) if h == 0 else decode(side, h - 1, rows, width))
        x = x + decode(passed, h, rows, width)
        sums[h] = x + decode(diagonal, h, rows, width)
    high, col = lax.axis_index("row") // near, lax.axis_index("col")
    emit(groups, [sums[lax.rem(col + n_col - (high ^ j), n_col)] for j in far], outs)


def far_kernel(groups, arrived, keep, *refs):
    coded, outs = refs[:arrived], refs[arrived:]
    rows, width = keep.shape[1:]
    values = []
    for i in range(sum(groups)):
        x = keep[i]
        for part in coded:
            x = x + decode(part, i, rows, width)
        values.append(x)
    emit(groups, values, outs)


def last_kernel(targets, size, keep, *refs):
    coded, out = refs[:-1], refs[-1]
    x = keep[0]
    for part in coded:
        x = x + decode(part, 0, targets * size, x.shape[1])
    for t in range(targets):
        out[:, t, :] = x[t * size : (t + 1) * size, :]


def offsets(masks):
    order = [0]
    for mask in masks:
        order = [mask | o for o in order] + order
    return order


def body(n_row, n_col, amplitudes, integrals, screen, owner_map):
    half, depth, width = amplitudes.shape
    slots, targets, out_width = integrals.shape[1], owner_map.shape[1], integrals.shape[3]
    size = half * n_col // n_row
    near = n_row // n_col
    spec = pl.BlockSpec(memory_space=pltpu.VMEM)
    smem = pl.BlockSpec(memory_space=pltpu.SMEM)
    hbm = pl.BlockSpec(memory_space=pltpu.HBM)
    params = pltpu.CompilerParams(vmem_limit_bytes=24 * 1024 * 1024)
    block = (targets * size, out_width)

    def vmem(x):
        return pltpu.with_memory_space_constraint(x, pltpu.VMEM)

    def swap(x, mask):
        return lax.ppermute(x, "row", [(i, i ^ mask) for i in range(n_row)])

    def call(kernel, name, out_shape, *operands, **more):
        single = not isinstance(out_shape, list)
        return pl.pallas_call(
            kernel,
            out_shape=out_shape,
            in_specs=[spec] * len(operands),
            out_specs=spec if single else [spec] * len(out_shape),
            compiler_params=params,
            name=name,
            **more,
        )(*[vmem(x) for x in operands])

    def coded(count, more=0):
        count *= out_width // LANES
        return pltpu.VMEM((count * block[0] + more + spare(count), LANES), jnp.int16)

    def kept(count):
        return pltpu.VMEM((count,) + block, jnp.float32)

    others = [
        lax.ppermute(amplitudes, "col", [(i, (i + step) % n_col) for i in range(n_col)])
        for step in range(1, n_col)
    ]
    half_cost = pl.CostEstimate(
        flops=2 * half * depth * targets * width * out_width, bytes_accessed=0, transcendentals=0
    )
    tiles, aim, send, keep = pl.pallas_call(
        functools.partial(early_kernel, size),
        out_shape=[
            pltpu.VMEM((depth * slots, width, out_width), jnp.bfloat16),
            pltpu.SMEM((depth * slots,), jnp.int32),
            kept(4),
            kept(4),
        ],
        in_specs=[hbm] * 4,
        out_specs=[spec, smem, spec, spec],
        scratch_shapes=[
            pltpu.SMEM(screen.shape, jnp.int32),
            pltpu.SMEM(owner_map.shape, jnp.int32),
            pltpu.VMEM(amplitudes.shape, jnp.bfloat16),
            pltpu.VMEM((targets + 1, half, out_width), jnp.float32),
            pltpu.SemaphoreType.DMA((depth,)),
            pltpu.SemaphoreType.DMA((3,)),
        ],
        cost_estimate=pl.CostEstimate(
            flops=half_cost.flops, bytes_accessed=integrals.size * 2, transcendentals=0
        ),
        compiler_params=params,
        name="early_half",
    )(*[pltpu.with_memory_space_constraint(x, pltpu.HBM) for x in (screen, owner_map, amplitudes, integrals)])
    got = swap(send, 1)

    lates = n_col - 1
    late_send, late_keep = pl.pallas_call(
        functools.partial(late_kernel, size, lates),
        out_shape=[coded(lates * 4), kept(lates * 4)],
        in_specs=[spec] * n_col + [smem],
        out_specs=[spec, spec],
        scratch_shapes=[
            pltpu.VMEM((lates * 4,) + block, jnp.float32),
            pltpu.VMEM((lates, targets + 1, half, out_width), jnp.float32),
        ],
        cost_estimate=half_cost,
        compiler_params=params,
        name="late_half",
    )(*[vmem(o) for o in others], vmem(tiles), pltpu.with_memory_space_constraint(aim, pltpu.SMEM))
    late_got = swap(late_send, 1)
    def to_side(x):
        return lax.ppermute(x, "row", [(i, i ^ (ALONG if i % 2 else ACROSS)) for i in range(n_row)])

    ahead, early = call(early_sums_kernel, "early_sums", [coded(2, SPARE), kept(2)], keep, got)
    ahead = to_side(ahead)
    side, diagonal, keep = call(
        functools.partial(near_kernel, n_col),
        "near_sums",
        [coded(2 * lates), coded(n_col), kept(n_col)],
        early,
        late_keep,
        late_got,
    )
    side = to_side(side)
    diagonal = swap(diagonal, ACROSS | ALONG)
    each = out_width // LANES
    passed = call(functools.partial(pass_kernel, each * block[0], each), "pass_on", coded(n_col), ahead, side)
    arrived = [ahead, side, diagonal, swap(passed, 1)]

    masks = [near << b for b in range(n_col.bit_length() - 1)]
    plans, far = [], [0]
    for stage in reversed([masks[at : at + 2] for at in range(0, len(masks), 2)]):
        partners = offsets(stage)
        plans.insert(0, (partners, len(far)))
        far = [p | o for p in partners for o in far]
    for at, (partners, count) in enumerate(plans):
        groups = [count] * len(partners)
        if at == 0:
            offs = [o // near for o in far]
            kernel = functools.partial(sort_kernel, n_col, near, offs, groups)
            more = dict(scratch_shapes=[pltpu.VMEM((n_col,) + block, jnp.float32)])
        else:
            kernel, more = functools.partial(far_kernel, groups, len(arrived)), {}
        *parts, keep = call(
            kernel, "far_sums", [coded(count)] * (len(partners) - 1) + [kept(count)], keep, *arrived, **more
        )
        arrived = [swap(part, partner) for part, partner in zip(parts, partners)]
    return pl.pallas_call(
        functools.partial(last_kernel, targets, size),
        out_shape=jax.ShapeDtypeStruct((size, targets, out_width), jnp.float32),
        in_specs=[spec] * (1 + len(arrived)),
        out_specs=spec,
        compiler_params=params,
        name="own_block",
    )(vmem(keep), *[vmem(part) for part in arrived])


def solution(mesh):
    return jax.shard_map(
        functools.partial(body, mesh.shape["row"], mesh.shape["col"]),
        mesh=mesh,
        in_specs=(
            P("col", "row", None),
            P("row", "col", None, None),
            P("row", "col"),
            P("col", None),
        ),
        out_specs=P("row", "col", None),
        check_vma=False,
    )
```

time: 91.3 us -> 22.2 us (0.24)
  waiting for transfers between devices: 59.1 us -> 7.17 us
  between operations: 13.4 us -> 0.08 us
  starting transfers between devices: 0.01 us -> 10.7 us
  blocking collectives: 7.12 us -> 0 us
  matrix products: 5.22 us -> 0 us
  local copies, waits for them, and re-layouts: 4.57 us -> 0 us
  Pallas kernels: 0 us -> 4.1 us
  other arithmetic: 1.73 us -> 0 us
    reduce_scatter x1 -> x0, waiting for transfers between devices: 59.1 us -> none  [body(): lax.psum_scatter(jnp.einsum('pkw,kawv->pav', gathered, placed, preferred_...]
    ppermute x0 -> x8, starting transfers between devices: none -> 10.7 us  [the longest x5 4.72 us: swap(): return lax.ppermute(x, 'row', [(i, i ^ mask) for i in range(n_row)])]
    ppermute x0 -> x8, waiting for transfers between devices: none -> 7.17 us  [the longest x5 4.67 us: swap(): return lax.ppermute(x, 'row', [(i, i ^ mask) for i in range(n_row)])]
    all_gather x1 -> x0, blocking collectives: 7.12 us -> none  [body(): gathered = lax.all_gather(amplitudes, 'col', axis=0, tiled=True)]
    dot_general x2 -> x0, matrix products: 5.22 us -> none  [the longest x1 3.24 us: body(): jnp.einsum('pkw,kawv->pav', gathered, placed, preferred_element_type=jnp....]
    pallas_call x0 -> x7, Pallas kernels: none -> 4.1 us  [the longest x1 2.38 us: body(): pl.pallas_call(functools.partial(early_kernel, size), out_shape=[pltpu.VM...]
    dot_general x1 -> x0, local copies, waits for them, and re-layouts: 2.66 us -> none  [body(): jnp.einsum('pkw,kawv->pav', gathered, placed, preferred_element_type=jnp....]
    unnamed x4 -> x0, local copies, waits for them, and re-layouts: 1.82 us -> none
  transfers between devices with their start and end apart: 1 -> 8, of which waited for: 1 -> 4; matrix products, arithmetic and copies ran while one was open for 0% -> 0% of each run, Pallas kernels for 0% -> 15%
where the time goes in v4:
time: 22.2 us; the launch traced here: 22.1 us
  starting transfers between devices  10.7 us (48%)
  waiting for transfers between devices  7.17 us (32%)
  Pallas kernels  4.1 us (18%)
    ppermute x5, starting transfers between devices, swap(): return lax.ppermute(x, 'row', [(i, i ^ mask) for i in range(n_row)])  4.72 us
    ppermute x5, waiting for transfers between devices, swap(): return lax.ppermute(x, 'row', [(i, i ^ mask) for i in range(n_row)])  4.67 us
    ppermute x2, starting transfers between devices, to_side(): lax.ppermute(x, 'row', [(i, i ^ (ALONG if i % 2 else ACROSS)) for i in ra...  3.03 us
    ppermute x1, starting transfers between devices, body(): lax.ppermute(amplitudes, 'col', [(i, (i + step) % n_col) for i in range(n...  2.97 us
    pallas_call x1, Pallas kernels, body(): pl.pallas_call(functools.partial(early_kernel, size), out_shape=[pltpu.VM...  2.38 us
    ppermute x2, waiting for transfers between devices, to_side(): lax.ppermute(x, 'row', [(i, i ^ (ALONG if i % 2 else ACROSS)) for i in ra...  1.27 us
    ppermute x1, waiting for transfers between devices, body(): lax.ppermute(amplitudes, 'col', [(i, (i + step) % n_col) for i in range(n...  1.24 us
    pallas_call x1, Pallas kernels, body(): pl.pallas_call(functools.partial(late_kernel, size, lates), out_shape=[co...  0.77 us
  transfers between devices with their start and end apart: 8, of which 4 were waited for; matrix products, arithmetic and copies ran while one was open for 0% of the time, Pallas kernels for 15%

profile of v4, /device:TPU:0, one launch (start us, length us, event | category | flops | bytes accessed | tf_op | source)
XLA Modules:
  0.0 22.1 jit_solution(3490910734709909416)
XLA Ops:
  0.0 3.0 %collective-permute-start.1 = (bf16[64,4,256]{2,1,0:T(4,128)(2,1)}, bf16[64,4,256]{2,1,0:T(4,128)(2,1)S(1)}, u32[]{:S(2)}, u32[]{:S(2)}) collective-permute-start(bf16[64,4,256]{2,1,0:T(4,128)(2,1)} %own_hbm.1), channel_id=1, source_target_pairs={{0,1},{1,0},{2,3},{3,2},{4,5},{5,4},{6,7},{7,6},{8,9},{9,8},{10,11... | collective-permute-start | bytes 393224 | tf_op jit(solution)/shard_map/ppermute | solution.py:243
  3.0 2.4 %early_half.1 = (bf16[24,256,256]{2,1,0:T(8,128)(2,1)S(1)}, s32[24]{0:T(128)S(4)}, f32[4,64,256]{2,1,0:T(8,128)S(1)}, f32[4,64,256]{2,1,0:T(8,128)S(1)}) custom-call(s32[4,6]{1,0:T(4,128)} %screen_hbm.1, s32[1,8]{1,0:T(1,128)} %owner_hbm.1, bf16[64,4,256]{2,1,0:T(4,128)(2,1)} %own_hbm.1, bf16[4,6,256,256]{3,2,1,0:T(8,128)(2,1)} %integrals.1), custom_call_target="tpu_custom_call" | custom-call | flops 268435456 | bytes 3145728 | tf_op jit(solution)/shard_map/early_half/pallas_call | solution.py:249
  5.4 0.1 collective-permute-start
  5.4 1.2 %collective-permute-done.1.refs_0_ = bf16[64,4,256]{2,1,0:T(4,128)(2,1)S(1)} collective-permute-done((bf16[64,4,256]{2,1,0:T(4,128)(2,1)}, bf16[64,4,256]{2,1,0:T(4,128)(2,1)S(1)}, u32[]{:S(2)}, u32[]{:S(2)}) %collective-permute-start.1) | collective-permute-done | bytes 131104 | tf_op jit(solution)/shard_map/ppermute | solution.py:243
  6.7 0.8 %late_half.1 = (s16[528,128]{1,0:T(8,128)(2,1)S(1)}, f32[4,64,256]{2,1,0:T(8,128)S(1)}) custom-call(bf16[64,4,256]{2,1,0:T(4,128)(2,1)S(1)} %collective-permute-done.1.refs_0_, bf16[24,256,256]{2,1,0:T(8,128)(2,1)S(1)} %get-tuple-element.21.refs_1_, s32[24]{0:T(128)S(4)} %get-tuple-element.22.refs_2_), custom_call_target="tpu_custom_call" | custom-call | flops 268435456 | tf_op jit(solution)/shard_map/late_half/pallas_call | solution.py:276
  7.4 0.1 collective-permute-start.2
  7.5 0.0 collective-permute-done.got
  7.5 0.1 early_sums.1
  7.6 1.8 %collective-permute-start.3 = (s16[288,128]{1,0:T(8,128)(2,1)S(1)}, s16[288,128]{1,0:T(8,128)(2,1)S(1)}, u32[]{:S(2)}, u32[]{:S(2)}) collective-permute-start(s16[288,128]{1,0:T(8,128)(2,1)S(1)} %get-tuple-element.26), channel_id=1, source_target_pairs={{0,4},{2,10},{4,0},{6,14},{8,12},{10,2},{12,8},{14,6},{16,20},{18,... | collective-permute-start | bytes 221192 | tf_op jit(solution)/shard_map/ppermute | solution.py:291
  9.4 0.0 collective-permute-done.2.late_got
  9.4 0.1 near_sums.1
  9.5 1.3 %collective-permute-start.4 = (s16[272,128]{1,0:T(8,128)(2,1)S(1)}, s16[272,128]{1,0:T(8,128)(2,1)S(1)}, u32[]{:S(2)}, u32[]{:S(2)}) collective-permute-start(s16[272,128]{1,0:T(8,128)(2,1)S(1)} %get-tuple-element.27), channel_id=1, source_target_pairs={{0,4},{2,10},{4,0},{6,14},{8,12},{10,2},{12,8},{14,6},{16,20},{18,... | collective-permute-start | bytes 208904 | tf_op jit(solution)/shard_map/ppermute | solution.py:291
  10.8 1.9 %collective-permute-start.5 = (s16[272,128]{1,0:T(8,128)(2,1)S(1)}, s16[272,128]{1,0:T(8,128)(2,1)S(1)}, u32[]{:S(2)}, u32[]{:S(2)}) collective-permute-start(s16[272,128]{1,0:T(8,128)(2,1)S(1)} %get-tuple-element.28), channel_id=1, source_target_pairs={{0,12},{2,14},{4,8},{6,10},{8,4},{10,6},{12,0},{14,2},{16,28},{18,... | collective-permute-start | bytes 208904 | tf_op jit(solution)/shard_map/ppermute | solution.py:221
  12.6 0.0 collective-permute-done.3.ahead
  12.6 1.3 %collective-permute-done.4.side = s16[272,128]{1,0:T(8,128)(2,1)S(1)} collective-permute-done((s16[272,128]{1,0:T(8,128)(2,1)S(1)}, s16[272,128]{1,0:T(8,128)(2,1)S(1)}, u32[]{:S(2)}, u32[]{:S(2)}) %collective-permute-start.4) | collective-permute-done | bytes 69664 | tf_op jit(solution)/shard_map/ppermute | solution.py:291
  13.9 0.1 collective-permute-start.6
  14.0 2.0 %collective-permute-done.5.diagonal = s16[272,128]{1,0:T(8,128)(2,1)S(1)} collective-permute-done((s16[272,128]{1,0:T(8,128)(2,1)S(1)}, s16[272,128]{1,0:T(8,128)(2,1)S(1)}, u32[]{:S(2)}, u32[]{:S(2)}) %collective-permute-start.5) | collective-permute-done | bytes 69664 | tf_op jit(solution)/shard_map/ppermute | solution.py:221
  16.0 0.0 collective-permute-done.6.passed
  16.0 0.1 far_sums.1
  16.1 2.7 %collective-permute-start.7 = (s16[144,128]{1,0:T(8,128)(2,1)S(1)}, s16[144,128]{1,0:T(8,128)(2,1)S(1)}, u32[]{:S(2)}, u32[]{:S(2)}) collective-permute-start(s16[144,128]{1,0:T(8,128)(2,1)S(1)} %get-tuple-element.30), channel_id=1, source_target_pairs={{0,16},{2,18},{4,20},{6,22},{8,24},{10,26},{12,28},{14,30},{16,0},... | collective-permute-start | bytes 110600 | tf_op jit(solution)/shard_map/ppermute | solution.py:221
  18.7 2.7 %collective-permute-done.7.refs_0_ = s16[144,128]{1,0:T(8,128)(2,1)S(1)} collective-permute-done((s16[144,128]{1,0:T(8,128)(2,1)S(1)}, s16[144,128]{1,0:T(8,128)(2,1)S(1)}, u32[]{:S(2)}, u32[]{:S(2)}) %collective-permute-start.7) | collective-permute-done | bytes 36896 | tf_op jit(solution)/shard_map/ppermute | solution.py:221
  21.4 0.7 %own_block.1 = f32[8,8,256]{2,1,0:T(8,128)} custom-call(f32[1,64,256]{2,1,0:T(8,128)S(1)} %get-tuple-element.29.keep, s16[144,128]{1,0:T(8,128)(2,1)S(1)} %collective-permute-done.7.refs_0_), custom_call_target="tpu_custom_call" | custom-call | tf_op jit(solution)/shard_map/own_block/pallas_call | solution.py:327
  (1 shorter events, 0.0 us)
Async XLA Ops:
  0.0 6.7 %collective-permute-start.1 = (bf16[64,4,256]{2,1,0:T(4,128)(2,1)}, bf16[64,4,256]{2,1,0:T(4,128)(2,1)S(1)}, u32[]{:S(2)}, u32[]{:S(2)}) collective-permute-start(bf16[64,4,256]{2,1,0:T(4,128)(2,1)} %own_hbm.1), channel_id=1, source_target_pairs={{0,1},{1,0},{2,3},{3,2},{4,5},{5,4},{6,7},{7,6},{8,9},{9,8},{10,11... | collective-permute-start | bytes 393224 | tf_op jit(solution)/shard_map/ppermute | solution.py:243
  5.4 2.2 %collective-permute-start = (f32[4,64,256]{2,1,0:T(8,128)S(1)}, f32[4,64,256]{2,1,0:T(8,128)S(1)}, u32[]{:S(2)}, u32[]{:S(2)}) collective-permute-start(f32[4,64,256]{2,1,0:T(8,128)S(1)} %get-tuple-element.19), channel_id=1, source_target_pairs={{0,2},{2,0},{4,6},{6,4},{8,10},{10,8},{12,14},{14,12},{16,18},{18,... | collective-permute-start | bytes 786440 | tf_op jit(solution)/shard_map/ppermute | solution.py:221
  7.4 1.9 %collective-permute-start.2 = (s16[528,128]{1,0:T(8,128)(2,1)S(1)}, s16[528,128]{1,0:T(8,128)(2,1)S(1)}, u32[]{:S(2)}, u32[]{:S(2)}) collective-permute-start(s16[528,128]{1,0:T(8,128)(2,1)S(1)} %get-tuple-element.24), channel_id=1, source_target_pairs={{0,2},{2,0},{4,6},{6,4},{8,10},{10,8},{12,14},{14,12},{16,18},{18,... | collective-permute-start | bytes 405512 | tf_op jit(solution)/shard_map/ppermute | solution.py:221
  7.6 5.0 %collective-permute-start.3 = (s16[288,128]{1,0:T(8,128)(2,1)S(1)}, s16[288,128]{1,0:T(8,128)(2,1)S(1)}, u32[]{:S(2)}, u32[]{:S(2)}) collective-permute-start(s16[288,128]{1,0:T(8,128)(2,1)S(1)} %get-tuple-element.26), channel_id=1, source_target_pairs={{0,4},{2,10},{4,0},{6,14},{8,12},{10,2},{12,8},{14,6},{16,20},{18,... | collective-permute-start | bytes 221192 | tf_op jit(solution)/shard_map/ppermute | solution.py:291
  9.5 4.4 %collective-permute-start.4 = (s16[272,128]{1,0:T(8,128)(2,1)S(1)}, s16[272,128]{1,0:T(8,128)(2,1)S(1)}, u32[]{:S(2)}, u32[]{:S(2)}) collective-permute-start(s16[272,128]{1,0:T(8,128)(2,1)S(1)} %get-tuple-element.27), channel_id=1, source_target_pairs={{0,4},{2,10},{4,0},{6,14},{8,12},{10,2},{12,8},{14,6},{16,20},{18,... | collective-permute-start | bytes 208904 | tf_op jit(solution)/shard_map/ppermute | solution.py:291
  10.8 5.2 %collective-permute-start.5 = (s16[272,128]{1,0:T(8,128)(2,1)S(1)}, s16[272,128]{1,0:T(8,128)(2,1)S(1)}, u32[]{:S(2)}, u32[]{:S(2)}) collective-permute-start(s16[272,128]{1,0:T(8,128)(2,1)S(1)} %get-tuple-element.28), channel_id=1, source_target_pairs={{0,12},{2,14},{4,8},{6,10},{8,4},{10,6},{12,0},{14,2},{16,28},{18,... | collective-permute-start | bytes 208904 | tf_op jit(solution)/shard_map/ppermute | solution.py:221
  13.9 2.1 %collective-permute-start.6 = (s16[272,128]{1,0:T(8,128)(2,1)S(1)}, s16[272,128]{1,0:T(8,128)(2,1)S(1)}, u32[]{:S(2)}, u32[]{:S(2)}) collective-permute-start(s16[272,128]{1,0:T(8,128)(2,1)S(1)} %pass_on.1), channel_id=1, source_target_pairs={{0,2},{2,0},{4,6},{6,4},{8,10},{10,8},{12,14},{14,12},{16,18},{18,... | collective-permute-start | bytes 208904 | tf_op jit(solution)/shard_map/ppermute | solution.py:221
  16.1 5.3 %collective-permute-start.7 = (s16[144,128]{1,0:T(8,128)(2,1)S(1)}, s16[144,128]{1,0:T(8,128)(2,1)S(1)}, u32[]{:S(2)}, u32[]{:S(2)}) collective-permute-start(s16[144,128]{1,0:T(8,128)(2,1)S(1)} %get-tuple-element.30), channel_id=1, source_target_pairs={{0,16},{2,18},{4,20},{6,22},{8,24},{10,26},{12,28},{14,30},{16,0},... | collective-permute-start | bytes 110600 | tf_op jit(solution)/shard_map/ppermute | solution.py:221

commit v5 on v4

--- a/solution.py
+++ b/solution.py
@@ -22,14 +22,24 @@
             ref[at, t * size : (t + 1) * size, :] = total[t, pl.ds(first, size), :]
 
 
-def lay_out(size, totals, keep, send):
-    second = lax.rem(lax.axis_index("row"), 2) == 1
+def pairs_of(masks):
+    return [masks[at : at + 2] for at in range(0, len(masks), 2)]
+
+
+def lay_out(size, n_col, step, totals, keep, send):
+    row, col = lax.axis_index("row"), lax.axis_index("col")
+    second = lax.rem(row, 2) == 1
     mine, other = jnp.where(second, ALONG, ACROSS), jnp.where(second, ACROSS, ALONG)
+    near = totals[0].shape[1] // size
     for h, total in enumerate(totals):
+        offset = (row // near) ^ lax.rem(col + n_col - step - h, n_col)
+        flip = 0
+        for stage in pairs_of([1 << b for b in range(n_col.bit_length() - 1)]):
+            flip = flip ^ jnp.where(offset & sum(stage) != 0, 1, 0)
         kept = (ACROSS | ALONG, mine, mine ^ 1, 0)
         sent = (ACROSS | ALONG | 1, other ^ 1, other, 1)
-        places = [(keep, 4 * h + at, j) for at, j in enumerate(kept)]
-        place(size, total, places + [(send, 4 * h + at, j) for at, j in enumerate(sent)])
+        places = [(keep, 4 * h + at, j ^ flip) for at, j in enumerate(kept)]
+        place(size, total, places + [(send, 4 * h + at, j ^ flip) for at, j in enumerate(sent)])
 
 
 def sides(raw):
@@ -72,7 +82,7 @@
 
 
 def early_kernel(
-    size, screen_hbm, owner_hbm, own_hbm, integrals,
+    size, n_col, screen_hbm, owner_hbm, own_hbm, integrals,
     tiles, aim, send, keep, screen, owner, raw, total, sems, small,
 ):
     depth, slots = screen.shape
@@ -101,7 +111,7 @@
         copies[k].wait()
         for s in range(slots):
             add_tile(lhs[k], tiles, aim, k * slots + s, total)
-    lay_out(size, [total], keep, send)
+    lay_out(size, n_col, 0, [total], keep, send)
 
 
 def add_tile(lhs, tiles, aim, i, total):
@@ -117,7 +127,7 @@
         lhs = sides(raw[...])
         for i in range(aim.shape[0]):
             add_tile(lhs[i // slots], tiles, aim, i, totals.at[h])
-    lay_out(size, [totals.at[h] for h in range(count)], keep, send)
+    lay_out(size, count + 1, 1, [totals.at[h] for h in range(count)], keep, send)
     encode([send[i] for i in range(4 * count)], out)
 
 
@@ -247,7 +257,7 @@
         flops=2 * half * depth * targets * width * out_width, bytes_accessed=0, transcendentals=0
     )
     tiles, aim, send, keep = pl.pallas_call(
-        functools.partial(early_kernel, size),
+        functools.partial(early_kernel, size, n_col),
         out_shape=[
             pltpu.VMEM((depth * slots, width, out_width), jnp.bfloat16),
             pltpu.SMEM((depth * slots,), jnp.int32),
@@ -308,7 +318,7 @@
 
     masks = [near << b for b in range(n_col.bit_length() - 1)]
     plans, far = [], [0]
-    for stage in reversed([masks[at : at + 2] for at in range(0, len(masks), 2)]):
+    for stage in reversed(pairs_of(masks)):
         partners = offsets(stage)
         plans.insert(0, (partners, len(far)))
         far = [p | o for p in partners for o in far]
@@ -323,7 +333,7 @@
         *parts, keep = call(
             kernel, "far_sums", [coded(count)] * (len(partners) - 1) + [kept(count)], keep, *arrived, **more
         )
-        arrived = [swap(part, partner) for part, partner in zip(parts, partners)]
+        arrived = [swap(part, partner | 1) for part, partner in zip(parts, partners)]
     return pl.pallas_call(
         functools.partial(last_kernel, targets, size),
         out_shape=jax.ShapeDtypeStruct((size, targets, out_width), jnp.float32),

time: 22.2 us -> 21.4 us (0.964)
  starting transfers between devices: 10.7 us -> 9.73 us
    ppermute x5, starting transfers between devices: 4.72 us -> 3.73 us  [swap(): return lax.ppermute(x, 'row', [(i, i ^ mask) for i in range(n_row)])]
  transfers between devices with their start and end apart: 8 -> 8, of which waited for: 4 -> 4; matrix products, arithmetic and copies ran while one was open for 0% -> 0% of each run, Pallas kernels for 15% -> 16%
where the time goes in v5:
time: 21.4 us; the launch traced here: 21.3 us
  starting transfers between devices  9.73 us (45%)
  waiting for transfers between devices  7.34 us (34%)
  Pallas kernels  4.1 us (19%)
    ppermute x5, waiting for transfers between devices, swap(): return lax.ppermute(x, 'row', [(i, i ^ mask) for i in range(n_row)])  4.83 us
    ppermute x5, starting transfers between devices, swap(): return lax.ppermute(x, 'row', [(i, i ^ mask) for i in range(n_row)])  3.73 us
    ppermute x2, starting transfers between devices, to_side(): lax.ppermute(x, 'row', [(i, i ^ (ALONG if i % 2 else ACROSS)) for i in ra...  3.03 us
    ppermute x1, starting transfers between devices, body(): lax.ppermute(amplitudes, 'col', [(i, (i + step) % n_col) for i in range(n...  2.97 us
    pallas_call x1, Pallas kernels, body(): pl.pallas_call(functools.partial(early_kernel, size, n_col), out_shape=[p...  2.38 us
    ppermute x2, waiting for transfers between devices, to_side(): lax.ppermute(x, 'row', [(i, i ^ (ALONG if i % 2 else ACROSS)) for i in ra...  1.27 us
    ppermute x1, waiting for transfers between devices, body(): lax.ppermute(amplitudes, 'col', [(i, (i + step) % n_col) for i in range(n...  1.24 us
    pallas_call x1, Pallas kernels, body(): pl.pallas_call(functools.partial(late_kernel, size, lates), out_shape=[co...  0.77 us
  transfers between devices with their start and end apart: 8, of which 4 were waited for; matrix products, arithmetic and copies ran while one was open for 0% of the time, Pallas kernels for 16%

profile of v5, /device:TPU:0, one launch (start us, length us, event | category | flops | bytes accessed | tf_op | source)
XLA Modules:
  0.0 21.3 jit_solution(10530293704775672392)
XLA Ops:
  0.0 3.0 %collective-permute-start.1 = (bf16[64,4,256]{2,1,0:T(4,128)(2,1)}, bf16[64,4,256]{2,1,0:T(4,128)(2,1)S(1)}, u32[]{:S(2)}, u32[]{:S(2)}) collective-permute-start(bf16[64,4,256]{2,1,0:T(4,128)(2,1)} %own_hbm.1), channel_id=1, source_target_pairs={{0,1},{1,0},{2,3},{3,2},{4,5},{5,4},{6,7},{7,6},{8,9},{9,8},{10,11... | collective-permute-start | bytes 393224 | tf_op jit(solution)/shard_map/ppermute | solution.py:253
  3.0 2.4 %early_half.1 = (bf16[24,256,256]{2,1,0:T(8,128)(2,1)S(1)}, s32[24]{0:T(128)S(4)}, f32[4,64,256]{2,1,0:T(8,128)S(1)}, f32[4,64,256]{2,1,0:T(8,128)S(1)}) custom-call(s32[4,6]{1,0:T(4,128)} %screen_hbm.1, s32[1,8]{1,0:T(1,128)} %owner_hbm.1, bf16[64,4,256]{2,1,0:T(4,128)(2,1)} %own_hbm.1, bf16[4,6,256,256]{3,2,1,0:T(8,128)(2,1)} %integrals.1), custom_call_target="tpu_custom_call" | custom-call | flops 268435456 | bytes 3145728 | tf_op jit(solution)/shard_map/early_half/pallas_call | solution.py:259
  5.4 0.1 collective-permute-start
  5.4 1.2 %collective-permute-done.1.refs_0_ = bf16[64,4,256]{2,1,0:T(4,128)(2,1)S(1)} collective-permute-done((bf16[64,4,256]{2,1,0:T(4,128)(2,1)}, bf16[64,4,256]{2,1,0:T(4,128)(2,1)S(1)}, u32[]{:S(2)}, u32[]{:S(2)}) %collective-permute-start.1) | collective-permute-done | bytes 131104 | tf_op jit(solution)/shard_map/ppermute | solution.py:253
  6.7 0.8 %late_half.1 = (s16[528,128]{1,0:T(8,128)(2,1)S(1)}, f32[4,64,256]{2,1,0:T(8,128)S(1)}) custom-call(bf16[64,4,256]{2,1,0:T(4,128)(2,1)S(1)} %collective-permute-done.1.refs_0_, bf16[24,256,256]{2,1,0:T(8,128)(2,1)S(1)} %get-tuple-element.21.refs_1_, s32[24]{0:T(128)S(4)} %get-tuple-element.22.refs_2_), custom_call_target="tpu_custom_call" | custom-call | flops 268435456 | tf_op jit(solution)/shard_map/late_half/pallas_call | solution.py:286
  7.4 0.1 collective-permute-start.2
  7.5 0.0 collective-permute-done.got
  7.5 0.1 early_sums.1
  7.6 1.8 %collective-permute-start.3 = (s16[288,128]{1,0:T(8,128)(2,1)S(1)}, s16[288,128]{1,0:T(8,128)(2,1)S(1)}, u32[]{:S(2)}, u32[]{:S(2)}) collective-permute-start(s16[288,128]{1,0:T(8,128)(2,1)S(1)} %get-tuple-element.26), channel_id=1, source_target_pairs={{0,4},{2,10},{4,0},{6,14},{8,12},{10,2},{12,8},{14,6},{16,20},{18,... | collective-permute-start | bytes 221192 | tf_op jit(solution)/shard_map/ppermute | solution.py:301
  9.4 0.0 collective-permute-done.2.late_got
  9.4 0.1 near_sums.1
  9.5 1.3 %collective-permute-start.4 = (s16[272,128]{1,0:T(8,128)(2,1)S(1)}, s16[272,128]{1,0:T(8,128)(2,1)S(1)}, u32[]{:S(2)}, u32[]{:S(2)}) collective-permute-start(s16[272,128]{1,0:T(8,128)(2,1)S(1)} %get-tuple-element.27), channel_id=1, source_target_pairs={{0,4},{2,10},{4,0},{6,14},{8,12},{10,2},{12,8},{14,6},{16,20},{18,... | collective-permute-start | bytes 208904 | tf_op jit(solution)/shard_map/ppermute | solution.py:301
  10.8 1.9 %collective-permute-start.5 = (s16[272,128]{1,0:T(8,128)(2,1)S(1)}, s16[272,128]{1,0:T(8,128)(2,1)S(1)}, u32[]{:S(2)}, u32[]{:S(2)}) collective-permute-start(s16[272,128]{1,0:T(8,128)(2,1)S(1)} %get-tuple-element.28), channel_id=1, source_target_pairs={{0,12},{2,14},{4,8},{6,10},{8,4},{10,6},{12,0},{14,2},{16,28},{18,... | collective-permute-start | bytes 208904 | tf_op jit(solution)/shard_map/ppermute | solution.py:231
  12.6 0.0 collective-permute-done.3.ahead
  12.6 1.3 %collective-permute-done.4.side = s16[272,128]{1,0:T(8,128)(2,1)S(1)} collective-permute-done((s16[272,128]{1,0:T(8,128)(2,1)S(1)}, s16[272,128]{1,0:T(8,128)(2,1)S(1)}, u32[]{:S(2)}, u32[]{:S(2)}) %collective-permute-start.4) | collective-permute-done | bytes 69664 | tf_op jit(solution)/shard_map/ppermute | solution.py:301
  13.9 0.1 collective-permute-start.6
  14.0 2.0 %collective-permute-done.5.diagonal = s16[272,128]{1,0:T(8,128)(2,1)S(1)} collective-permute-done((s16[272,128]{1,0:T(8,128)(2,1)S(1)}, s16[272,128]{1,0:T(8,128)(2,1)S(1)}, u32[]{:S(2)}, u32[]{:S(2)}) %collective-permute-start.5) | collective-permute-done | bytes 69664 | tf_op jit(solution)/shard_map/ppermute | solution.py:231
  16.0 0.0 collective-permute-done.6.passed
  16.0 0.1 far_sums.1
  16.1 1.7 %collective-permute-start.7 = (s16[144,128]{1,0:T(8,128)(2,1)S(1)}, s16[144,128]{1,0:T(8,128)(2,1)S(1)}, u32[]{:S(2)}, u32[]{:S(2)}) collective-permute-start(s16[144,128]{1,0:T(8,128)(2,1)S(1)} %get-tuple-element.30), channel_id=1, source_target_pairs={{0,18},{2,16},{4,22},{6,20},{8,26},{10,24},{12,30},{14,28},{16,2},... | collective-permute-start | bytes 110600 | tf_op jit(solution)/shard_map/ppermute | solution.py:231
  17.8 2.8 %collective-permute-done.7.refs_0_ = s16[144,128]{1,0:T(8,128)(2,1)S(1)} collective-permute-done((s16[144,128]{1,0:T(8,128)(2,1)S(1)}, s16[144,128]{1,0:T(8,128)(2,1)S(1)}, u32[]{:S(2)}, u32[]{:S(2)}) %collective-permute-start.7) | collective-permute-done | bytes 36896 | tf_op jit(solution)/shard_map/ppermute | solution.py:231
  20.6 0.7 %own_block.1 = f32[8,8,256]{2,1,0:T(8,128)} custom-call(f32[1,64,256]{2,1,0:T(8,128)S(1)} %get-tuple-element.29.keep, s16[144,128]{1,0:T(8,128)(2,1)S(1)} %collective-permute-done.7.refs_0_), custom_call_target="tpu_custom_call" | custom-call | tf_op jit(solution)/shard_map/own_block/pallas_call | solution.py:337
  (1 shorter events, 0.0 us)
Async XLA Ops:
  0.0 6.7 %collective-permute-start.1 = (bf16[64,4,256]{2,1,0:T(4,128)(2,1)}, bf16[64,4,256]{2,1,0:T(4,128)(2,1)S(1)}, u32[]{:S(2)}, u32[]{:S(2)}) collective-permute-start(bf16[64,4,256]{2,1,0:T(4,128)(2,1)} %own_hbm.1), channel_id=1, source_target_pairs={{0,1},{1,0},{2,3},{3,2},{4,5},{5,4},{6,7},{7,6},{8,9},{9,8},{10,11... | collective-permute-start | bytes 393224 | tf_op jit(solution)/shard_map/ppermute | solution.py:253
  5.4 2.2 %collective-permute-start = (f32[4,64,256]{2,1,0:T(8,128)S(1)}, f32[4,64,256]{2,1,0:T(8,128)S(1)}, u32[]{:S(2)}, u32[]{:S(2)}) collective-permute-start(f32[4,64,256]{2,1,0:T(8,128)S(1)} %get-tuple-element.19), channel_id=1, source_target_pairs={{0,2},{2,0},{4,6},{6,4},{8,10},{10,8},{12,14},{14,12},{16,18},{18,... | collective-permute-start | bytes 786440 | tf_op jit(solution)/shard_map/ppermute | solution.py:231
  7.4 1.9 %collective-permute-start.2 = (s16[528,128]{1,0:T(8,128)(2,1)S(1)}, s16[528,128]{1,0:T(8,128)(2,1)S(1)}, u32[]{:S(2)}, u32[]{:S(2)}) collective-permute-start(s16[528,128]{1,0:T(8,128)(2,1)S(1)} %get-tuple-element.24), channel_id=1, source_target_pairs={{0,2},{2,0},{4,6},{6,4},{8,10},{10,8},{12,14},{14,12},{16,18},{18,... | collective-permute-start | bytes 405512 | tf_op jit(solution)/shard_map/ppermute | solution.py:231
  7.6 5.0 %collective-permute-start.3 = (s16[288,128]{1,0:T(8,128)(2,1)S(1)}, s16[288,128]{1,0:T(8,128)(2,1)S(1)}, u32[]{:S(2)}, u32[]{:S(2)}) collective-permute-start(s16[288,128]{1,0:T(8,128)(2,1)S(1)} %get-tuple-element.26), channel_id=1, source_target_pairs={{0,4},{2,10},{4,0},{6,14},{8,12},{10,2},{12,8},{14,6},{16,20},{18,... | collective-permute-start | bytes 221192 | tf_op jit(solution)/shard_map/ppermute | solution.py:301
  9.5 4.4 %collective-permute-start.4 = (s16[272,128]{1,0:T(8,128)(2,1)S(1)}, s16[272,128]{1,0:T(8,128)(2,1)S(1)}, u32[]{:S(2)}, u32[]{:S(2)}) collective-permute-start(s16[272,128]{1,0:T(8,128)(2,1)S(1)} %get-tuple-element.27), channel_id=1, source_target_pairs={{0,4},{2,10},{4,0},{6,14},{8,12},{10,2},{12,8},{14,6},{16,20},{18,... | collective-permute-start | bytes 208904 | tf_op jit(solution)/shard_map/ppermute | solution.py:301
  10.8 5.2 %collective-permute-start.5 = (s16[272,128]{1,0:T(8,128)(2,1)S(1)}, s16[272,128]{1,0:T(8,128)(2,1)S(1)}, u32[]{:S(2)}, u32[]{:S(2)}) collective-permute-start(s16[272,128]{1,0:T(8,128)(2,1)S(1)} %get-tuple-element.28), channel_id=1, source_target_pairs={{0,12},{2,14},{4,8},{6,10},{8,4},{10,6},{12,0},{14,2},{16,28},{18,... | collective-permute-start | bytes 208904 | tf_op jit(solution)/shard_map/ppermute | solution.py:231
  13.9 2.1 %collective-permute-start.6 = (s16[272,128]{1,0:T(8,128)(2,1)S(1)}, s16[272,128]{1,0:T(8,128)(2,1)S(1)}, u32[]{:S(2)}, u32[]{:S(2)}) collective-permute-start(s16[272,128]{1,0:T(8,128)(2,1)S(1)} %pass_on.1), channel_id=1, source_target_pairs={{0,2},{2,0},{4,6},{6,4},{8,10},{10,8},{12,14},{14,12},{16,18},{18,... | collective-permute-start | bytes 208904 | tf_op jit(solution)/shard_map/ppermute | solution.py:231
  16.1 4.5 %collective-permute-start.7 = (s16[144,128]{1,0:T(8,128)(2,1)S(1)}, s16[144,128]{1,0:T(8,128)(2,1)S(1)}, u32[]{:S(2)}, u32[]{:S(2)}) collective-permute-start(s16[144,128]{1,0:T(8,128)(2,1)S(1)} %get-tuple-element.30), channel_id=1, source_target_pairs={{0,18},{2,16},{4,22},{6,20},{8,26},{10,24},{12,30},{14,28},{16,2},... | collective-permute-start | bytes 110600 | tf_op jit(solution)/shard_map/ppermute | solution.py:231

commit v6 on v5

--- a/solution.py
+++ b/solution.py
@@ -36,8 +36,8 @@
         flip = 0
         for stage in pairs_of([1 << b for b in range(n_col.bit_length() - 1)]):
             flip = flip ^ jnp.where(offset & sum(stage) != 0, 1, 0)
-        kept = (ACROSS | ALONG, mine, mine ^ 1, 0)
-        sent = (ACROSS | ALONG | 1, other ^ 1, other, 1)
+        kept = (ACROSS | ALONG | 1, mine ^ 1, mine, 0)
+        sent = (ACROSS | ALONG, other, other ^ 1, 1)
         places = [(keep, 4 * h + at, j ^ flip) for at, j in enumerate(kept)]
         place(size, total, places + [(send, 4 * h + at, j ^ flip) for at, j in enumerate(sent)])
 
@@ -298,7 +298,7 @@
     )(*[vmem(o) for o in others], vmem(tiles), pltpu.with_memory_space_constraint(aim, pltpu.SMEM))
     late_got = swap(late_send, 1)
     def to_side(x):
-        return lax.ppermute(x, "row", [(i, i ^ (ALONG if i % 2 else ACROSS)) for i in range(n_row)])
+        return lax.ppermute(x, "row", [(i, i ^ (ALONG if i % 2 else ACROSS) ^ 1) for i in range(n_row)])
 
     ahead, early = call(early_sums_kernel, "early_sums", [coded(2, SPARE), kept(2)], keep, got)
     ahead = to_side(ahead)
@@ -311,7 +311,7 @@
         late_got,
     )
     side = to_side(side)
-    diagonal = swap(diagonal, ACROSS | ALONG)
+    diagonal = swap(diagonal, ACROSS | ALONG | 1)
     each = out_width // LANES
     passed = call(functools.partial(pass_kernel, each * block[0], each), "pass_on", coded(n_col), ahead, side)
     arrived = [ahead, side, diagonal, swap(passed, 1)]

time: 21.4 us -> 20.9 us (0.977)
  waiting for transfers between devices: 7.34 us -> 6.37 us
  starting transfers between devices: 9.73 us -> 10.2 us
    ppermute x5, waiting for transfers between devices: 4.83 us -> 3.69 us  [swap(): return lax.ppermute(x, 'row', [(i, i ^ mask) for i in range(n_row)])]
    ppermute x5, starting transfers between devices: 3.73 us -> 4.11 us  [swap(): return lax.ppermute(x, 'row', [(i, i ^ mask) for i in range(n_row)])]
where the time goes in v6:
time: 20.9 us; the launch traced here: 20.7 us
  starting transfers between devices  10.2 us (49%)
  waiting for transfers between devices  6.37 us (30%)
  Pallas kernels  4.1 us (20%)
    ppermute x5, starting transfers between devices, swap(): return lax.ppermute(x, 'row', [(i, i ^ mask) for i in range(n_row)])  4.11 us
    ppermute x5, waiting for transfers between devices, swap(): return lax.ppermute(x, 'row', [(i, i ^ mask) for i in range(n_row)])  3.69 us
    ppermute x2, starting transfers between devices, to_side(): lax.ppermute(x, 'row', [(i, i ^ (ALONG if i % 2 else ACROSS) ^ 1) for i i...  3.12 us
    ppermute x1, starting transfers between devices, body(): lax.ppermute(amplitudes, 'col', [(i, (i + step) % n_col) for i in range(n...  2.97 us
    pallas_call x1, Pallas kernels, body(): pl.pallas_call(functools.partial(early_kernel, size, n_col), out_shape=[p...  2.38 us
    ppermute x2, waiting for transfers between devices, to_side(): lax.ppermute(x, 'row', [(i, i ^ (ALONG if i % 2 else ACROSS) ^ 1) for i i...  1.44 us
    ppermute x1, waiting for transfers between devices, body(): lax.ppermute(amplitudes, 'col', [(i, (i + step) % n_col) for i in range(n...  1.24 us
    pallas_call x1, Pallas kernels, body(): pl.pallas_call(functools.partial(late_kernel, size, lates), out_shape=[co...  0.77 us
  transfers between devices with their start and end apart: 8, of which 4 were waited for; matrix products, arithmetic and copies ran while one was open for 0% of the time, Pallas kernels for 16%

profile of v6, /device:TPU:0, one launch (start us, length us, event | category | flops | bytes accessed | tf_op | source)
XLA Modules:
  0.0 20.7 jit_solution(9019814495271167329)
XLA Ops:
  0.0 3.0 %collective-permute-start.1 = (bf16[64,4,256]{2,1,0:T(4,128)(2,1)}, bf16[64,4,256]{2,1,0:T(4,128)(2,1)S(1)}, u32[]{:S(2)}, u32[]{:S(2)}) collective-permute-start(bf16[64,4,256]{2,1,0:T(4,128)(2,1)} %own_hbm.1), channel_id=1, source_target_pairs={{0,1},{1,0},{2,3},{3,2},{4,5},{5,4},{6,7},{7,6},{8,9},{9,8},{10,11... | collective-permute-start | bytes 393224 | tf_op jit(solution)/shard_map/ppermute | solution.py:253
  3.0 2.4 %early_half.1 = (bf16[24,256,256]{2,1,0:T(8,128)(2,1)S(1)}, s32[24]{0:T(128)S(4)}, f32[4,64,256]{2,1,0:T(8,128)S(1)}, f32[4,64,256]{2,1,0:T(8,128)S(1)}) custom-call(s32[4,6]{1,0:T(4,128)} %screen_hbm.1, s32[1,8]{1,0:T(1,128)} %owner_hbm.1, bf16[64,4,256]{2,1,0:T(4,128)(2,1)} %own_hbm.1, bf16[4,6,256,256]{3,2,1,0:T(8,128)(2,1)} %integrals.1), custom_call_target="tpu_custom_call" | custom-call | flops 268435456 | bytes 3145728 | tf_op jit(solution)/shard_map/early_half/pallas_call | solution.py:259
  5.4 0.1 collective-permute-start
  5.4 1.2 %collective-permute-done.1.refs_0_ = bf16[64,4,256]{2,1,0:T(4,128)(2,1)S(1)} collective-permute-done((bf16[64,4,256]{2,1,0:T(4,128)(2,1)}, bf16[64,4,256]{2,1,0:T(4,128)(2,1)S(1)}, u32[]{:S(2)}, u32[]{:S(2)}) %collective-permute-start.1) | collective-permute-done | bytes 131104 | tf_op jit(solution)/shard_map/ppermute | solution.py:253
  6.7 0.8 %late_half.1 = (s16[528,128]{1,0:T(8,128)(2,1)S(1)}, f32[4,64,256]{2,1,0:T(8,128)S(1)}) custom-call(bf16[64,4,256]{2,1,0:T(4,128)(2,1)S(1)} %collective-permute-done.1.refs_0_, bf16[24,256,256]{2,1,0:T(8,128)(2,1)S(1)} %get-tuple-element.21.refs_1_, s32[24]{0:T(128)S(4)} %get-tuple-element.22.refs_2_), custom_call_target="tpu_custom_call" | custom-call | flops 268435456 | tf_op jit(solution)/shard_map/late_half/pallas_call | solution.py:286
  7.4 0.1 collective-permute-start.2
  7.5 0.0 collective-permute-done.got
  7.5 0.1 early_sums.1
  7.6 1.9 %collective-permute-start.3 = (s16[288,128]{1,0:T(8,128)(2,1)S(1)}, s16[288,128]{1,0:T(8,128)(2,1)S(1)}, u32[]{:S(2)}, u32[]{:S(2)}) collective-permute-start(s16[288,128]{1,0:T(8,128)(2,1)S(1)} %get-tuple-element.26), channel_id=1, source_target_pairs={{0,6},{2,8},{4,2},{6,12},{8,14},{10,0},{12,10},{14,4},{16,22},{18,... | collective-permute-start | bytes 221192 | tf_op jit(solution)/shard_map/ppermute | solution.py:301
  9.5 0.0 collective-permute-done.2.late_got
  9.5 0.1 near_sums.1
  9.6 1.3 %collective-permute-start.4 = (s16[272,128]{1,0:T(8,128)(2,1)S(1)}, s16[272,128]{1,0:T(8,128)(2,1)S(1)}, u32[]{:S(2)}, u32[]{:S(2)}) collective-permute-start(s16[272,128]{1,0:T(8,128)(2,1)S(1)} %get-tuple-element.27), channel_id=1, source_target_pairs={{0,6},{2,8},{4,2},{6,12},{8,14},{10,0},{12,10},{14,4},{16,22},{18,... | collective-permute-start | bytes 208904 | tf_op jit(solution)/shard_map/ppermute | solution.py:301
  10.9 1.1 %collective-permute-start.5 = (s16[272,128]{1,0:T(8,128)(2,1)S(1)}, s16[272,128]{1,0:T(8,128)(2,1)S(1)}, u32[]{:S(2)}, u32[]{:S(2)}) collective-permute-start(s16[272,128]{1,0:T(8,128)(2,1)S(1)} %get-tuple-element.28), channel_id=1, source_target_pairs={{0,14},{2,12},{4,10},{6,8},{8,6},{10,4},{12,2},{14,0},{16,30},{18,... | collective-permute-start | bytes 208904 | tf_op jit(solution)/shard_map/ppermute | solution.py:231
  11.9 0.0 collective-permute-done.3.ahead
  11.9 1.4 %collective-permute-done.4.side = s16[272,128]{1,0:T(8,128)(2,1)S(1)} collective-permute-done((s16[272,128]{1,0:T(8,128)(2,1)S(1)}, s16[272,128]{1,0:T(8,128)(2,1)S(1)}, u32[]{:S(2)}, u32[]{:S(2)}) %collective-permute-start.4) | collective-permute-done | bytes 69664 | tf_op jit(solution)/shard_map/ppermute | solution.py:301
  13.4 0.2 collective-permute-start.6
  13.6 2.0 %collective-permute-done.5.diagonal = s16[272,128]{1,0:T(8,128)(2,1)S(1)} collective-permute-done((s16[272,128]{1,0:T(8,128)(2,1)S(1)}, s16[272,128]{1,0:T(8,128)(2,1)S(1)}, u32[]{:S(2)}, u32[]{:S(2)}) %collective-permute-start.5) | collective-permute-done | bytes 69664 | tf_op jit(solution)/shard_map/ppermute | solution.py:231
  15.6 0.0 collective-permute-done.6.passed
  15.6 0.1 far_sums.1
  15.7 2.7 %collective-permute-start.7 = (s16[144,128]{1,0:T(8,128)(2,1)S(1)}, s16[144,128]{1,0:T(8,128)(2,1)S(1)}, u32[]{:S(2)}, u32[]{:S(2)}) collective-permute-start(s16[144,128]{1,0:T(8,128)(2,1)S(1)} %get-tuple-element.30), channel_id=1, source_target_pairs={{0,18},{2,16},{4,22},{6,20},{8,26},{10,24},{12,30},{14,28},{16,2},... | collective-permute-start | bytes 110600 | tf_op jit(solution)/shard_map/ppermute | solution.py:231
  18.4 1.6 %collective-permute-done.7.refs_0_ = s16[144,128]{1,0:T(8,128)(2,1)S(1)} collective-permute-done((s16[144,128]{1,0:T(8,128)(2,1)S(1)}, s16[144,128]{1,0:T(8,128)(2,1)S(1)}, u32[]{:S(2)}, u32[]{:S(2)}) %collective-permute-start.7) | collective-permute-done | bytes 36896 | tf_op jit(solution)/shard_map/ppermute | solution.py:231
  20.1 0.7 %own_block.1 = f32[8,8,256]{2,1,0:T(8,128)} custom-call(f32[1,64,256]{2,1,0:T(8,128)S(1)} %get-tuple-element.29.keep, s16[144,128]{1,0:T(8,128)(2,1)S(1)} %collective-permute-done.7.refs_0_), custom_call_target="tpu_custom_call" | custom-call | tf_op jit(solution)/shard_map/own_block/pallas_call | solution.py:337
  (1 shorter events, 0.0 us)
Async XLA Ops:
  0.0 6.7 %collective-permute-start.1 = (bf16[64,4,256]{2,1,0:T(4,128)(2,1)}, bf16[64,4,256]{2,1,0:T(4,128)(2,1)S(1)}, u32[]{:S(2)}, u32[]{:S(2)}) collective-permute-start(bf16[64,4,256]{2,1,0:T(4,128)(2,1)} %own_hbm.1), channel_id=1, source_target_pairs={{0,1},{1,0},{2,3},{3,2},{4,5},{5,4},{6,7},{7,6},{8,9},{9,8},{10,11... | collective-permute-start | bytes 393224 | tf_op jit(solution)/shard_map/ppermute | solution.py:253
  5.4 2.2 %collective-permute-start = (f32[4,64,256]{2,1,0:T(8,128)S(1)}, f32[4,64,256]{2,1,0:T(8,128)S(1)}, u32[]{:S(2)}, u32[]{:S(2)}) collective-permute-start(f32[4,64,256]{2,1,0:T(8,128)S(1)} %get-tuple-element.19), channel_id=1, source_target_pairs={{0,2},{2,0},{4,6},{6,4},{8,10},{10,8},{12,14},{14,12},{16,18},{18,... | collective-permute-start | bytes 786440 | tf_op jit(solution)/shard_map/ppermute | solution.py:231
  7.4 2.0 %collective-permute-start.2 = (s16[528,128]{1,0:T(8,128)(2,1)S(1)}, s16[528,128]{1,0:T(8,128)(2,1)S(1)}, u32[]{:S(2)}, u32[]{:S(2)}) collective-permute-start(s16[528,128]{1,0:T(8,128)(2,1)S(1)} %get-tuple-element.24), channel_id=1, source_target_pairs={{0,2},{2,0},{4,6},{6,4},{8,10},{10,8},{12,14},{14,12},{16,18},{18,... | collective-permute-start | bytes 405512 | tf_op jit(solution)/shard_map/ppermute | solution.py:231
  7.6 4.3 %collective-permute-start.3 = (s16[288,128]{1,0:T(8,128)(2,1)S(1)}, s16[288,128]{1,0:T(8,128)(2,1)S(1)}, u32[]{:S(2)}, u32[]{:S(2)}) collective-permute-start(s16[288,128]{1,0:T(8,128)(2,1)S(1)} %get-tuple-element.26), channel_id=1, source_target_pairs={{0,6},{2,8},{4,2},{6,12},{8,14},{10,0},{12,10},{14,4},{16,22},{18,... | collective-permute-start | bytes 221192 | tf_op jit(solution)/shard_map/ppermute | solution.py:301
  9.6 3.8 %collective-permute-start.4 = (s16[272,128]{1,0:T(8,128)(2,1)S(1)}, s16[272,128]{1,0:T(8,128)(2,1)S(1)}, u32[]{:S(2)}, u32[]{:S(2)}) collective-permute-start(s16[272,128]{1,0:T(8,128)(2,1)S(1)} %get-tuple-element.27), channel_id=1, source_target_pairs={{0,6},{2,8},{4,2},{6,12},{8,14},{10,0},{12,10},{14,4},{16,22},{18,... | collective-permute-start | bytes 208904 | tf_op jit(solution)/shard_map/ppermute | solution.py:301
  10.9 4.8 %collective-permute-start.5 = (s16[272,128]{1,0:T(8,128)(2,1)S(1)}, s16[272,128]{1,0:T(8,128)(2,1)S(1)}, u32[]{:S(2)}, u32[]{:S(2)}) collective-permute-start(s16[272,128]{1,0:T(8,128)(2,1)S(1)} %get-tuple-element.28), channel_id=1, source_target_pairs={{0,14},{2,12},{4,10},{6,8},{8,6},{10,4},{12,2},{14,0},{16,30},{18,... | collective-permute-start | bytes 208904 | tf_op jit(solution)/shard_map/ppermute | solution.py:231
  13.4 2.2 %collective-permute-start.6 = (s16[272,128]{1,0:T(8,128)(2,1)S(1)}, s16[272,128]{1,0:T(8,128)(2,1)S(1)}, u32[]{:S(2)}, u32[]{:S(2)}) collective-permute-start(s16[272,128]{1,0:T(8,128)(2,1)S(1)} %pass_on.1), channel_id=1, source_target_pairs={{0,2},{2,0},{4,6},{6,4},{8,10},{10,8},{12,14},{14,12},{16,18},{18,... | collective-permute-start | bytes 208904 | tf_op jit(solution)/shard_map/ppermute | solution.py:231
  15.7 4.3 %collective-permute-start.7 = (s16[144,128]{1,0:T(8,128)(2,1)S(1)}, s16[144,128]{1,0:T(8,128)(2,1)S(1)}, u32[]{:S(2)}, u32[]{:S(2)}) collective-permute-start(s16[144,128]{1,0:T(8,128)(2,1)S(1)} %get-tuple-element.30), channel_id=1, source_target_pairs={{0,18},{2,16},{4,22},{6,20},{8,26},{10,24},{12,30},{14,28},{16,2},... | collective-permute-start | bytes 110600 | tf_op jit(solution)/shard_map/ppermute | solution.py:231

commit v7 on v6

--- a/solution.py
+++ b/solution.py
@@ -120,7 +120,7 @@
 
 
 def late_kernel(size, count, *refs):
-    others, (tiles, aim, out, keep, send, totals) = refs[:count], refs[count:]
+    others, (tiles, aim, send, keep, totals) = refs[:count], refs[count:]
     slots = aim.shape[0] // others[0].shape[1]
     totals[...] = jnp.zeros(totals.shape, totals.dtype)
     for h, raw in enumerate(others):
@@ -128,7 +128,6 @@
         for i in range(aim.shape[0]):
             add_tile(lhs[i // slots], tiles, aim, i, totals.at[h])
     lay_out(size, count + 1, 1, [totals.at[h] for h in range(count)], keep, send)
-    encode([send[i] for i in range(4 * count)], out)
 
 
 def early_sums_kernel(keep, got, ahead, out):
@@ -142,7 +141,7 @@
     rows, width = early.shape[1:]
     sums = []
     for at in range(4):
-        sums.append([late_keep[i] + decode(late_got, i, rows, width) for i in range(at, (n_col - 1) * 4, 4)])
+        sums.append([late_keep[i] + late_got[i] for i in range(at, (n_col - 1) * 4, 4)])
     encode(sums[1] + sums[2], side)
     encode([early[0]] + sums[0], diagonal)
     out[0] = early[1]
@@ -285,11 +284,10 @@
     lates = n_col - 1
     late_send, late_keep = pl.pallas_call(
         functools.partial(late_kernel, size, lates),
-        out_shape=[coded(lates * 4), kept(lates * 4)],
+        out_shape=[kept(lates * 4), kept(lates * 4)],
         in_specs=[spec] * n_col + [smem],
         out_specs=[spec, spec],
         scratch_shapes=[
-            pltpu.VMEM((lates * 4,) + block, jnp.float32),
             pltpu.VMEM((lates, targets + 1, half, out_width), jnp.float32),
         ],
         cost_estimate=half_cost,

time: 20.9 us -> 20.8 us (level)
  no operation moved by 1% of the time
where the time goes in v7:
time: 20.8 us; the launch traced here: 20.7 us
  starting transfers between devices  10.4 us (50%)
  waiting for transfers between devices  6.2 us (30%)
  Pallas kernels  4.04 us (19%)
    ppermute x5, starting transfers between devices, swap(): return lax.ppermute(x, 'row', [(i, i ^ mask) for i in range(n_row)])  4.29 us
    ppermute x5, waiting for transfers between devices, swap(): return lax.ppermute(x, 'row', [(i, i ^ mask) for i in range(n_row)])  3.69 us
    ppermute x2, starting transfers between devices, to_side(): lax.ppermute(x, 'row', [(i, i ^ (ALONG if i % 2 else ACROSS) ^ 1) for i i...  3.11 us
    ppermute x1, starting transfers between devices, body(): lax.ppermute(amplitudes, 'col', [(i, (i + step) % n_col) for i in range(n...  2.97 us
    pallas_call x1, Pallas kernels, body(): pl.pallas_call(functools.partial(early_kernel, size, n_col), out_shape=[p...  2.37 us
    ppermute x2, waiting for transfers between devices, to_side(): lax.ppermute(x, 'row', [(i, i ^ (ALONG if i % 2 else ACROSS) ^ 1) for i i...  1.26 us
    ppermute x1, waiting for transfers between devices, body(): lax.ppermute(amplitudes, 'col', [(i, (i + step) % n_col) for i in range(n...  1.24 us
    pallas_call x1, Pallas kernels, body(): pl.pallas_call(functools.partial(late_kernel, size, lates), out_shape=[ke...  0.72 us
  transfers between devices with their start and end apart: 8, of which 4 were waited for; matrix products, arithmetic and copies ran while one was open for 0% of the time, Pallas kernels for 16%

profile of v7, /device:TPU:0, one launch (start us, length us, event | category | flops | bytes accessed | tf_op | source)
XLA Modules:
  0.0 20.7 jit_solution(4617609904825942704)
XLA Ops:
  0.0 3.0 %collective-permute-start.1 = (bf16[64,4,256]{2,1,0:T(4,128)(2,1)}, bf16[64,4,256]{2,1,0:T(4,128)(2,1)S(1)}, u32[]{:S(2)}, u32[]{:S(2)}) collective-permute-start(bf16[64,4,256]{2,1,0:T(4,128)(2,1)} %own_hbm.1), channel_id=1, source_target_pairs={{0,1},{1,0},{2,3},{3,2},{4,5},{5,4},{6,7},{7,6},{8,9},{9,8},{10,11... | collective-permute-start | bytes 393224 | tf_op jit(solution)/shard_map/ppermute | solution.py:252
  3.0 2.4 %early_half.1 = (bf16[24,256,256]{2,1,0:T(8,128)(2,1)S(1)}, s32[24]{0:T(128)S(4)}, f32[4,64,256]{2,1,0:T(8,128)S(1)}, f32[4,64,256]{2,1,0:T(8,128)S(1)}) custom-call(s32[4,6]{1,0:T(4,128)} %screen_hbm.1, s32[1,8]{1,0:T(1,128)} %owner_hbm.1, bf16[64,4,256]{2,1,0:T(4,128)(2,1)} %own_hbm.1, bf16[4,6,256,256]{3,2,1,0:T(8,128)(2,1)} %integrals.1), custom_call_target="tpu_custom_call" | custom-call | flops 268435456 | bytes 3145728 | tf_op jit(solution)/shard_map/early_half/pallas_call | solution.py:258
  5.4 0.1 collective-permute-start
  5.4 1.2 %collective-permute-done.1.refs_0_ = bf16[64,4,256]{2,1,0:T(4,128)(2,1)S(1)} collective-permute-done((bf16[64,4,256]{2,1,0:T(4,128)(2,1)}, bf16[64,4,256]{2,1,0:T(4,128)(2,1)S(1)}, u32[]{:S(2)}, u32[]{:S(2)}) %collective-permute-start.1) | collective-permute-done | bytes 131104 | tf_op jit(solution)/shard_map/ppermute | solution.py:252
  6.7 0.7 %late_half.1 = (f32[4,64,256]{2,1,0:T(8,128)S(1)}, f32[4,64,256]{2,1,0:T(8,128)S(1)}) custom-call(bf16[64,4,256]{2,1,0:T(4,128)(2,1)S(1)} %collective-permute-done.1.refs_0_, bf16[24,256,256]{2,1,0:T(8,128)(2,1)S(1)} %get-tuple-element.21.refs_1_, s32[24]{0:T(128)S(4)} %get-tuple-element.22.refs_2_), custom_call_target="tpu_custom_call" | custom-call | flops 268435456 | tf_op jit(solution)/shard_map/late_half/pallas_call | solution.py:285
  7.4 0.1 collective-permute-start.2
  7.5 0.0 collective-permute-done.got
  7.5 0.1 early_sums.1
  7.6 1.9 %collective-permute-start.3 = (s16[288,128]{1,0:T(8,128)(2,1)S(1)}, s16[288,128]{1,0:T(8,128)(2,1)S(1)}, u32[]{:S(2)}, u32[]{:S(2)}) collective-permute-start(s16[288,128]{1,0:T(8,128)(2,1)S(1)} %get-tuple-element.26), channel_id=1, source_target_pairs={{0,6},{2,8},{4,2},{6,12},{8,14},{10,0},{12,10},{14,4},{16,22},{18,... | collective-permute-start | bytes 221192 | tf_op jit(solution)/shard_map/ppermute | solution.py:299
  9.4 0.0 collective-permute-done.2.late_got
  9.4 0.1 near_sums.1
  9.5 1.3 %collective-permute-start.4 = (s16[272,128]{1,0:T(8,128)(2,1)S(1)}, s16[272,128]{1,0:T(8,128)(2,1)S(1)}, u32[]{:S(2)}, u32[]{:S(2)}) collective-permute-start(s16[272,128]{1,0:T(8,128)(2,1)S(1)} %get-tuple-element.27), channel_id=1, source_target_pairs={{0,6},{2,8},{4,2},{6,12},{8,14},{10,0},{12,10},{14,4},{16,22},{18,... | collective-permute-start | bytes 208904 | tf_op jit(solution)/shard_map/ppermute | solution.py:299
  10.8 1.3 %collective-permute-start.5 = (s16[272,128]{1,0:T(8,128)(2,1)S(1)}, s16[272,128]{1,0:T(8,128)(2,1)S(1)}, u32[]{:S(2)}, u32[]{:S(2)}) collective-permute-start(s16[272,128]{1,0:T(8,128)(2,1)S(1)} %get-tuple-element.28), channel_id=1, source_target_pairs={{0,14},{2,12},{4,10},{6,8},{8,6},{10,4},{12,2},{14,0},{16,30},{18,... | collective-permute-start | bytes 208904 | tf_op jit(solution)/shard_map/ppermute | solution.py:230
  12.1 0.0 collective-permute-done.3.ahead
  12.1 1.3 %collective-permute-done.4.side = s16[272,128]{1,0:T(8,128)(2,1)S(1)} collective-permute-done((s16[272,128]{1,0:T(8,128)(2,1)S(1)}, s16[272,128]{1,0:T(8,128)(2,1)S(1)}, u32[]{:S(2)}, u32[]{:S(2)}) %collective-permute-start.4) | collective-permute-done | bytes 69664 | tf_op jit(solution)/shard_map/ppermute | solution.py:299
  13.3 0.2 collective-permute-start.6
  13.5 2.0 %collective-permute-done.5.diagonal = s16[272,128]{1,0:T(8,128)(2,1)S(1)} collective-permute-done((s16[272,128]{1,0:T(8,128)(2,1)S(1)}, s16[272,128]{1,0:T(8,128)(2,1)S(1)}, u32[]{:S(2)}, u32[]{:S(2)}) %collective-permute-start.5) | collective-permute-done | bytes 69664 | tf_op jit(solution)/shard_map/ppermute | solution.py:230
  15.5 0.0 collective-permute-done.6.passed
  15.5 0.1 far_sums.1
  15.7 2.7 %collective-permute-start.7 = (s16[144,128]{1,0:T(8,128)(2,1)S(1)}, s16[144,128]{1,0:T(8,128)(2,1)S(1)}, u32[]{:S(2)}, u32[]{:S(2)}) collective-permute-start(s16[144,128]{1,0:T(8,128)(2,1)S(1)} %get-tuple-element.30), channel_id=1, source_target_pairs={{0,18},{2,16},{4,22},{6,20},{8,26},{10,24},{12,30},{14,28},{16,2},... | collective-permute-start | bytes 110600 | tf_op jit(solution)/shard_map/ppermute | solution.py:230
  18.4 1.7 %collective-permute-done.7.refs_0_ = s16[144,128]{1,0:T(8,128)(2,1)S(1)} collective-permute-done((s16[144,128]{1,0:T(8,128)(2,1)S(1)}, s16[144,128]{1,0:T(8,128)(2,1)S(1)}, u32[]{:S(2)}, u32[]{:S(2)}) %collective-permute-start.7) | collective-permute-done | bytes 36896 | tf_op jit(solution)/shard_map/ppermute | solution.py:230
  20.0 0.7 %own_block.1 = f32[8,8,256]{2,1,0:T(8,128)} custom-call(f32[1,64,256]{2,1,0:T(8,128)S(1)} %get-tuple-element.29.keep, s16[144,128]{1,0:T(8,128)(2,1)S(1)} %collective-permute-done.7.refs_0_), custom_call_target="tpu_custom_call" | custom-call | tf_op jit(solution)/shard_map/own_block/pallas_call | solution.py:335
  (1 shorter events, 0.0 us)
Async XLA Ops:
  0.0 6.7 %collective-permute-start.1 = (bf16[64,4,256]{2,1,0:T(4,128)(2,1)}, bf16[64,4,256]{2,1,0:T(4,128)(2,1)S(1)}, u32[]{:S(2)}, u32[]{:S(2)}) collective-permute-start(bf16[64,4,256]{2,1,0:T(4,128)(2,1)} %own_hbm.1), channel_id=1, source_target_pairs={{0,1},{1,0},{2,3},{3,2},{4,5},{5,4},{6,7},{7,6},{8,9},{9,8},{10,11... | collective-permute-start | bytes 393224 | tf_op jit(solution)/shard_map/ppermute | solution.py:252
  5.4 2.1 %collective-permute-start = (f32[4,64,256]{2,1,0:T(8,128)S(1)}, f32[4,64,256]{2,1,0:T(8,128)S(1)}, u32[]{:S(2)}, u32[]{:S(2)}) collective-permute-start(f32[4,64,256]{2,1,0:T(8,128)S(1)} %get-tuple-element.19), channel_id=1, source_target_pairs={{0,2},{2,0},{4,6},{6,4},{8,10},{10,8},{12,14},{14,12},{16,18},{18,... | collective-permute-start | bytes 786440 | tf_op jit(solution)/shard_map/ppermute | solution.py:230
  7.4 2.0 %collective-permute-start.2 = (f32[4,64,256]{2,1,0:T(8,128)S(1)}, f32[4,64,256]{2,1,0:T(8,128)S(1)}, u32[]{:S(2)}, u32[]{:S(2)}) collective-permute-start(f32[4,64,256]{2,1,0:T(8,128)S(1)} %get-tuple-element.24), channel_id=1, source_target_pairs={{0,2},{2,0},{4,6},{6,4},{8,10},{10,8},{12,14},{14,12},{16,18},{18,... | collective-permute-start | bytes 786440 | tf_op jit(solution)/shard_map/ppermute | solution.py:230
  7.6 4.5 %collective-permute-start.3 = (s16[288,128]{1,0:T(8,128)(2,1)S(1)}, s16[288,128]{1,0:T(8,128)(2,1)S(1)}, u32[]{:S(2)}, u32[]{:S(2)}) collective-permute-start(s16[288,128]{1,0:T(8,128)(2,1)S(1)} %get-tuple-element.26), channel_id=1, source_target_pairs={{0,6},{2,8},{4,2},{6,12},{8,14},{10,0},{12,10},{14,4},{16,22},{18,... | collective-permute-start | bytes 221192 | tf_op jit(solution)/shard_map/ppermute | solution.py:299
  9.5 3.8 %collective-permute-start.4 = (s16[272,128]{1,0:T(8,128)(2,1)S(1)}, s16[272,128]{1,0:T(8,128)(2,1)S(1)}, u32[]{:S(2)}, u32[]{:S(2)}) collective-permute-start(s16[272,128]{1,0:T(8,128)(2,1)S(1)} %get-tuple-element.27), channel_id=1, source_target_pairs={{0,6},{2,8},{4,2},{6,12},{8,14},{10,0},{12,10},{14,4},{16,22},{18,... | collective-permute-start | bytes 208904 | tf_op jit(solution)/shard_map/ppermute | solution.py:299
  10.8 4.8 %collective-permute-start.5 = (s16[272,128]{1,0:T(8,128)(2,1)S(1)}, s16[272,128]{1,0:T(8,128)(2,1)S(1)}, u32[]{:S(2)}, u32[]{:S(2)}) collective-permute-start(s16[272,128]{1,0:T(8,128)(2,1)S(1)} %get-tuple-element.28), channel_id=1, source_target_pairs={{0,14},{2,12},{4,10},{6,8},{8,6},{10,4},{12,2},{14,0},{16,30},{18,... | collective-permute-start | bytes 208904 | tf_op jit(solution)/shard_map/ppermute | solution.py:230
  13.3 2.2 %collective-permute-start.6 = (s16[272,128]{1,0:T(8,128)(2,1)S(1)}, s16[272,128]{1,0:T(8,128)(2,1)S(1)}, u32[]{:S(2)}, u32[]{:S(2)}) collective-permute-start(s16[272,128]{1,0:T(8,128)(2,1)S(1)} %pass_on.1), channel_id=1, source_target_pairs={{0,2},{2,0},{4,6},{6,4},{8,10},{10,8},{12,14},{14,12},{16,18},{18,... | collective-permute-start | bytes 208904 | tf_op jit(solution)/shard_map/ppermute | solution.py:230
  15.7 4.3 %collective-permute-start.7 = (s16[144,128]{1,0:T(8,128)(2,1)S(1)}, s16[144,128]{1,0:T(8,128)(2,1)S(1)}, u32[]{:S(2)}, u32[]{:S(2)}) collective-permute-start(s16[144,128]{1,0:T(8,128)(2,1)S(1)} %get-tuple-element.30), channel_id=1, source_target_pairs={{0,18},{2,16},{4,22},{6,20},{8,26},{10,24},{12,30},{14,28},{16,2},... | collective-permute-start | bytes 110600 | tf_op jit(solution)/shard_map/ppermute | solution.py:230

commit v8 on v7

--- a/solution.py
+++ b/solution.py
@@ -10,6 +10,7 @@
 SPARE = 16
 LEAST = -100
 LANES = 128
+PARTS = (3, 4, 5, 6)
 ACROSS, ALONG = 2, 4
 
 
@@ -81,9 +82,26 @@
     return jnp.concatenate(parts, axis=1)
 
 
+def list_live(screen, owner, live):
+    depth, slots = screen.shape
+    end = depth * slots
+    for at in range(end):
+        for n, value in enumerate((0, 0, owner.shape[1])):
+            live[n * (end + 1) + at] = value
+    count = 0
+    for k in range(depth):
+        for s in range(slots):
+            name = screen[k, s]
+            at = jnp.where(name >= 0, count, end)
+            for n, value in enumerate((k * slots + s, k, owner[0, jnp.maximum(name, 0)])):
+                live[n * (end + 1) + at] = value
+            count = count + jnp.where(name >= 0, 1, 0)
+    live[end] = count
+
+
 def early_kernel(
     size, n_col, screen_hbm, owner_hbm, own_hbm, integrals,
-    tiles, aim, send, keep, screen, owner, raw, total, sems, small,
+    tiles, live, send, keep, screen, owner, aim, raw, total, sems, small,
 ):
     depth, slots = screen.shape
     targets = owner.shape[1]
@@ -106,6 +124,7 @@
         for s in range(slots):
             name = screen[k, s]
             aim[k * slots + s] = jnp.where(name >= 0, owner[0, jnp.maximum(name, 0)], targets)
+    list_live(screen, owner, live)
     lhs = sides(raw[...])
     for k in range(depth):
         copies[k].wait()
@@ -120,13 +139,22 @@
 
 
 def late_kernel(size, count, *refs):
-    others, (tiles, aim, send, keep, totals) = refs[:count], refs[count:]
-    slots = aim.shape[0] // others[0].shape[1]
+    others, (tiles, live, send, keep, lhs, totals) = refs[:count], refs[count:]
+    slots = tiles.shape[0]
     totals[...] = jnp.zeros(totals.shape, totals.dtype)
     for h, raw in enumerate(others):
-        lhs = sides(raw[...])
-        for i in range(aim.shape[0]):
-            add_tile(lhs[i // slots], tiles, aim, i, totals.at[h])
+        for k, side in enumerate(sides(raw[...])):
+            lhs[k, h] = side
+    sizes = [0] + [slots * part // 6 for part in PARTS]
+    for low, high in zip(sizes, sizes[1:]):
+
+        @pl.when(jnp.logical_and(live[slots] > low, live[slots] <= high))
+        def _():
+            for h in range(count):
+                for i in range(high):
+                    tile, k, t = (live[n * (slots + 1) + i] for n in range(3))
+                    totals[h, t] += jnp.dot(lhs[k, h], tiles[tile], preferred_element_type=jnp.float32)
+
     lay_out(size, count + 1, 1, [totals.at[h] for h in range(count)], keep, send)
 
 
@@ -255,11 +283,11 @@
     half_cost = pl.CostEstimate(
         flops=2 * half * depth * targets * width * out_width, bytes_accessed=0, transcendentals=0
     )
-    tiles, aim, send, keep = pl.pallas_call(
+    tiles, live, send, keep = pl.pallas_call(
         functools.partial(early_kernel, size, n_col),
         out_shape=[
             pltpu.VMEM((depth * slots, width, out_width), jnp.bfloat16),
-            pltpu.SMEM((depth * slots,), jnp.int32),
+            pltpu.SMEM((3 * (depth * slots + 1),), jnp.int32),
             kept(4),
             kept(4),
         ],
@@ -268,6 +296,7 @@
         scratch_shapes=[
             pltpu.SMEM(screen.shape, jnp.int32),
             pltpu.SMEM(owner_map.shape, jnp.int32),
+            pltpu.SMEM((depth * slots,), jnp.int32),
             pltpu.VMEM(amplitudes.shape, jnp.bfloat16),
             pltpu.VMEM((targets + 1, half, out_width), jnp.float32),
             pltpu.SemaphoreType.DMA((depth,)),
@@ -288,12 +317,13 @@
         in_specs=[spec] * n_col + [smem],
         out_specs=[spec, spec],
         scratch_shapes=[
+            pltpu.VMEM((depth, lates, half, width), jnp.bfloat16),
             pltpu.VMEM((lates, targets + 1, half, out_width), jnp.float32),
         ],
         cost_estimate=half_cost,
         compiler_params=params,
         name="late_half",
-    )(*[vmem(o) for o in others], vmem(tiles), pltpu.with_memory_space_constraint(aim, pltpu.SMEM))
+    )(*[vmem(o) for o in others], vmem(tiles), pltpu.with_memory_space_constraint(live, pltpu.SMEM))
     late_got = swap(late_send, 1)
     def to_side(x):
         return lax.ppermute(x, "row", [(i, i ^ (ALONG if i % 2 else ACROSS) ^ 1) for i in range(n_row)])

time: 20.8 us -> 20.8 us (level)
  starting transfers between devices: 10.4 us -> 10.1 us
  Pallas kernels: 4.04 us -> 4.27 us
  transfers between devices with their start and end apart: 8 -> 8, of which waited for: 4 -> 4; matrix products, arithmetic and copies ran while one was open for 0% -> 0% of each run, Pallas kernels for 16% -> 17%
where the time goes in v8:
time: 20.8 us; the launch traced here: 20.7 us
  starting transfers between devices  10.1 us (49%)
  waiting for transfers between devices  6.23 us (30%)
  Pallas kernels  4.27 us (21%)
    ppermute x5, starting transfers between devices, swap(): return lax.ppermute(x, 'row', [(i, i ^ mask) for i in range(n_row)])  4.11 us
    ppermute x5, waiting for transfers between devices, swap(): return lax.ppermute(x, 'row', [(i, i ^ mask) for i in range(n_row)])  3.87 us
    ppermute x2, starting transfers between devices, to_side(): lax.ppermute(x, 'row', [(i, i ^ (ALONG if i % 2 else ACROSS) ^ 1) for i i...  3.03 us
    ppermute x1, starting transfers between devices, body(): lax.ppermute(amplitudes, 'col', [(i, (i + step) % n_col) for i in range(n...  2.97 us
    pallas_call x1, Pallas kernels, body(): pl.pallas_call(functools.partial(early_kernel, size, n_col), out_shape=[p...  2.53 us
    ppermute x2, waiting for transfers between devices, to_side(): lax.ppermute(x, 'row', [(i, i ^ (ALONG if i % 2 else ACROSS) ^ 1) for i i...  1.26 us
    ppermute x1, waiting for transfers between devices, body(): lax.ppermute(amplitudes, 'col', [(i, (i + step) % n_col) for i in range(n...  1.09 us
    pallas_call x1, Pallas kernels, body(): pl.pallas_call(functools.partial(late_kernel, size, lates), out_shape=[ke...  0.8 us
  transfers between devices with their start and end apart: 8, of which 4 were waited for; matrix products, arithmetic and copies ran while one was open for 0% of the time, Pallas kernels for 17%

profile of v8, /device:TPU:0, one launch (start us, length us, event | category | flops | bytes accessed | tf_op | source)
XLA Modules:
  0.0 20.7 jit_solution(7743838169457357712)
XLA Ops:
  0.0 3.0 %collective-permute-start.1 = (bf16[64,4,256]{2,1,0:T(4,128)(2,1)}, bf16[64,4,256]{2,1,0:T(4,128)(2,1)S(1)}, u32[]{:S(2)}, u32[]{:S(2)}) collective-permute-start(bf16[64,4,256]{2,1,0:T(4,128)(2,1)} %own_hbm.1), channel_id=1, source_target_pairs={{0,1},{1,0},{2,3},{3,2},{4,5},{5,4},{6,7},{7,6},{8,9},{9,8},{10,11... | collective-permute-start | bytes 393224 | tf_op jit(solution)/shard_map/ppermute | solution.py:280
  3.0 2.5 %early_half.1 = (bf16[24,256,256]{2,1,0:T(8,128)(2,1)S(1)}, s32[75]{0:T(128)S(4)}, f32[4,64,256]{2,1,0:T(8,128)S(1)}, f32[4,64,256]{2,1,0:T(8,128)S(1)}) custom-call(s32[4,6]{1,0:T(4,128)} %screen_hbm.1, s32[1,8]{1,0:T(1,128)} %owner_hbm.1, bf16[64,4,256]{2,1,0:T(4,128)(2,1)} %own_hbm.1, bf16[4,6,256,256]{3,2,1,0:T(8,128)(2,1)} %integrals.1), custom_call_target="tpu_custom_call" | custom-call | flops 268435456 | bytes 3145728 | tf_op jit(solution)/shard_map/early_half/pallas_call | solution.py:286
  5.5 0.1 collective-permute-start
  5.6 1.1 %collective-permute-done.1.refs_0_ = bf16[64,4,256]{2,1,0:T(4,128)(2,1)S(1)} collective-permute-done((bf16[64,4,256]{2,1,0:T(4,128)(2,1)}, bf16[64,4,256]{2,1,0:T(4,128)(2,1)S(1)}, u32[]{:S(2)}, u32[]{:S(2)}) %collective-permute-start.1) | collective-permute-done | bytes 131104 | tf_op jit(solution)/shard_map/ppermute | solution.py:280
  6.7 0.8 %late_half.1 = (f32[4,64,256]{2,1,0:T(8,128)S(1)}, f32[4,64,256]{2,1,0:T(8,128)S(1)}) custom-call(bf16[64,4,256]{2,1,0:T(4,128)(2,1)S(1)} %collective-permute-done.1.refs_0_, bf16[24,256,256]{2,1,0:T(8,128)(2,1)S(1)} %get-tuple-element.21.refs_1_, s32[75]{0:T(128)S(4)} %get-tuple-element.22.refs_2_), custom_call_target="tpu_custom_call" | custom-call | flops 268435456 | tf_op jit(solution)/shard_map/late_half/pallas_call | solution.py:314
  7.5 0.1 collective-permute-start.2
  7.6 0.0 collective-permute-done.got
  7.6 0.1 early_sums.1
  7.6 1.7 %collective-permute-start.3 = (s16[288,128]{1,0:T(8,128)(2,1)S(1)}, s16[288,128]{1,0:T(8,128)(2,1)S(1)}, u32[]{:S(2)}, u32[]{:S(2)}) collective-permute-start(s16[288,128]{1,0:T(8,128)(2,1)S(1)} %get-tuple-element.26), channel_id=1, source_target_pairs={{0,6},{2,8},{4,2},{6,12},{8,14},{10,0},{12,10},{14,4},{16,22},{18,... | collective-permute-start | bytes 221192 | tf_op jit(solution)/shard_map/ppermute | solution.py:329
  9.3 0.0 collective-permute-done.2.late_got
  9.3 0.1 near_sums.1
  9.4 1.3 %collective-permute-start.4 = (s16[272,128]{1,0:T(8,128)(2,1)S(1)}, s16[272,128]{1,0:T(8,128)(2,1)S(1)}, u32[]{:S(2)}, u32[]{:S(2)}) collective-permute-start(s16[272,128]{1,0:T(8,128)(2,1)S(1)} %get-tuple-element.27), channel_id=1, source_target_pairs={{0,6},{2,8},{4,2},{6,12},{8,14},{10,0},{12,10},{14,4},{16,22},{18,... | collective-permute-start | bytes 208904 | tf_op jit(solution)/shard_map/ppermute | solution.py:329
  10.8 1.2 %collective-permute-start.5 = (s16[272,128]{1,0:T(8,128)(2,1)S(1)}, s16[272,128]{1,0:T(8,128)(2,1)S(1)}, u32[]{:S(2)}, u32[]{:S(2)}) collective-permute-start(s16[272,128]{1,0:T(8,128)(2,1)S(1)} %get-tuple-element.28), channel_id=1, source_target_pairs={{0,14},{2,12},{4,10},{6,8},{8,6},{10,4},{12,2},{14,0},{16,30},{18,... | collective-permute-start | bytes 208904 | tf_op jit(solution)/shard_map/ppermute | solution.py:258
  12.0 0.0 collective-permute-done.3.ahead
  12.0 1.3 %collective-permute-done.4.side = s16[272,128]{1,0:T(8,128)(2,1)S(1)} collective-permute-done((s16[272,128]{1,0:T(8,128)(2,1)S(1)}, s16[272,128]{1,0:T(8,128)(2,1)S(1)}, u32[]{:S(2)}, u32[]{:S(2)}) %collective-permute-start.4) | collective-permute-done | bytes 69664 | tf_op jit(solution)/shard_map/ppermute | solution.py:329
  13.2 0.2 collective-permute-start.6
  13.4 2.1 %collective-permute-done.5.diagonal = s16[272,128]{1,0:T(8,128)(2,1)S(1)} collective-permute-done((s16[272,128]{1,0:T(8,128)(2,1)S(1)}, s16[272,128]{1,0:T(8,128)(2,1)S(1)}, u32[]{:S(2)}, u32[]{:S(2)}) %collective-permute-start.5) | collective-permute-done | bytes 69664 | tf_op jit(solution)/shard_map/ppermute | solution.py:258
  15.5 0.0 collective-permute-done.6.passed
  15.5 0.1 far_sums.1
  15.6 2.6 %collective-permute-start.7 = (s16[144,128]{1,0:T(8,128)(2,1)S(1)}, s16[144,128]{1,0:T(8,128)(2,1)S(1)}, u32[]{:S(2)}, u32[]{:S(2)}) collective-permute-start(s16[144,128]{1,0:T(8,128)(2,1)S(1)} %get-tuple-element.30), channel_id=1, source_target_pairs={{0,18},{2,16},{4,22},{6,20},{8,26},{10,24},{12,30},{14,28},{16,2},... | collective-permute-start | bytes 110600 | tf_op jit(solution)/shard_map/ppermute | solution.py:258
  18.3 1.7 %collective-permute-done.7.refs_0_ = s16[144,128]{1,0:T(8,128)(2,1)S(1)} collective-permute-done((s16[144,128]{1,0:T(8,128)(2,1)S(1)}, s16[144,128]{1,0:T(8,128)(2,1)S(1)}, u32[]{:S(2)}, u32[]{:S(2)}) %collective-permute-start.7) | collective-permute-done | bytes 36896 | tf_op jit(solution)/shard_map/ppermute | solution.py:258
  20.0 0.7 %own_block.1 = f32[8,8,256]{2,1,0:T(8,128)} custom-call(f32[1,64,256]{2,1,0:T(8,128)S(1)} %get-tuple-element.29.keep, s16[144,128]{1,0:T(8,128)(2,1)S(1)} %collective-permute-done.7.refs_0_), custom_call_target="tpu_custom_call" | custom-call | tf_op jit(solution)/shard_map/own_block/pallas_call | solution.py:365
  (1 shorter events, 0.0 us)
Async XLA Ops:
  0.0 6.7 %collective-permute-start.1 = (bf16[64,4,256]{2,1,0:T(4,128)(2,1)}, bf16[64,4,256]{2,1,0:T(4,128)(2,1)S(1)}, u32[]{:S(2)}, u32[]{:S(2)}) collective-permute-start(bf16[64,4,256]{2,1,0:T(4,128)(2,1)} %own_hbm.1), channel_id=1, source_target_pairs={{0,1},{1,0},{2,3},{3,2},{4,5},{5,4},{6,7},{7,6},{8,9},{9,8},{10,11... | collective-permute-start | bytes 393224 | tf_op jit(solution)/shard_map/ppermute | solution.py:280
  5.5 2.1 %collective-permute-start = (f32[4,64,256]{2,1,0:T(8,128)S(1)}, f32[4,64,256]{2,1,0:T(8,128)S(1)}, u32[]{:S(2)}, u32[]{:S(2)}) collective-permute-start(f32[4,64,256]{2,1,0:T(8,128)S(1)} %get-tuple-element.19), channel_id=1, source_target_pairs={{0,2},{2,0},{4,6},{6,4},{8,10},{10,8},{12,14},{14,12},{16,18},{18,... | collective-permute-start | bytes 786440 | tf_op jit(solution)/shard_map/ppermute | solution.py:258
  7.5 1.8 %collective-permute-start.2 = (f32[4,64,256]{2,1,0:T(8,128)S(1)}, f32[4,64,256]{2,1,0:T(8,128)S(1)}, u32[]{:S(2)}, u32[]{:S(2)}) collective-permute-start(f32[4,64,256]{2,1,0:T(8,128)S(1)} %get-tuple-element.24), channel_id=1, source_target_pairs={{0,2},{2,0},{4,6},{6,4},{8,10},{10,8},{12,14},{14,12},{16,18},{18,... | collective-permute-start | bytes 786440 | tf_op jit(solution)/shard_map/ppermute | solution.py:258
  7.6 4.3 %collective-permute-start.3 = (s16[288,128]{1,0:T(8,128)(2,1)S(1)}, s16[288,128]{1,0:T(8,128)(2,1)S(1)}, u32[]{:S(2)}, u32[]{:S(2)}) collective-permute-start(s16[288,128]{1,0:T(8,128)(2,1)S(1)} %get-tuple-element.26), channel_id=1, source_target_pairs={{0,6},{2,8},{4,2},{6,12},{8,14},{10,0},{12,10},{14,4},{16,22},{18,... | collective-permute-start | bytes 221192 | tf_op jit(solution)/shard_map/ppermute | solution.py:329
  9.4 3.8 %collective-permute-start.4 = (s16[272,128]{1,0:T(8,128)(2,1)S(1)}, s16[272,128]{1,0:T(8,128)(2,1)S(1)}, u32[]{:S(2)}, u32[]{:S(2)}) collective-permute-start(s16[272,128]{1,0:T(8,128)(2,1)S(1)} %get-tuple-element.27), channel_id=1, source_target_pairs={{0,6},{2,8},{4,2},{6,12},{8,14},{10,0},{12,10},{14,4},{16,22},{18,... | collective-permute-start | bytes 208904 | tf_op jit(solution)/shard_map/ppermute | solution.py:329
  10.8 4.8 %collective-permute-start.5 = (s16[272,128]{1,0:T(8,128)(2,1)S(1)}, s16[272,128]{1,0:T(8,128)(2,1)S(1)}, u32[]{:S(2)}, u32[]{:S(2)}) collective-permute-start(s16[272,128]{1,0:T(8,128)(2,1)S(1)} %get-tuple-element.28), channel_id=1, source_target_pairs={{0,14},{2,12},{4,10},{6,8},{8,6},{10,4},{12,2},{14,0},{16,30},{18,... | collective-permute-start | bytes 208904 | tf_op jit(solution)/shard_map/ppermute | solution.py:258
  13.2 2.3 %collective-permute-start.6 = (s16[272,128]{1,0:T(8,128)(2,1)S(1)}, s16[272,128]{1,0:T(8,128)(2,1)S(1)}, u32[]{:S(2)}, u32[]{:S(2)}) collective-permute-start(s16[272,128]{1,0:T(8,128)(2,1)S(1)} %pass_on.1), channel_id=1, source_target_pairs={{0,2},{2,0},{4,6},{6,4},{8,10},{10,8},{12,14},{14,12},{16,18},{18,... | collective-permute-start | bytes 208904 | tf_op jit(solution)/shard_map/ppermute | solution.py:258
  15.6 4.3 %collective-permute-start.7 = (s16[144,128]{1,0:T(8,128)(2,1)S(1)}, s16[144,128]{1,0:T(8,128)(2,1)S(1)}, u32[]{:S(2)}, u32[]{:S(2)}) collective-permute-start(s16[144,128]{1,0:T(8,128)(2,1)S(1)} %get-tuple-element.30), channel_id=1, source_target_pairs={{0,18},{2,16},{4,22},{6,20},{8,26},{10,24},{12,30},{14,28},{16,2},... | collective-permute-start | bytes 110600 | tf_op jit(solution)/shard_map/ppermute | solution.py:258

commit v9 on v7

--- a/solution.py
+++ b/solution.py
@@ -137,16 +137,17 @@
     out[1] = sums[3]
 
 
-def near_kernel(n_col, early, late_keep, late_got, side, diagonal, out):
-    rows, width = early.shape[1:]
-    sums = []
-    for at in range(4):
-        sums.append([late_keep[i] + late_got[i] for i in range(at, (n_col - 1) * 4, 4)])
-    encode(sums[1] + sums[2], side)
-    encode([early[0]] + sums[0], diagonal)
+def side_kernel(late_keep, late_got, side):
+    count = late_keep.shape[0]
+    encode([late_keep[i] + late_got[i] for at in (1, 2) for i in range(at, count, 4)], side)
+
+
+def near_kernel(early, late_keep, late_got, diagonal, out):
+    count = late_keep.shape[0]
+    encode([early[0]] + [late_keep[i] + late_got[i] for i in range(0, count, 4)], diagonal)
     out[0] = early[1]
-    for h in range(n_col - 1):
-        out[1 + h] = sums[3][h]
+    for h, i in enumerate(range(3, count, 4)):
+        out[1 + h] = late_keep[i] + late_got[i]
 
 
 def emit(groups, values, outs):
@@ -300,14 +301,8 @@
 
     ahead, early = call(early_sums_kernel, "early_sums", [coded(2, SPARE), kept(2)], keep, got)
     ahead = to_side(ahead)
-    side, diagonal, keep = call(
-        functools.partial(near_kernel, n_col),
-        "near_sums",
-        [coded(2 * lates), coded(n_col), kept(n_col)],
-        early,
-        late_keep,
-        late_got,
-    )
+    side = call(side_kernel, "side_sums", coded(2 * lates), late_keep, late_got)
+    diagonal, keep = call(near_kernel, "near_sums", [coded(n_col), kept(n_col)], early, late_keep, late_got)
     side = to_side(side)
     diagonal = swap(diagonal, ACROSS | ALONG | 1)
     each = out_width // LANES

time: 20.8 us -> 20.9 us (level)
  no operation moved by 1% of the time
where the time goes in v9:
time: 20.9 us; the launch traced here: 20.8 us
  starting transfers between devices  10.4 us (50%)
  waiting for transfers between devices  6.19 us (30%)
  Pallas kernels  4.06 us (19%)
    ppermute x5, starting transfers between devices, swap(): return lax.ppermute(x, 'row', [(i, i ^ mask) for i in range(n_row)])  4.35 us
    ppermute x5, waiting for transfers between devices, swap(): return lax.ppermute(x, 'row', [(i, i ^ mask) for i in range(n_row)])  3.83 us
    ppermute x2, starting transfers between devices, to_side(): lax.ppermute(x, 'row', [(i, i ^ (ALONG if i % 2 else ACROSS) ^ 1) for i i...  3.11 us
    ppermute x1, starting transfers between devices, body(): lax.ppermute(amplitudes, 'col', [(i, (i + step) % n_col) for i in range(n...  2.97 us
    pallas_call x1, Pallas kernels, body(): pl.pallas_call(functools.partial(early_kernel, size, n_col), out_shape=[p...  2.38 us
    ppermute x1, waiting for transfers between devices, body(): lax.ppermute(amplitudes, 'col', [(i, (i + step) % n_col) for i in range(n...  1.24 us
    ppermute x2, waiting for transfers between devices, to_side(): lax.ppermute(x, 'row', [(i, i ^ (ALONG if i % 2 else ACROSS) ^ 1) for i i...  1.13 us
    pallas_call x1, Pallas kernels, body(): pl.pallas_call(functools.partial(late_kernel, size, lates), out_shape=[ke...  0.72 us
  transfers between devices with their start and end apart: 8, of which 4 were waited for; matrix products, arithmetic and copies ran while one was open for 0% of the time, Pallas kernels for 16%

profile of v9, /device:TPU:0, one launch (start us, length us, event | category | flops | bytes accessed | tf_op | source)
XLA Modules:
  0.0 20.8 jit_solution(17620153068973868541)
XLA Ops:
  0.0 3.0 %collective-permute-start.1 = (bf16[64,4,256]{2,1,0:T(4,128)(2,1)}, bf16[64,4,256]{2,1,0:T(4,128)(2,1)S(1)}, u32[]{:S(2)}, u32[]{:S(2)}) collective-permute-start(bf16[64,4,256]{2,1,0:T(4,128)(2,1)} %own_hbm.1), channel_id=1, source_target_pairs={{0,1},{1,0},{2,3},{3,2},{4,5},{5,4},{6,7},{7,6},{8,9},{9,8},{10,11... | collective-permute-start | bytes 393224 | tf_op jit(solution)/shard_map/ppermute | solution.py:253
  3.0 2.4 %early_half.1 = (bf16[24,256,256]{2,1,0:T(8,128)(2,1)S(1)}, s32[24]{0:T(128)S(4)}, f32[4,64,256]{2,1,0:T(8,128)S(1)}, f32[4,64,256]{2,1,0:T(8,128)S(1)}) custom-call(s32[4,6]{1,0:T(4,128)} %screen_hbm.1, s32[1,8]{1,0:T(1,128)} %owner_hbm.1, bf16[64,4,256]{2,1,0:T(4,128)(2,1)} %own_hbm.1, bf16[4,6,256,256]{3,2,1,0:T(8,128)(2,1)} %integrals.1), custom_call_target="tpu_custom_call" | custom-call | flops 268435456 | bytes 3145728 | tf_op jit(solution)/shard_map/early_half/pallas_call | solution.py:259
  5.4 0.1 collective-permute-start
  5.4 1.2 %collective-permute-done.1.refs_0_ = bf16[64,4,256]{2,1,0:T(4,128)(2,1)S(1)} collective-permute-done((bf16[64,4,256]{2,1,0:T(4,128)(2,1)}, bf16[64,4,256]{2,1,0:T(4,128)(2,1)S(1)}, u32[]{:S(2)}, u32[]{:S(2)}) %collective-permute-start.1) | collective-permute-done | bytes 131104 | tf_op jit(solution)/shard_map/ppermute | solution.py:253
  6.7 0.7 %late_half.1 = (f32[4,64,256]{2,1,0:T(8,128)S(1)}, f32[4,64,256]{2,1,0:T(8,128)S(1)}) custom-call(bf16[64,4,256]{2,1,0:T(4,128)(2,1)S(1)} %collective-permute-done.1.refs_0_, bf16[24,256,256]{2,1,0:T(8,128)(2,1)S(1)} %get-tuple-element.20.refs_1_, s32[24]{0:T(128)S(4)} %get-tuple-element.21.refs_2_), custom_call_target="tpu_custom_call" | custom-call | flops 268435456 | tf_op jit(solution)/shard_map/late_half/pallas_call | solution.py:286
  7.4 0.1 collective-permute-start.2
  7.5 0.0 collective-permute-done.got
  7.5 0.1 early_sums.1
  7.6 1.9 %collective-permute-start.3 = (s16[288,128]{1,0:T(8,128)(2,1)S(1)}, s16[288,128]{1,0:T(8,128)(2,1)S(1)}, u32[]{:S(2)}, u32[]{:S(2)}) collective-permute-start(s16[288,128]{1,0:T(8,128)(2,1)S(1)} %get-tuple-element.25), channel_id=1, source_target_pairs={{0,6},{2,8},{4,2},{6,12},{8,14},{10,0},{12,10},{14,4},{16,22},{18,... | collective-permute-start | bytes 221192 | tf_op jit(solution)/shard_map/ppermute | solution.py:300
  9.4 0.0 collective-permute-done.2.late_got
  9.4 0.1 side_sums.1
  9.5 1.3 %collective-permute-start.4 = (s16[272,128]{1,0:T(8,128)(2,1)S(1)}, s16[272,128]{1,0:T(8,128)(2,1)S(1)}, u32[]{:S(2)}, u32[]{:S(2)}) collective-permute-start(s16[272,128]{1,0:T(8,128)(2,1)S(1)} %side_sums.1), channel_id=1, source_target_pairs={{0,6},{2,8},{4,2},{6,12},{8,14},{10,0},{12,10},{14,4},{16,22},{18,... | collective-permute-start | bytes 208904 | tf_op jit(solution)/shard_map/ppermute | solution.py:300
  10.7 0.1 near_sums.1
  10.8 1.3 %collective-permute-start.5 = (s16[272,128]{1,0:T(8,128)(2,1)S(1)}, s16[272,128]{1,0:T(8,128)(2,1)S(1)}, u32[]{:S(2)}, u32[]{:S(2)}) collective-permute-start(s16[272,128]{1,0:T(8,128)(2,1)S(1)} %get-tuple-element.26), channel_id=1, source_target_pairs={{0,14},{2,12},{4,10},{6,8},{8,6},{10,4},{12,2},{14,0},{16,30},{18,... | collective-permute-start | bytes 208904 | tf_op jit(solution)/shard_map/ppermute | solution.py:231
  12.1 0.0 collective-permute-done.3.ahead
  12.1 1.1 %collective-permute-done.4.side = s16[272,128]{1,0:T(8,128)(2,1)S(1)} collective-permute-done((s16[272,128]{1,0:T(8,128)(2,1)S(1)}, s16[272,128]{1,0:T(8,128)(2,1)S(1)}, u32[]{:S(2)}, u32[]{:S(2)}) %collective-permute-start.4) | collective-permute-done | bytes 69664 | tf_op jit(solution)/shard_map/ppermute | solution.py:300
  13.3 0.2 collective-permute-start.6
  13.5 2.2 %collective-permute-done.5.diagonal = s16[272,128]{1,0:T(8,128)(2,1)S(1)} collective-permute-done((s16[272,128]{1,0:T(8,128)(2,1)S(1)}, s16[272,128]{1,0:T(8,128)(2,1)S(1)}, u32[]{:S(2)}, u32[]{:S(2)}) %collective-permute-start.5) | collective-permute-done | bytes 69664 | tf_op jit(solution)/shard_map/ppermute | solution.py:231
  15.6 0.0 collective-permute-done.6.passed
  15.6 0.1 far_sums.1
  15.7 2.7 %collective-permute-start.7 = (s16[144,128]{1,0:T(8,128)(2,1)S(1)}, s16[144,128]{1,0:T(8,128)(2,1)S(1)}, u32[]{:S(2)}, u32[]{:S(2)}) collective-permute-start(s16[144,128]{1,0:T(8,128)(2,1)S(1)} %get-tuple-element.28), channel_id=1, source_target_pairs={{0,18},{2,16},{4,22},{6,20},{8,26},{10,24},{12,30},{14,28},{16,2},... | collective-permute-start | bytes 110600 | tf_op jit(solution)/shard_map/ppermute | solution.py:231
  18.4 1.6 %collective-permute-done.7.refs_0_ = s16[144,128]{1,0:T(8,128)(2,1)S(1)} collective-permute-done((s16[144,128]{1,0:T(8,128)(2,1)S(1)}, s16[144,128]{1,0:T(8,128)(2,1)S(1)}, u32[]{:S(2)}, u32[]{:S(2)}) %collective-permute-start.7) | collective-permute-done | bytes 36896 | tf_op jit(solution)/shard_map/ppermute | solution.py:231
  20.1 0.7 %own_block.1 = f32[8,8,256]{2,1,0:T(8,128)} custom-call(f32[1,64,256]{2,1,0:T(8,128)S(1)} %get-tuple-element.27.keep, s16[144,128]{1,0:T(8,128)(2,1)S(1)} %collective-permute-done.7.refs_0_), custom_call_target="tpu_custom_call" | custom-call | tf_op jit(solution)/shard_map/own_block/pallas_call | solution.py:330
  (1 shorter events, 0.0 us)
Async XLA Ops:
  0.0 6.7 %collective-permute-start.1 = (bf16[64,4,256]{2,1,0:T(4,128)(2,1)}, bf16[64,4,256]{2,1,0:T(4,128)(2,1)S(1)}, u32[]{:S(2)}, u32[]{:S(2)}) collective-permute-start(bf16[64,4,256]{2,1,0:T(4,128)(2,1)} %own_hbm.1), channel_id=1, source_target_pairs={{0,1},{1,0},{2,3},{3,2},{4,5},{5,4},{6,7},{7,6},{8,9},{9,8},{10,11... | collective-permute-start | bytes 393224 | tf_op jit(solution)/shard_map/ppermute | solution.py:253
  5.4 2.1 %collective-permute-start = (f32[4,64,256]{2,1,0:T(8,128)S(1)}, f32[4,64,256]{2,1,0:T(8,128)S(1)}, u32[]{:S(2)}, u32[]{:S(2)}) collective-permute-start(f32[4,64,256]{2,1,0:T(8,128)S(1)} %get-tuple-element.18), channel_id=1, source_target_pairs={{0,2},{2,0},{4,6},{6,4},{8,10},{10,8},{12,14},{14,12},{16,18},{18,... | collective-permute-start | bytes 786440 | tf_op jit(solution)/shard_map/ppermute | solution.py:231
  7.4 2.0 %collective-permute-start.2 = (f32[4,64,256]{2,1,0:T(8,128)S(1)}, f32[4,64,256]{2,1,0:T(8,128)S(1)}, u32[]{:S(2)}, u32[]{:S(2)}) collective-permute-start(f32[4,64,256]{2,1,0:T(8,128)S(1)} %get-tuple-element.23), channel_id=1, source_target_pairs={{0,2},{2,0},{4,6},{6,4},{8,10},{10,8},{12,14},{14,12},{16,18},{18,... | collective-permute-start | bytes 786440 | tf_op jit(solution)/shard_map/ppermute | solution.py:231
  7.6 4.6 %collective-permute-start.3 = (s16[288,128]{1,0:T(8,128)(2,1)S(1)}, s16[288,128]{1,0:T(8,128)(2,1)S(1)}, u32[]{:S(2)}, u32[]{:S(2)}) collective-permute-start(s16[288,128]{1,0:T(8,128)(2,1)S(1)} %get-tuple-element.25), channel_id=1, source_target_pairs={{0,6},{2,8},{4,2},{6,12},{8,14},{10,0},{12,10},{14,4},{16,22},{18,... | collective-permute-start | bytes 221192 | tf_op jit(solution)/shard_map/ppermute | solution.py:300
  9.5 3.8 %collective-permute-start.4 = (s16[272,128]{1,0:T(8,128)(2,1)S(1)}, s16[272,128]{1,0:T(8,128)(2,1)S(1)}, u32[]{:S(2)}, u32[]{:S(2)}) collective-permute-start(s16[272,128]{1,0:T(8,128)(2,1)S(1)} %side_sums.1), channel_id=1, source_target_pairs={{0,6},{2,8},{4,2},{6,12},{8,14},{10,0},{12,10},{14,4},{16,22},{18,... | collective-permute-start | bytes 208904 | tf_op jit(solution)/shard_map/ppermute | solution.py:300
  10.8 4.8 %collective-permute-start.5 = (s16[272,128]{1,0:T(8,128)(2,1)S(1)}, s16[272,128]{1,0:T(8,128)(2,1)S(1)}, u32[]{:S(2)}, u32[]{:S(2)}) collective-permute-start(s16[272,128]{1,0:T(8,128)(2,1)S(1)} %get-tuple-element.26), channel_id=1, source_target_pairs={{0,14},{2,12},{4,10},{6,8},{8,6},{10,4},{12,2},{14,0},{16,30},{18,... | collective-permute-start | bytes 208904 | tf_op jit(solution)/shard_map/ppermute | solution.py:231
  13.3 2.4 %collective-permute-start.6 = (s16[272,128]{1,0:T(8,128)(2,1)S(1)}, s16[272,128]{1,0:T(8,128)(2,1)S(1)}, u32[]{:S(2)}, u32[]{:S(2)}) collective-permute-start(s16[272,128]{1,0:T(8,128)(2,1)S(1)} %pass_on.1), channel_id=1, source_target_pairs={{0,2},{2,0},{4,6},{6,4},{8,10},{10,8},{12,14},{14,12},{16,18},{18,... | collective-permute-start | bytes 208904 | tf_op jit(solution)/shard_map/ppermute | solution.py:231
  15.7 4.3 %collective-permute-start.7 = (s16[144,128]{1,0:T(8,128)(2,1)S(1)}, s16[144,128]{1,0:T(8,128)(2,1)S(1)}, u32[]{:S(2)}, u32[]{:S(2)}) collective-permute-start(s16[144,128]{1,0:T(8,128)(2,1)S(1)} %get-tuple-element.28), channel_id=1, source_target_pairs={{0,18},{2,16},{4,22},{6,20},{8,26},{10,24},{12,30},{14,28},{16,2},... | collective-permute-start | bytes 110600 | tf_op jit(solution)/shard_map/ppermute | solution.py:231

commit v10 on v8

--- a/solution.py
+++ b/solution.py
@@ -139,7 +139,7 @@
 
 
 def late_kernel(size, count, *refs):
-    others, (tiles, live, send, keep, lhs, totals) = refs[:count], refs[count:]
+    others, (tiles, live, out, keep, send, lhs, totals) = refs[:count], refs[count:]
     slots = tiles.shape[0]
     totals[...] = jnp.zeros(totals.shape, totals.dtype)
     for h, raw in enumerate(others):
@@ -156,6 +156,7 @@
                     totals[h, t] += jnp.dot(lhs[k, h], tiles[tile], preferred_element_type=jnp.float32)
 
     lay_out(size, count + 1, 1, [totals.at[h] for h in range(count)], keep, send)
+    encode([send[i] for i in range(4 * count)], out)
 
 
 def early_sums_kernel(keep, got, ahead, out):
@@ -169,7 +170,7 @@
     rows, width = early.shape[1:]
     sums = []
     for at in range(4):
-        sums.append([late_keep[i] + late_got[i] for i in range(at, (n_col - 1) * 4, 4)])
+        sums.append([late_keep[i] + decode(late_got, i, rows, width) for i in range(at, (n_col - 1) * 4, 4)])
     encode(sums[1] + sums[2], side)
     encode([early[0]] + sums[0], diagonal)
     out[0] = early[1]
@@ -313,10 +314,11 @@
     lates = n_col - 1
     late_send, late_keep = pl.pallas_call(
         functools.partial(late_kernel, size, lates),
-        out_shape=[kept(lates * 4), kept(lates * 4)],
+        out_shape=[coded(lates * 4), kept(lates * 4)],
         in_specs=[spec] * n_col + [smem],
         out_specs=[spec, spec],
         scratch_shapes=[
+            pltpu.VMEM((lates * 4,) + block, jnp.float32),
             pltpu.VMEM((depth, lates, half, width), jnp.bfloat16),
             pltpu.VMEM((lates, targets + 1, half, out_width), jnp.float32),
         ],

time: 20.8 us -> 20.8 us (level)
    ppermute x5, waiting for transfers between devices: 3.87 us -> 3.51 us  [swap(): return lax.ppermute(x, 'row', [(i, i ^ mask) for i in range(n_row)])]
    ppermute x5, starting transfers between devices: 4.11 us -> 4.37 us  [swap(): return lax.ppermute(x, 'row', [(i, i ^ mask) for i in range(n_row)])]
where the time goes in v10:
time: 20.8 us; the launch traced here: 20.6 us
  starting transfers between devices  10.3 us (50%)
  waiting for transfers between devices  6.05 us (29%)
  Pallas kernels  4.25 us (20%)
    ppermute x5, starting transfers between devices, swap(): return lax.ppermute(x, 'row', [(i, i ^ mask) for i in range(n_row)])  4.37 us
    ppermute x5, waiting for transfers between devices, swap(): return lax.ppermute(x, 'row', [(i, i ^ mask) for i in range(n_row)])  3.51 us
    ppermute x1, starting transfers between devices, body(): lax.ppermute(amplitudes, 'col', [(i, (i + step) % n_col) for i in range(n...  2.97 us
    ppermute x2, starting transfers between devices, to_side(): lax.ppermute(x, 'row', [(i, i ^ (ALONG if i % 2 else ACROSS) ^ 1) for i i...  2.94 us
    pallas_call x1, Pallas kernels, body(): pl.pallas_call(functools.partial(early_kernel, size, n_col), out_shape=[p...  2.53 us
    ppermute x2, waiting for transfers between devices, to_side(): lax.ppermute(x, 'row', [(i, i ^ (ALONG if i % 2 else ACROSS) ^ 1) for i i...  1.44 us
    ppermute x1, waiting for transfers between devices, body(): lax.ppermute(amplitudes, 'col', [(i, (i + step) % n_col) for i in range(n...  1.09 us
    pallas_call x1, Pallas kernels, body(): pl.pallas_call(functools.partial(late_kernel, size, lates), out_shape=[co...  0.77 us
  transfers between devices with their start and end apart: 8, of which 4 were waited for; matrix products, arithmetic and copies ran while one was open for 0% of the time, Pallas kernels for 17%

profile of v10, /device:TPU:0, one launch (start us, length us, event | category | flops | bytes accessed | tf_op | source)
XLA Modules:
  0.0 20.6 jit_solution(1345968658845376632)
XLA Ops:
  0.0 3.0 %collective-permute-start.1 = (bf16[64,4,256]{2,1,0:T(4,128)(2,1)}, bf16[64,4,256]{2,1,0:T(4,128)(2,1)S(1)}, u32[]{:S(2)}, u32[]{:S(2)}) collective-permute-start(bf16[64,4,256]{2,1,0:T(4,128)(2,1)} %own_hbm.1), channel_id=1, source_target_pairs={{0,1},{1,0},{2,3},{3,2},{4,5},{5,4},{6,7},{7,6},{8,9},{9,8},{10,11... | collective-permute-start | bytes 393224 | tf_op jit(solution)/shard_map/ppermute | solution.py:281
  3.0 2.5 %early_half.1 = (bf16[24,256,256]{2,1,0:T(8,128)(2,1)S(1)}, s32[75]{0:T(128)S(4)}, f32[4,64,256]{2,1,0:T(8,128)S(1)}, f32[4,64,256]{2,1,0:T(8,128)S(1)}) custom-call(s32[4,6]{1,0:T(4,128)} %screen_hbm.1, s32[1,8]{1,0:T(1,128)} %owner_hbm.1, bf16[64,4,256]{2,1,0:T(4,128)(2,1)} %own_hbm.1, bf16[4,6,256,256]{3,2,1,0:T(8,128)(2,1)} %integrals.1), custom_call_target="tpu_custom_call" | custom-call | flops 268435456 | bytes 3145728 | tf_op jit(solution)/shard_map/early_half/pallas_call | solution.py:287
  5.5 0.1 collective-permute-start
  5.6 1.1 %collective-permute-done.1.refs_0_ = bf16[64,4,256]{2,1,0:T(4,128)(2,1)S(1)} collective-permute-done((bf16[64,4,256]{2,1,0:T(4,128)(2,1)}, bf16[64,4,256]{2,1,0:T(4,128)(2,1)S(1)}, u32[]{:S(2)}, u32[]{:S(2)}) %collective-permute-start.1) | collective-permute-done | bytes 131104 | tf_op jit(solution)/shard_map/ppermute | solution.py:281
  6.7 0.8 %late_half.1 = (s16[528,128]{1,0:T(8,128)(2,1)S(1)}, f32[4,64,256]{2,1,0:T(8,128)S(1)}) custom-call(bf16[64,4,256]{2,1,0:T(4,128)(2,1)S(1)} %collective-permute-done.1.refs_0_, bf16[24,256,256]{2,1,0:T(8,128)(2,1)S(1)} %get-tuple-element.21.refs_1_, s32[75]{0:T(128)S(4)} %get-tuple-element.22.refs_2_), custom_call_target="tpu_custom_call" | custom-call | flops 268435456 | tf_op jit(solution)/shard_map/late_half/pallas_call | solution.py:315
  7.4 0.1 collective-permute-start.2
  7.5 0.0 collective-permute-done.got
  7.5 0.1 early_sums.1
  7.6 1.8 %collective-permute-start.3 = (s16[288,128]{1,0:T(8,128)(2,1)S(1)}, s16[288,128]{1,0:T(8,128)(2,1)S(1)}, u32[]{:S(2)}, u32[]{:S(2)}) collective-permute-start(s16[288,128]{1,0:T(8,128)(2,1)S(1)} %get-tuple-element.26), channel_id=1, source_target_pairs={{0,6},{2,8},{4,2},{6,12},{8,14},{10,0},{12,10},{14,4},{16,22},{18,... | collective-permute-start | bytes 221192 | tf_op jit(solution)/shard_map/ppermute | solution.py:331
  9.4 0.0 collective-permute-done.2.late_got
  9.4 0.1 near_sums.1
  9.5 1.2 %collective-permute-start.4 = (s16[272,128]{1,0:T(8,128)(2,1)S(1)}, s16[272,128]{1,0:T(8,128)(2,1)S(1)}, u32[]{:S(2)}, u32[]{:S(2)}) collective-permute-start(s16[272,128]{1,0:T(8,128)(2,1)S(1)} %get-tuple-element.27), channel_id=1, source_target_pairs={{0,6},{2,8},{4,2},{6,12},{8,14},{10,0},{12,10},{14,4},{16,22},{18,... | collective-permute-start | bytes 208904 | tf_op jit(solution)/shard_map/ppermute | solution.py:331
  10.7 1.2 %collective-permute-start.5 = (s16[272,128]{1,0:T(8,128)(2,1)S(1)}, s16[272,128]{1,0:T(8,128)(2,1)S(1)}, u32[]{:S(2)}, u32[]{:S(2)}) collective-permute-start(s16[272,128]{1,0:T(8,128)(2,1)S(1)} %get-tuple-element.28), channel_id=1, source_target_pairs={{0,14},{2,12},{4,10},{6,8},{8,6},{10,4},{12,2},{14,0},{16,30},{18,... | collective-permute-start | bytes 208904 | tf_op jit(solution)/shard_map/ppermute | solution.py:259
  11.8 0.0 collective-permute-done.3.ahead
  11.9 1.4 %collective-permute-done.4.side = s16[272,128]{1,0:T(8,128)(2,1)S(1)} collective-permute-done((s16[272,128]{1,0:T(8,128)(2,1)S(1)}, s16[272,128]{1,0:T(8,128)(2,1)S(1)}, u32[]{:S(2)}, u32[]{:S(2)}) %collective-permute-start.4) | collective-permute-done | bytes 69664 | tf_op jit(solution)/shard_map/ppermute | solution.py:331
  13.3 0.3 %collective-permute-start.6 = (s16[272,128]{1,0:T(8,128)(2,1)S(1)}, s16[272,128]{1,0:T(8,128)(2,1)S(1)}, u32[]{:S(2)}, u32[]{:S(2)}) collective-permute-start(s16[272,128]{1,0:T(8,128)(2,1)S(1)} %pass_on.1), channel_id=1, source_target_pairs={{0,2},{2,0},{4,6},{6,4},{8,10},{10,8},{12,14},{14,12},{16,18},{18,... | collective-permute-start | bytes 208904 | tf_op jit(solution)/shard_map/ppermute | solution.py:259
  13.6 1.9 %collective-permute-done.5.diagonal = s16[272,128]{1,0:T(8,128)(2,1)S(1)} collective-permute-done((s16[272,128]{1,0:T(8,128)(2,1)S(1)}, s16[272,128]{1,0:T(8,128)(2,1)S(1)}, u32[]{:S(2)}, u32[]{:S(2)}) %collective-permute-start.5) | collective-permute-done | bytes 69664 | tf_op jit(solution)/shard_map/ppermute | solution.py:259
  15.4 0.0 collective-permute-done.6.passed
  15.4 0.1 far_sums.1
  15.5 2.8 %collective-permute-start.7 = (s16[144,128]{1,0:T(8,128)(2,1)S(1)}, s16[144,128]{1,0:T(8,128)(2,1)S(1)}, u32[]{:S(2)}, u32[]{:S(2)}) collective-permute-start(s16[144,128]{1,0:T(8,128)(2,1)S(1)} %get-tuple-element.30), channel_id=1, source_target_pairs={{0,18},{2,16},{4,22},{6,20},{8,26},{10,24},{12,30},{14,28},{16,2},... | collective-permute-start | bytes 110600 | tf_op jit(solution)/shard_map/ppermute | solution.py:259
  18.3 1.6 %collective-permute-done.7.refs_0_ = s16[144,128]{1,0:T(8,128)(2,1)S(1)} collective-permute-done((s16[144,128]{1,0:T(8,128)(2,1)S(1)}, s16[144,128]{1,0:T(8,128)(2,1)S(1)}, u32[]{:S(2)}, u32[]{:S(2)}) %collective-permute-start.7) | collective-permute-done | bytes 36896 | tf_op jit(solution)/shard_map/ppermute | solution.py:259
  20.0 0.7 %own_block.1 = f32[8,8,256]{2,1,0:T(8,128)} custom-call(f32[1,64,256]{2,1,0:T(8,128)S(1)} %get-tuple-element.29.keep, s16[144,128]{1,0:T(8,128)(2,1)S(1)} %collective-permute-done.7.refs_0_), custom_call_target="tpu_custom_call" | custom-call | tf_op jit(solution)/shard_map/own_block/pallas_call | solution.py:367
  (1 shorter events, 0.0 us)
Async XLA Ops:
  0.0 6.7 %collective-permute-start.1 = (bf16[64,4,256]{2,1,0:T(4,128)(2,1)}, bf16[64,4,256]{2,1,0:T(4,128)(2,1)S(1)}, u32[]{:S(2)}, u32[]{:S(2)}) collective-permute-start(bf16[64,4,256]{2,1,0:T(4,128)(2,1)} %own_hbm.1), channel_id=1, source_target_pairs={{0,1},{1,0},{2,3},{3,2},{4,5},{5,4},{6,7},{7,6},{8,9},{9,8},{10,11... | collective-permute-start | bytes 393224 | tf_op jit(solution)/shard_map/ppermute | solution.py:281
  5.5 2.0 %collective-permute-start = (f32[4,64,256]{2,1,0:T(8,128)S(1)}, f32[4,64,256]{2,1,0:T(8,128)S(1)}, u32[]{:S(2)}, u32[]{:S(2)}) collective-permute-start(f32[4,64,256]{2,1,0:T(8,128)S(1)} %get-tuple-element.19), channel_id=1, source_target_pairs={{0,2},{2,0},{4,6},{6,4},{8,10},{10,8},{12,14},{14,12},{16,18},{18,... | collective-permute-start | bytes 786440 | tf_op jit(solution)/shard_map/ppermute | solution.py:259
  7.4 1.9 %collective-permute-start.2 = (s16[528,128]{1,0:T(8,128)(2,1)S(1)}, s16[528,128]{1,0:T(8,128)(2,1)S(1)}, u32[]{:S(2)}, u32[]{:S(2)}) collective-permute-start(s16[528,128]{1,0:T(8,128)(2,1)S(1)} %get-tuple-element.24), channel_id=1, source_target_pairs={{0,2},{2,0},{4,6},{6,4},{8,10},{10,8},{12,14},{14,12},{16,18},{18,... | collective-permute-start | bytes 405512 | tf_op jit(solution)/shard_map/ppermute | solution.py:259
  7.6 4.2 %collective-permute-start.3 = (s16[288,128]{1,0:T(8,128)(2,1)S(1)}, s16[288,128]{1,0:T(8,128)(2,1)S(1)}, u32[]{:S(2)}, u32[]{:S(2)}) collective-permute-start(s16[288,128]{1,0:T(8,128)(2,1)S(1)} %get-tuple-element.26), channel_id=1, source_target_pairs={{0,6},{2,8},{4,2},{6,12},{8,14},{10,0},{12,10},{14,4},{16,22},{18,... | collective-permute-start | bytes 221192 | tf_op jit(solution)/shard_map/ppermute | solution.py:331
  9.5 3.8 %collective-permute-start.4 = (s16[272,128]{1,0:T(8,128)(2,1)S(1)}, s16[272,128]{1,0:T(8,128)(2,1)S(1)}, u32[]{:S(2)}, u32[]{:S(2)}) collective-permute-start(s16[272,128]{1,0:T(8,128)(2,1)S(1)} %get-tuple-element.27), channel_id=1, source_target_pairs={{0,6},{2,8},{4,2},{6,12},{8,14},{10,0},{12,10},{14,4},{16,22},{18,... | collective-permute-start | bytes 208904 | tf_op jit(solution)/shard_map/ppermute | solution.py:331
  10.7 4.8 %collective-permute-start.5 = (s16[272,128]{1,0:T(8,128)(2,1)S(1)}, s16[272,128]{1,0:T(8,128)(2,1)S(1)}, u32[]{:S(2)}, u32[]{:S(2)}) collective-permute-start(s16[272,128]{1,0:T(8,128)(2,1)S(1)} %get-tuple-element.28), channel_id=1, source_target_pairs={{0,14},{2,12},{4,10},{6,8},{8,6},{10,4},{12,2},{14,0},{16,30},{18,... | collective-permute-start | bytes 208904 | tf_op jit(solution)/shard_map/ppermute | solution.py:259
  13.3 2.1 %collective-permute-start.6 = (s16[272,128]{1,0:T(8,128)(2,1)S(1)}, s16[272,128]{1,0:T(8,128)(2,1)S(1)}, u32[]{:S(2)}, u32[]{:S(2)}) collective-permute-start(s16[272,128]{1,0:T(8,128)(2,1)S(1)} %pass_on.1), channel_id=1, source_target_pairs={{0,2},{2,0},{4,6},{6,4},{8,10},{10,8},{12,14},{14,12},{16,18},{18,... | collective-permute-start | bytes 208904 | tf_op jit(solution)/shard_map/ppermute | solution.py:259
  15.5 4.4 %collective-permute-start.7 = (s16[144,128]{1,0:T(8,128)(2,1)S(1)}, s16[144,128]{1,0:T(8,128)(2,1)S(1)}, u32[]{:S(2)}, u32[]{:S(2)}) collective-permute-start(s16[144,128]{1,0:T(8,128)(2,1)S(1)} %get-tuple-element.30), channel_id=1, source_target_pairs={{0,18},{2,16},{4,22},{6,20},{8,26},{10,24},{12,30},{14,28},{16,2},... | collective-permute-start | bytes 110600 | tf_op jit(solution)/shard_map/ppermute | solution.py:259
